TPU v7x, 32 devices: a whole 2x2x4 slice. The times are simulated.
32 devices in a mesh: dp: 8 (over y, x, core), ctx: 4 (over z).
Axes of the slice: x: 2, y: 2, z: 4, core: 2. Of those that a mesh axis runs over, the one named last changes fastest.
Arguments:
- hidden: bfloat16 [8, 1024, 1536], P('dp', 'ctx'), may hold values from -6 to 6
- cotangent: bfloat16 [8, 1024, 1536], P('dp', 'ctx'), may hold values from -6 to 6
- span_order: int32 [8, 8], P('dp'), may hold values from 0 to 7, each once within a row
- attn_gain: bfloat16 [1536], P(('dp', 'ctx')), may hold values from 0.25 to 1.75
- w_query: bfloat16 [1536, 1536], P(('dp', 'ctx')), may hold values from -0.15625 to 0.15625
- b_query: bfloat16 [1536], P(('dp', 'ctx')), may hold values from -3 to 3
- w_key: bfloat16 [1536, 256], P(('dp', 'ctx')), may hold values from -0.15625 to 0.15625
- b_key: bfloat16 [256], P(('dp', 'ctx')), may hold values from -3 to 3
- w_value: bfloat16 [1536, 256], P(('dp', 'ctx')), may hold values from -0.15625 to 0.15625
- b_value: bfloat16 [256], P(('dp', 'ctx')), may hold values from -3 to 3
- w_out: bfloat16 [1536, 1536], P(('dp', 'ctx')), may hold values from -0.625 to 0.625
- ffn_gain: bfloat16 [1536], P(('dp', 'ctx')), may hold values from 0.25 to 1.75
- w_gate: bfloat16 [1536, 8960], P(('dp', 'ctx')), may hold values from -0.15625 to 0.15625
- w_up: bfloat16 [1536, 8960], P(('dp', 'ctx')), may hold values from -0.15625 to 0.15625
- w_down: bfloat16 [1536, 8960], P(('dp', 'ctx')), may hold values from -0.125 to 0.125
Outputs:
- result: bfloat16 [8, 1024, 1536], P('dp', 'ctx')
- hidden_grad: float32 [8, 1024, 1536], P('dp', 'ctx')
- attn_gain_grad: float32 [1536], P(('dp', 'ctx'))
- w_query_grad: float32 [1536, 1536], P(('dp', 'ctx'))
- b_query_grad: float32 [1536], P(('dp', 'ctx'))
- w_key_grad: float32 [1536, 256], P(('dp', 'ctx'))
- b_key_grad: float32 [256], P(('dp', 'ctx'))
- w_value_grad: float32 [1536, 256], P(('dp', 'ctx'))
- b_value_grad: float32 [256], P(('dp', 'ctx'))
- w_out_grad: float32 [1536, 1536], P(('dp', 'ctx'))
- ffn_gain_grad: float32 [1536], P(('dp', 'ctx'))
- w_gate_grad: float32 [1536, 8960], P(('dp', 'ctx'))
- w_up_grad: float32 [1536, 8960], P(('dp', 'ctx'))
- w_down_grad: float32 [1536, 8960], P(('dp', 'ctx'))
Inputs may be any that keep to these rules, and one draw needn't show every extreme that they name: `span_order`: each row is a permutation; entry j of a row names the block of 128 positions that the row's stored places j * 128 to (j + 1) * 128 - 1 hold.
All inputs are finite; a program needn't handle non-finite values.
Results may differ from a plain program's by a relative error of at most 0.019.
Values may be sent and summed in bfloat16 or wider, within the bound.
A program may use at most 384 MiB of HBM per device.

v0:
```python
import jax
import jax.numpy as jnp
from jax import lax
from jax.sharding import PartitionSpec as P

D = 1536
HEADS = 12
KV_HEADS = 2
HD = 128


norm_eps = 1e-06
rope_base = 10000.0
masked_fill = -1e30


def angles_for(places, width):
    half = width // 2
    freqs = rope_base ** (-(jnp.arange(half, dtype=jnp.float32) * 2.0 / width))
    angles = places.astype(jnp.float32)[:, None] * freqs[None, :]
    return (jnp.cos(angles)[:, None, :], jnp.sin(angles)[:, None, :])


def rotate(values, cosine, sine):
    half = values.shape[-1] // 2
    first = values[..., :half]
    second = values[..., half:]
    return jnp.concatenate(
        [first * cosine - second * sine, second * cosine + first * sine], axis=-1
    )


def rotate_back(values, cosine, sine):
    half = values.shape[-1] // 2
    first = values[..., :half]
    second = values[..., half:]
    return jnp.concatenate(
        [first * cosine + second * sine, second * cosine - first * sine], axis=-1
    )


def norm_forward(source, gain):
    factor = lax.rsqrt(jnp.mean(source * source, axis=-1, keepdims=True) + norm_eps)
    return (factor, (source * factor * gain).astype(jnp.bfloat16))


def norm_backward(source, factor, gain, grad_normed):
    unit = source * factor
    gain_grad = jnp.sum(grad_normed * unit, axis=0)
    scaled = grad_normed * gain
    source_grad = factor * (scaled - unit * jnp.mean(scaled * unit, axis=-1, keepdims=True))
    return (source_grad, gain_grad)


def right_dot(left, weight):
    return jnp.einsum("rf,df->rd", left, weight, preferred_element_type=jnp.float32)


def plain_dot(left, weight):
    return jnp.dot(left, weight, preferred_element_type=jnp.float32)


def owned_columns(values, ctx_size, ctx_rank, shard_rows):
    rows = values.shape[0]
    blocks = values.shape[1] // (shard_rows * ctx_size)
    shaped = values.reshape(rows, blocks, ctx_size, shard_rows)
    picked = lax.dynamic_index_in_dim(shaped, ctx_rank, axis=2, keepdims=False)
    return picked.reshape(rows, blocks * shard_rows)


def outer_add(left, right):
    return jnp.einsum("rc,rf->cf", left, right, preferred_element_type=jnp.float32)


def per_device(
    hidden,
    cotangent,
    span_order,
    attn_gain,
    w_query,
    b_query,
    w_key,
    b_key,
    w_value,
    b_value,
    w_out,
    ffn_gain,
    w_gate,
    w_up,
    w_down,
):
    ctx_size = lax.axis_size("ctx")
    ctx_rank = lax.axis_index("ctx")
    batches = hidden.shape[0]
    length = hidden.shape[1]
    span_len = length // 2
    seq_len = length * ctx_size
    row_count = batches * length
    groups = HEADS // KV_HEADS
    shard_rows = w_query.shape[0]
    head_scale = HD ** (-0.5)
    kv_width = KV_HEADS * HD
    q_width = HEADS * HD
    places = jnp.arange(seq_len, dtype=jnp.int32)
    every_pos = jnp.repeat(span_order, span_len, axis=1) * span_len + places[None, :] % span_len
    local_pos = lax.dynamic_slice_in_dim(every_pos, ctx_rank * length, length, 1)
    cosine, sine = angles_for(local_pos.reshape(row_count), HD)
    allowed = (every_pos[:, None, :] <= local_pos[:, :, None])[:, None, None]
    attn_full = (
        lax.all_gather(attn_gain, ("dp", "ctx"), axis=0, tiled=True),
        lax.all_gather(w_query, ("dp", "ctx"), axis=0, tiled=True),
        lax.all_gather(w_key, ("dp", "ctx"), axis=0, tiled=True),
        lax.all_gather(w_value, ("dp", "ctx"), axis=0, tiled=True),
        lax.all_gather(w_out, ("dp", "ctx"), axis=0, tiled=True),
        lax.all_gather(b_query, ("dp", "ctx"), axis=0, tiled=True),
        lax.all_gather(b_key, ("dp", "ctx"), axis=0, tiled=True),
        lax.all_gather(b_value, ("dp", "ctx"), axis=0, tiled=True),
    )
    gain_one = attn_full[0].astype(jnp.float32)
    source = hidden.reshape(row_count, D).astype(jnp.float32)
    attn_factor, normed = norm_forward(source, gain_one)
    query_raw = plain_dot(normed, attn_full[1]) + attn_full[5].astype(jnp.float32)
    key_raw = plain_dot(normed, attn_full[2]) + attn_full[6].astype(jnp.float32)
    value_low = (plain_dot(normed, attn_full[3]) + attn_full[7].astype(jnp.float32)).astype(
        jnp.bfloat16
    )
    query_rot = rotate(query_raw.reshape(row_count, HEADS, HD), cosine, sine).astype(jnp.bfloat16)
    query_rot = query_rot.reshape(batches, length, KV_HEADS, groups, HD)
    key_rot = rotate(key_raw.reshape(row_count, KV_HEADS, HD), cosine, sine).astype(jnp.bfloat16)
    key_rot = key_rot.reshape(batches, length, kv_width)
    key_all, value_all = (
        lax.all_gather(key_rot, "ctx", axis=1, tiled=True),
        lax.all_gather(value_low.reshape(batches, length, kv_width), "ctx", axis=1, tiled=True),
    )
    key_all = key_all.reshape(batches, seq_len, KV_HEADS, HD)
    value_all = value_all.reshape(batches, seq_len, KV_HEADS, HD)
    scores = (
        jnp.einsum("bqkgd,bskd->bkgqs", query_rot, key_all, preferred_element_type=jnp.float32)
        * head_scale
    )
    masked = jnp.where(allowed, scores, masked_fill)
    row_max = jnp.max(masked, axis=-1, keepdims=True)
    expo = jnp.exp(masked - row_max)
    expo_sum = jnp.sum(expo, axis=-1, keepdims=True)
    log_total = row_max + jnp.log(expo_sum)
    attend = (expo / expo_sum).astype(jnp.bfloat16)
    mixed = jnp.einsum("bkgqs,bskd->bqkgd", attend, value_all, preferred_element_type=jnp.float32)
    mixed = mixed.reshape(row_count, q_width).astype(jnp.bfloat16)
    resid = source + right_dot(mixed, attn_full[4])
    ffn_full = (
        lax.all_gather(ffn_gain, ("dp", "ctx"), axis=0, tiled=True),
        lax.all_gather(w_gate, ("dp", "ctx"), axis=0, tiled=True),
        lax.all_gather(w_up, ("dp", "ctx"), axis=0, tiled=True),
        lax.all_gather(w_down, ("dp", "ctx"), axis=0, tiled=True),
    )
    gain_two = ffn_full[0].astype(jnp.float32)
    ffn_factor, normed_two = norm_forward(resid, gain_two)
    gate_pre = plain_dot(normed_two, ffn_full[1])
    up_pre = plain_dot(normed_two, ffn_full[2])
    sigmoid_gate = jax.nn.sigmoid(gate_pre)
    silu_gate = gate_pre * sigmoid_gate
    act = (silu_gate * up_pre).astype(jnp.bfloat16)
    output = resid + right_dot(act, ffn_full[3])
    result = output.astype(jnp.bfloat16).reshape(batches, length, D)
    ffn_back = (
        lax.all_gather(ffn_gain, ("dp", "ctx"), axis=0, tiled=True),
        lax.all_gather(w_gate, ("dp", "ctx"), axis=0, tiled=True),
        lax.all_gather(w_up, ("dp", "ctx"), axis=0, tiled=True),
        lax.all_gather(w_down, ("dp", "ctx"), axis=0, tiled=True),
    )
    grad_out = cotangent.reshape(row_count, D)
    grad_plain = grad_out.astype(jnp.float32)
    grad_act = plain_dot(grad_out, ffn_back[3])
    grad_gate = (grad_act * up_pre * sigmoid_gate * (1.0 + gate_pre * (1.0 - sigmoid_gate))).astype(
        jnp.bfloat16
    )
    grad_up = (grad_act * silu_gate).astype(jnp.bfloat16)
    pieces = (
        lax.all_gather(normed_two, "ctx", axis=0, tiled=True),
        lax.all_gather(grad_gate, "ctx", axis=0, tiled=True),
        lax.all_gather(grad_up, "ctx", axis=0, tiled=True),
        lax.all_gather(act, "ctx", axis=0, tiled=True),
        lax.all_gather(grad_out, "ctx", axis=0, tiled=True),
    )
    picked_in = owned_columns(pieces[0], ctx_size, ctx_rank, shard_rows)
    picked_out = owned_columns(pieces[4], ctx_size, ctx_rank, shard_rows)
    w_gate_grad, w_up_grad, w_down_grad = (
        lax.psum_scatter(
            outer_add(picked_in, pieces[1]).astype(jnp.bfloat16),
            "dp",
            scatter_dimension=0,
            tiled=True,
        ).astype(jnp.float32),
        lax.psum_scatter(
            outer_add(picked_in, pieces[2]).astype(jnp.bfloat16),
            "dp",
            scatter_dimension=0,
            tiled=True,
        ).astype(jnp.float32),
        lax.psum_scatter(
            outer_add(picked_out, pieces[3]).astype(jnp.bfloat16),
            "dp",
            scatter_dimension=0,
            tiled=True,
        ).astype(jnp.float32),
    )
    grad_norm_two = right_dot(grad_gate, ffn_back[1]) + right_dot(grad_up, ffn_back[2])
    resid_back, ffn_gain_part = norm_backward(resid, ffn_factor, gain_two, grad_norm_two)
    grad_resid = grad_plain + resid_back
    attn_back = (
        lax.all_gather(attn_gain, ("dp", "ctx"), axis=0, tiled=True),
        lax.all_gather(w_query, ("dp", "ctx"), axis=0, tiled=True),
        lax.all_gather(w_key, ("dp", "ctx"), axis=0, tiled=True),
        lax.all_gather(w_value, ("dp", "ctx"), axis=0, tiled=True),
        lax.all_gather(w_out, ("dp", "ctx"), axis=0, tiled=True),
        lax.all_gather(b_query, ("dp", "ctx"), axis=0, tiled=True),
        lax.all_gather(b_key, ("dp", "ctx"), axis=0, tiled=True),
        lax.all_gather(b_value, ("dp", "ctx"), axis=0, tiled=True),
    )
    grad_attn = grad_resid.astype(jnp.bfloat16)
    grad_mixed = plain_dot(grad_attn, attn_back[4]).astype(jnp.bfloat16)
    grad_mixed = grad_mixed.reshape(batches, length, KV_HEADS, groups, HD)
    scores = (
        jnp.einsum("bqkgd,bskd->bkgqs", query_rot, key_all, preferred_element_type=jnp.float32)
        * head_scale
    )
    masked = jnp.where(allowed, scores, masked_fill)
    attend_full = jnp.exp(masked - log_total)
    attend = attend_full.astype(jnp.bfloat16)
    grad_attend = jnp.einsum(
        "bqkgd,bskd->bkgqs", grad_mixed, value_all, preferred_element_type=jnp.float32
    )
    value_grad_all = jnp.einsum(
        "bkgqs,bqkgd->bskd", attend, grad_mixed, preferred_element_type=jnp.float32
    )
    delta = jnp.sum(grad_attend * attend_full, axis=-1, keepdims=True)
    grad_scores = (attend_full * (grad_attend - delta)).astype(jnp.bfloat16)
    query_grad_rot = (
        jnp.einsum("bkgqs,bskd->bqkgd", grad_scores, key_all, preferred_element_type=jnp.float32)
        * head_scale
    )
    key_grad_all = (
        jnp.einsum("bkgqs,bqkgd->bskd", grad_scores, query_rot, preferred_element_type=jnp.float32)
        * head_scale
    )
    key_grad_rot, value_grad = (
        lax.psum_scatter(
            key_grad_all.reshape(batches, seq_len, kv_width), "ctx", scatter_dimension=1, tiled=True
        ),
        lax.psum_scatter(
            value_grad_all.reshape(batches, seq_len, kv_width),
            "ctx",
            scatter_dimension=1,
            tiled=True,
        ),
    )
    query_grad = (
        rotate_back(query_grad_rot.reshape(row_count, HEADS, HD), cosine, sine)
        .reshape(row_count, q_width)
        .astype(jnp.bfloat16)
    )
    key_grad = (
        rotate_back(key_grad_rot.reshape(row_count, KV_HEADS, HD), cosine, sine)
        .reshape(row_count, kv_width)
        .astype(jnp.bfloat16)
    )
    value_grad = value_grad.reshape(row_count, kv_width).astype(jnp.bfloat16)
    proj_grad = jnp.concatenate([query_grad, key_grad, value_grad], axis=1)
    pieces = (
        lax.all_gather(normed, "ctx", axis=0, tiled=True),
        lax.all_gather(proj_grad, "ctx", axis=0, tiled=True),
        lax.all_gather(grad_attn, "ctx", axis=0, tiled=True),
        lax.all_gather(mixed, "ctx", axis=0, tiled=True),
    )
    picked_in = owned_columns(pieces[0], ctx_size, ctx_rank, shard_rows)
    picked_out = owned_columns(pieces[2], ctx_size, ctx_rank, shard_rows)
    proj_sum, w_out_grad = (
        lax.psum_scatter(
            outer_add(picked_in, pieces[1]).astype(jnp.bfloat16),
            "dp",
            scatter_dimension=0,
            tiled=True,
        ).astype(jnp.float32),
        lax.psum_scatter(
            outer_add(picked_out, pieces[3]).astype(jnp.bfloat16),
            "dp",
            scatter_dimension=0,
            tiled=True,
        ).astype(jnp.float32),
    )
    grad_norm_one = (
        right_dot(query_grad, attn_back[1])
        + right_dot(key_grad, attn_back[2])
        + right_dot(value_grad, attn_back[3])
    )
    source_back, attn_gain_part = norm_backward(source, attn_factor, gain_one, grad_norm_one)
    hidden_grad = (grad_resid + source_back).reshape(batches, length, D)
    query_bias_part = jnp.sum(query_grad.astype(jnp.float32), axis=0)
    key_bias_part = jnp.sum(key_grad.astype(jnp.float32), axis=0)
    value_bias_part = jnp.sum(value_grad.astype(jnp.float32), axis=0)
    small_sums = (
        lax.psum_scatter(attn_gain_part, ("dp", "ctx"), scatter_dimension=0, tiled=True),
        lax.psum_scatter(query_bias_part, ("dp", "ctx"), scatter_dimension=0, tiled=True),
        lax.psum_scatter(key_bias_part, ("dp", "ctx"), scatter_dimension=0, tiled=True),
        lax.psum_scatter(value_bias_part, ("dp", "ctx"), scatter_dimension=0, tiled=True),
        lax.psum_scatter(ffn_gain_part, ("dp", "ctx"), scatter_dimension=0, tiled=True),
    )
    w_query_grad = proj_sum[:, :q_width]
    w_key_grad = proj_sum[:, q_width : q_width + kv_width]
    w_value_grad = proj_sum[:, q_width + kv_width :]
    return (
        result,
        hidden_grad,
        small_sums[0],
        w_query_grad,
        small_sums[1],
        w_key_grad,
        small_sums[2],
        w_value_grad,
        small_sums[3],
        w_out_grad,
        small_sums[4],
        w_gate_grad,
        w_up_grad,
        w_down_grad,
    )


def solution(mesh):
    placed = (
        P("dp", "ctx", None),
        P("dp", "ctx", None),
        P("dp", None),
        P(("dp", "ctx")),
        P(("dp", "ctx"), None),
        P(("dp", "ctx")),
        P(("dp", "ctx"), None),
        P(("dp", "ctx")),
        P(("dp", "ctx"), None),
        P(("dp", "ctx")),
        P(("dp", "ctx"), None),
        P(("dp", "ctx")),
        P(("dp", "ctx"), None),
        P(("dp", "ctx"), None),
        P(("dp", "ctx"), None),
    )
    return jax.shard_map(
        per_device,
        mesh=mesh,
        in_specs=placed,
        out_specs=(
            P("dp", "ctx", None),
            P("dp", "ctx", None),
            P(("dp", "ctx")),
            P(("dp", "ctx"), None),
            P(("dp", "ctx")),
            P(("dp", "ctx"), None),
            P(("dp", "ctx")),
            P(("dp", "ctx"), None),
            P(("dp", "ctx")),
            P(("dp", "ctx"), None),
            P(("dp", "ctx")),
            P(("dp", "ctx"), None),
            P(("dp", "ctx"), None),
            P(("dp", "ctx"), None),
        ),
        check_vma=False,
    )
```

profile of v0, /device:TPU:0, one launch (start us, length us, event | category | flops | bytes accessed | tf_op | source)
XLA Modules:
  0.0 2443.8 jit_solution(4614260419344166207)
XLA Ops:
  14.9 42.5 %all-reduce.11 = (bf16[1536]{0:T(1024)(128)(2,1)S(1)}, bf16[256]{0:T(256)(128)(2,1)S(1)}, bf16[1536]{0:T(1024)(128)(2,1)S(1)}, bf16[256]{0:T(256)(128)(2,1)S(1)}, bf16[1536]{0:T(1024)(128)(2,1)S(1)}) all-reduce(bf16[1536]{0:T(1024)(128)(2,1)S(1)} %dynamic-update-slice, ...), channel_id=1, replica_groups=mesh['dp'=8,'ctx'=4] {'dp','ctx'}, use_global_device_ids=true, to_apply=%add | all-reduce | flops 5120 | bytes 20480
  59.6 77.3 %all_gather.77 = bf16[1536,256]{1,0:T(8,128)(2,1)S(1)} all-gather(bf16[48,256]{1,0:T(8,128)(2,1)} %param.23), channel_id=1, replica_groups=mesh['dp'=8,'ctx'=4] {'dp','ctx'}, dimensions={0}, use_global_device_ids=true | all-gather | bytes 811008 | tf_op jit(solution)/shard_map/all_gather | solution.py:113
  137.5 17.7 all-gather
  157.1 80.5 %all_gather.80 = bf16[1536,256]{1,0:T(8,128)(2,1)S(1)} all-gather(bf16[48,256]{1,0:T(8,128)(2,1)S(1)} %copy-done.23), channel_id=1, replica_groups=mesh['dp'=8,'ctx'=4] {'dp','ctx'}, dimensions={0}, use_global_device_ids=true | all-gather | bytes 811008 | tf_op jit(solution)/shard_map/all_gather | solution.py:112
  238.2 18.0 all_gather.82
  256.5 4.9 convolution_add_fusion.5
  276.0 3.8 fusion.27
  279.8 4.1 multiply_reduce_fusion.2
  284.2 46.6 %all-gather.21.cloned.1.call-done = bf16[1536,8960]{1,0:T(8,128)(2,1)} async-done(((bf16[48,8960]{1,0:T(8,128)(2,1)}), bf16[1536,8960]{1,0:T(8,128)(2,1)}) %all-gather.21.cloned.1.call-update) | async-done | bytes 27525136 | tf_op jit(solution)/shard_map/all_gather | solution.py:152
  330.8 14.9 fusion.47
  345.7 151.9 %all-gather.23.cloned.1.call-done = bf16[1536,8960]{1,0:T(8,128)(2,1)} async-done(((bf16[48,8960]{1,0:T(8,128)(2,1)}), bf16[1536,8960]{1,0:T(8,128)(2,1)}) %all-gather.23.cloned.1.call-update) | async-done | bytes 27525136 | tf_op jit(solution)/shard_map/all_gather | solution.py:153
  497.6 15.2 fusion.48
  512.9 151.6 %all-gather.25.cloned.1.call-done = bf16[1536,8960]{1,0:T(8,128)(2,1)} async-done(((bf16[48,8960]{1,0:T(8,128)(2,1)}), bf16[1536,8960]{1,0:T(8,128)(2,1)}) %all-gather.25.cloned.1.call-update) | async-done | bytes 27525136 | tf_op jit(solution)/shard_map/all_gather | solution.py:154
  664.5 25.1 %multiply_convert_fusion = (bf16[256,8960]{1,0:T(8,128)(2,1)}, bf16[256,8960]{1,0:T(8,128)(2,1)}, bf16[256,8960]{1,0:T(8,128)(2,1)}) fusion(f32[256,8960]{1,0:T(8,128)} %fusion.47, f32[256,8960]{1,0:T(8,128)} %fusion.48, bf16[1536,8960]{1,0:T(8,128)(2,1)} %all-gather.25.cloned.1.call-done, bf16[1,256,1536]{2,1,0:T(8,128)(2,1)S(1)} %copy-done.7), kind=kOutput, calls=%fused_computation.14 | convolution fusion | flops 7080837120 | bytes 60424192 | tf_op jit(solution)/shard_map/dot_general | solution.py:60
  689.6 14.9 fusion.49
  704.5 14.7 multiply_reduce_fusion
  721.7 4.8 convolution_convert_fusion.5
  728.0 10.4 fusion
  740.7 6.2 fusion.9
  747.0 3.5 fusion.30
  750.5 8.0 fusion.7
  760.6 3.8 convolution_multiply_fusion
  765.0 10.9 reduce-scatter.8.cloned.1.call-done
  777.0 27.7 %reduce-scatter.10.cloned.1.call-done = f32[1,256,256]{1,2,0:T(8,128)} async-done(((f32[1,1024,256]{1,2,0:T(8,128)}), f32[1,256,256]{1,2,0:T(8,128)}) %reduce-scatter.10.cloned.1.call-update) | async-done | bytes 262160 | tf_op jit(solution)/shard_map/reduce_scatter | solution.py:250
  810.6 58.4 %all-gather.31.cloned.1.call-done = bf16[1024,1536]{1,0:T(8,128)(2,1)} async-done(((bf16[256,1536]{1,0:T(8,128)(2,1)}), bf16[1024,1536]{1,0:T(8,128)(2,1)}) %all-gather.31.cloned.1.call-update) | async-done | bytes 3145744 | tf_op jit(solution)/shard_map/all_gather | solution.py:272
  869.0 4.6 copy.78
  874.9 58.4 %all-gather.33.cloned.1.call-done = bf16[1024,1536]{0,1:T(8,128)(2,1)} async-done(((bf16[256,1536]{0,1:T(8,128)(2,1)}), bf16[1024,1536]{0,1:T(8,128)(2,1)}) %all-gather.33.cloned.1.call-update) | async-done | bytes 3145744 | tf_op jit(solution)/shard_map/all_gather | solution.py:273
  933.3 4.3 convolution_convert_fusion.4
  937.7 58.7 %all-gather.27.cloned.1.call-done = bf16[1024,1536]{1,0:T(8,128)(2,1)} async-done(((bf16[256,1536]{1,0:T(8,128)(2,1)}), bf16[1024,1536]{1,0:T(8,128)(2,1)}) %all-gather.27.cloned.1.call-update) | async-done | bytes 3145744 | tf_op jit(solution)/shard_map/all_gather | solution.py:270
  996.4 4.7 copy.77
  1002.3 75.5 %all-gather.29.cloned.1.call-done = bf16[1024,2048]{0,1:T(8,128)(2,1)} async-done(((bf16[256,2048]{0,1:T(8,128)(2,1)}), bf16[1024,2048]{0,1:T(8,128)(2,1)}) %all-gather.29.cloned.1.call-update) | async-done | bytes 4194320 | tf_op jit(solution)/shard_map/all_gather | solution.py:271
  1077.8 5.2 convolution_convert_fusion.3
  1083.0 57.9 %all-gather.35.cloned.1.call-done = bf16[1024,1536]{1,0:T(8,128)(2,1)} async-done(((bf16[256,1536]{1,0:T(8,128)(2,1)}), bf16[1024,1536]{1,0:T(8,128)(2,1)}) %all-gather.35.cloned.1.call-update) | async-done | bytes 3145744 | tf_op jit(solution)/shard_map/all_gather | solution.py:179
  1141.0 4.7 copy.79
  1146.9 308.4 %all-gather.37.cloned.1.call-done = bf16[1024,8960]{1,0:T(8,128)(2,1)} async-done(((bf16[256,8960]{1,0:T(8,128)(2,1)}), bf16[1024,8960]{1,0:T(8,128)(2,1)}) %all-gather.37.cloned.1.call-update) | async-done | bytes 18350096 | tf_op jit(solution)/shard_map/all_gather | solution.py:180
  1455.3 15.4 convolution_convert_fusion.2
  1470.7 299.0 %all-gather.39.cloned.1.call-done = bf16[1024,8960]{1,0:T(8,128)(2,1)} async-done(((bf16[256,8960]{1,0:T(8,128)(2,1)}), bf16[1024,8960]{1,0:T(8,128)(2,1)}) %all-gather.39.cloned.1.call-update) | async-done | bytes 18350096 | tf_op jit(solution)/shard_map/all_gather | solution.py:181
  1769.7 15.4 convolution_convert_fusion.1
  1785.4 48.1 %all-gather.43.cloned.1.call-done = bf16[1,1024,1536]{1,2,0:T(8,128)(2,1)} async-done(((bf16[1,256,1536]{1,2,0:T(8,128)(2,1)}), bf16[1,1024,1536]{1,2,0:T(8,128)(2,1)}) %all-gather.43.cloned.1.call-update) | async-done | bytes 3145744 | tf_op jit(solution)/shard_map/all_gather | solution.py:183
  1834.7 312.5 %all-gather.41.cloned.1.call-done = bf16[1024,8960]{1,0:T(8,128)(2,1)} async-done(((bf16[256,8960]{1,0:T(8,128)(2,1)}), bf16[1024,8960]{1,0:T(8,128)(2,1)}) %all-gather.41.cloned.1.call-update) | async-done | bytes 18350096 | tf_op jit(solution)/shard_map/all_gather | solution.py:182
  2147.1 15.3 convolution_convert_fusion
  2162.5 5.3 fusion.50
  2167.9 13.9 fusion.14
  2185.7 39.3 %all-reduce.10 = (f32[1536]{0:T(1024)S(1)}, f32[1536]{0:T(1024)S(1)}, f32[256]{0:T(256)S(1)}, f32[256]{0:T(256)S(1)}, f32[1536]{0:T(1024)S(1)}) all-reduce(f32[1536]{0:T(1024)S(1)} %get-tuple-element.16, f32[1536]{0:T(1024)S(1)} %bitcast.193, f32[256]{0:T(256)S(1)} %bitcast.197, ...), channel_id=6, replica_groups=mesh['dp'=8,'ctx'=4] {'dp','ctx'}, use_global_device_ids=true, to_apply=%region_10.11.clone | all-reduce | flops 5120 | bytes 40960
  2227.9 3.9 fusion.24
  2236.5 61.1 %reduce-scatter.16.cloned.1.call-done = bf16[48,8960]{1,0:T(8,128)(2,1)} async-done(((bf16[384,8960]{1,0:T(8,128)(2,1)}), bf16[48,8960]{1,0:T(8,128)(2,1)}) %reduce-scatter.16.cloned.1.call-update) | async-done | bytes 860176 | tf_op jit(solution)/shard_map/reduce_scatter | solution.py:188
  2300.1 65.5 %reduce-scatter.18.cloned.1.call-done = bf16[48,8960]{1,0:T(8,128)(2,1)} async-done(((bf16[384,8960]{1,0:T(8,128)(2,1)}), bf16[48,8960]{1,0:T(8,128)(2,1)}) %reduce-scatter.18.cloned.1.call-update) | async-done | bytes 860176 | tf_op jit(solution)/shard_map/reduce_scatter | solution.py:194
  2368.0 66.0 %reduce-scatter.20.cloned.1.call-done = bf16[48,8960]{1,0:T(8,128)(2,1)} async-done(((bf16[384,8960]{1,0:T(8,128)(2,1)}), bf16[48,8960]{1,0:T(8,128)(2,1)}) %reduce-scatter.20.cloned.1.call-update) | async-done | bytes 860176 | tf_op jit(solution)/shard_map/reduce_scatter | solution.py:200
  (184 shorter events, 67.9 us)
Async XLA Ops:
  7.2 129.7 %copy-start.2 = (bf16[1,256,1536]{2,1,0:T(8,128)(2,1)S(1)}, bf16[1,256,1536]{2,1,0:T(8,128)(2,1)}, u32[]{:S(2)}) copy-start(bf16[1,256,1536]{2,1,0:T(8,128)(2,1)} %param.15) | copy-start | bytes 2359300
  7.2 249.3 %all-gather.17.cloned.1.call-start = ((), (), s32[]{:S(2)}) async-start(), calls=%async_computation.7 | async-start | bytes 4866048 | tf_op jit(solution)/shard_map/all_gather | solution.py:111
  7.9 271.9 %all-gather.19.cloned.1.call-start = ((), (), s32[]{:S(2)}) async-start(), calls=%async_computation.8 | async-start | bytes 4866048 | tf_op jit(solution)/shard_map/all_gather | solution.py:114
  8.7 322.2 %all-gather.21.cloned.1.call-start = ((), (), s32[]{:S(2)}) async-start(), calls=%async_computation.9 | async-start | bytes 28385280 | tf_op jit(solution)/shard_map/all_gather | solution.py:152
  9.4 147.7 %copy-start.23 = (bf16[48,256]{1,0:T(8,128)(2,1)S(1)}, bf16[48,256]{1,0:T(8,128)(2,1)}, u32[]{:S(2)}) copy-start(bf16[48,256]{1,0:T(8,128)(2,1)} %param.21) | copy-start | bytes 73732
  9.4 488.2 %all-gather.23.cloned.1.call-start = ((), (), s32[]{:S(2)}) async-start(), calls=%async_computation.10 | async-start | bytes 28385280 | tf_op jit(solution)/shard_map/all_gather | solution.py:153
  10.0 654.5 %all-gather.25.cloned.1.call-start = ((), (), s32[]{:S(2)}) async-start(), calls=%async_computation.11 | async-start | bytes 28385280 | tf_op jit(solution)/shard_map/all_gather | solution.py:154
  10.6 765.3 %reduce-scatter.8.cloned.1.call-start = ((), (), s32[]{:S(2)}) async-start(), calls=%async_computation.12 | async-start | bytes 1310720 | tf_op jit(solution)/shard_map/reduce_scatter | solution.py:247
  57.4 79.7 %copy-start.19 = (f32[1536]{0:T(1024)}, f32[1536]{0:T(1024)S(1)}, u32[]{:S(2)}) copy-start(f32[1536]{0:T(1024)S(1)} %convert_element_type.157) | copy-start | bytes 18436
  59.6 77.6 %copy-start.26 = (f32[256]{0:T(256)}, f32[256]{0:T(256)S(1)}, u32[]{:S(2)}) copy-start(f32[256]{0:T(256)S(1)} %add_rsqrt_fusion.1) | copy-start | bytes 3076
  136.9 19.9 copy-start.16
  137.1 124.3 %copy-start.6 = (bf16[256,1536]{1,0:T(8,128)(2,1)}, bf16[256,1536]{1,0:T(8,128)(2,1)S(1)}, u32[]{:S(2)}) copy-start(bf16[256,1536]{1,0:T(8,128)(2,1)S(1)} %fusion.19) | copy-start | bytes 2359300
  237.7 23.7 copy-start.9
  264.4 4.2 copy-start.12
  271.5 4.5 copy-start
  271.5 4.5 copy-start.18
  279.8 4.2 copy-start.21
  283.9 435.3 %copy-start.24 = (f32[256]{0:T(256)}, f32[256]{0:T(256)S(1)}, u32[]{:S(2)}) copy-start(f32[256]{0:T(256)S(1)} %add_rsqrt_fusion) | copy-start | bytes 3076
  284.2 46.6 %copy-start.14 = (bf16[256,1536]{1,0:T(8,128)(2,1)}, bf16[256,1536]{1,0:T(8,128)(2,1)S(1)}, u32[]{:S(2)}) copy-start(bf16[256,1536]{1,0:T(8,128)(2,1)S(1)} %multiply_convert_fusion.3) | copy-start | bytes 2359300
  345.7 318.7 %copy-start.7 = (bf16[1,256,1536]{2,1,0:T(8,128)(2,1)S(1)}, bf16[1,256,1536]{2,1,0:T(8,128)(2,1)}, u32[]{:S(2)}) copy-start(bf16[1,256,1536]{2,1,0:T(8,128)(2,1)} %param.16) | copy-start | bytes 2359300
  728.0 10.4 slice-start
  728.0 11.6 slice-start.1
  728.0 12.7 slice-start.2
  740.7 6.2 copy-start.5
  750.4 10.2 copy-start.13
  750.5 54.3 %reduce-scatter.10.cloned.1.call-start = ((), (), s32[]{:S(2)}) async-start(), calls=%async_computation.13 | async-start | bytes 1310720 | tf_op jit(solution)/shard_map/reduce_scatter | solution.py:250
  758.5 110.5 %all-gather.31.cloned.1.call-start = ((), (), s32[]{:S(2)}) async-start(), calls=%async_computation.17 | async-start | bytes 3932160 | tf_op jit(solution)/shard_map/all_gather | solution.py:272
  759.3 174.0 %all-gather.33.cloned.1.call-start = ((), (), s32[]{:S(2)}) async-start(), calls=%async_computation.18 | async-start | bytes 3932160 | tf_op jit(solution)/shard_map/all_gather | solution.py:273
  760.0 236.4 %all-gather.27.cloned.1.call-start = ((), (), s32[]{:S(2)}) async-start(), calls=%async_computation.14 | async-start | bytes 3932160 | tf_op jit(solution)/shard_map/all_gather | solution.py:270
  760.6 317.2 %all-gather.29.cloned.1.call-start = ((), (), s32[]{:S(2)}) async-start(), calls=%async_computation.15 | async-start | bytes 5242880 | tf_op jit(solution)/shard_map/all_gather | solution.py:271
  765.0 43.2 %copy-start.15 = (bf16[256,12,128]{0,2,1:T(8,128)(2,1)}, bf16[256,12,128]{0,2,1:T(8,128)(2,1)S(1)}, u32[]{:S(2)}) copy-start(bf16[256,12,128]{0,2,1:T(8,128)(2,1)S(1)} %get-tuple-element.33) | copy-start | bytes 2359300
  806.8 334.1 %all-gather.35.cloned.1.call-start = ((), (), s32[]{:S(2)}) async-start(), calls=%async_computation.20 | async-start | bytes 3932160 | tf_op jit(solution)/shard_map/all_gather | solution.py:179
  807.4 647.8 %all-gather.37.cloned.1.call-start = ((), (), s32[]{:S(2)}) async-start(), calls=%async_computation.21 | async-start | bytes 22937600 | tf_op jit(solution)/shard_map/all_gather | solution.py:180
  808.2 961.5 %all-gather.39.cloned.1.call-start = ((), (), s32[]{:S(2)}) async-start(), calls=%async_computation.23 | async-start | bytes 22937600 | tf_op jit(solution)/shard_map/all_gather | solution.py:181
  808.8 1024.7 %all-gather.43.cloned.1.call-start = ((), (), s32[]{:S(2)}) async-start(), calls=%async_computation.27 | async-start | bytes 3932160 | tf_op jit(solution)/shard_map/all_gather | solution.py:183
  810.0 1337.1 %all-gather.41.cloned.1.call-start = ((), (), s32[]{:S(2)}) async-start(), calls=%async_computation.25 | async-start | bytes 22937600 | tf_op jit(solution)/shard_map/all_gather | solution.py:182
  810.6 1421.2 %reduce-scatter.14.cloned.1.call-start = ((), (), s32[]{:S(2)}) async-start(), calls=%async_computation.19 | async-start | bytes 1327104 | tf_op jit(solution)/shard_map/reduce_scatter | solution.py:284
  937.6 1295.8 %reduce-scatter.12.cloned.1.call-start = ((), (), s32[]{:S(2)}) async-start(), calls=%async_computation.16 | async-start | bytes 1769472 | tf_op jit(solution)/shard_map/reduce_scatter | solution.py:278
  1083.0 1214.6 %reduce-scatter.16.cloned.1.call-start = ((), (), s32[]{:S(2)}) async-start(), calls=%async_computation.22 | async-start | bytes 7741440 | tf_op jit(solution)/shard_map/reduce_scatter | solution.py:188
  1470.6 894.9 %reduce-scatter.18.cloned.1.call-start = ((), (), s32[]{:S(2)}) async-start(), calls=%async_computation.24 | async-start | bytes 7741440 | tf_op jit(solution)/shard_map/reduce_scatter | solution.py:194
  1785.1 648.9 %reduce-scatter.20.cloned.1.call-start = ((), (), s32[]{:S(2)}) async-start(), calls=%async_computation.26 | async-start | bytes 7741440 | tf_op jit(solution)/shard_map/reduce_scatter | solution.py:200
  2162.5 5.4 slice-start.3
  2162.5 5.3 slice-start.4
  2167.8 13.9 copy-start.10
  2167.8 15.9 copy-start.20
  2167.8 15.9 copy-start.27
  2181.8 46.2 %copy-start.22 = (f32[1536]{0:T(1024)S(1)}, f32[1536]{0:T(1024)}, u32[]{:S(2)}) copy-start(f32[1536]{0:T(1024)} %convert_element_type.170) | copy-start | bytes 18436
  2181.8 46.2 %copy-start.25 = (f32[256]{0:T(256)S(1)}, f32[256]{0:T(256)}, u32[]{:S(2)}) copy-start(f32[256]{0:T(256)} %copy-done.24) | copy-start | bytes 3076
  (7 other events, 16.9 us)
Sparse Core Ops, SparseCore 0:
  10.8 67.9 all-gather.16
  81.6 68.0 all-gather.18
  152.6 178.2 all-gather.20
  333.5 164.0 all-gather.22
  500.3 164.0 all-gather.24
  750.6 25.2 reduce-scatter.7
  778.9 25.8 reduce-scatter.9
  806.9 62.1 all-gather.30
  871.2 62.0 all-gather.32
  934.7 61.6 all-gather.26
  998.6 79.1 all-gather.28
  1079.2 61.6 all-gather.34
  1142.5 312.6 all-gather.36
  1456.7 312.9 all-gather.38
  1771.1 62.3 all-gather.42
  1834.9 312.2 all-gather.40
  2150.8 35.6 reduce-scatter.13
  2190.6 38.4 reduce-scatter.11
  2233.0 64.5 reduce-scatter.15
  2300.9 64.5 reduce-scatter.17
  2369.4 64.5 reduce-scatter.19
where the time goes:
time: 2450 us; the launch traced here: 2440 us
  waiting for transfers between devices  1870 us (76%)
  blocking collectives  275 us (11%)
  matrix products  211 us (9%)
  local copies, waits for them, and re-layouts  43.7 us (2%)
  other arithmetic  32.1 us (1%)
    all_gather x1, waiting for transfers between devices, per_device(): lax.all_gather(act, 'ctx', axis=0, tiled=True)  312 us
    all_gather x1, waiting for transfers between devices, per_device(): lax.all_gather(grad_gate, 'ctx', axis=0, tiled=True)  308 us
    all_gather x1, waiting for transfers between devices, per_device(): lax.all_gather(grad_up, 'ctx', axis=0, tiled=True)  299 us
    all_gather x1, waiting for transfers between devices, per_device(): lax.all_gather(w_up, ('dp', 'ctx'), axis=0, tiled=True)  152 us
    all_gather x1, waiting for transfers between devices, per_device(): lax.all_gather(w_down, ('dp', 'ctx'), axis=0, tiled=True)  152 us
    unnamed x2, blocking collectives  81.8 us
    all_gather x1, blocking collectives, per_device(): lax.all_gather(w_key, ('dp', 'ctx'), axis=0, tiled=True)  80.5 us
    all_gather x1, blocking collectives, per_device(): lax.all_gather(w_value, ('dp', 'ctx'), axis=0, tiled=True)  77.3 us
  transfers between devices with their start and end apart: 21, of which 17 were waited for; matrix products, arithmetic and copies ran while one was open for 8% of the time, Pallas kernels for 0%

commit v1 on v0

--- a/solution.py
+++ b/solution.py
@@ -1,6 +1,10 @@
+import functools
+
 import jax
 import jax.numpy as jnp
 from jax import lax
+from jax.experimental import pallas as pl
+from jax.experimental.pallas import tpu as pltpu
 from jax.sharding import PartitionSpec as P
 
 D = 1536
@@ -72,7 +76,483 @@
     return jnp.einsum("rc,rf->cf", left, right, preferred_element_type=jnp.float32)
 
 
-def per_device(
+MESH = pl.DeviceIdType.MESH
+
+
+def flip(index, mask):
+    for bit in (1, 2, 4, 8, 16):
+        if mask & bit:
+            index = index + bit - 2 * bit * ((index // bit) % 2)
+    return index
+
+
+def either(a, b):
+    return a + b - 2 * a * b
+
+
+def dot(a, b, dims):
+    return lax.dot_general(a, b, (dims, ((), ())), preferred_element_type=jnp.float32)
+
+
+def ffn_kernel(
+    ctx_size, n_own, go_own, go_p, go_y, go_py, go_core, sgu, sd, xgu, xd, zgu, zd, xzgu, xzd,
+    hr, dgu, dd,
+    wgu, wd, nt, go, ggu, act, csend, crecv, hpart, stage,
+    w_sem, io_sem, n_send, n_recv, f_send, f_recv, c_send, c_recv, o_send, o_recv, st_sem,
+):
+    dp = lax.axis_index("dp")
+    ctx = lax.axis_index("ctx")
+    me = dp * ctx_size + ctx
+    y, x, c = dp // 4, (dp // 2) % 2, dp % 2
+    h, p = ctx // 2, ctx % 2
+    width = wd.shape[1]
+    shard = sgu.shape[2]
+    rows, model = n_own.shape
+
+    def at(index):
+        return (index // ctx_size, index % ctx_size)
+
+    core = at(flip(me, 4))
+
+    def partner(o):
+        return (dp + (o // 2) * 4 * (1 - 2 * y), ctx + (o % 2) * (1 - 2 * p))
+
+    barrier = pltpu.get_barrier_semaphore()
+    for device in (core, partner(1), partner(2), partner(3)):
+        pl.semaphore_signal(barrier, inc=1, device_id=device, device_id_type=MESH)
+
+    load_n = pltpu.make_async_copy(n_own, nt.at[0], io_sem.at[0])
+    load_n.start()
+    go_loads = []
+    for o, ref in enumerate((go_own, go_p, go_y, go_py)):
+        go_loads.append(pltpu.make_async_copy(ref, go.at[2 * o], io_sem.at[1 + o]))
+        go_loads.append(pltpu.make_async_copy(go_core.at[o], go.at[2 * o + 1], io_sem.at[5 + o]))
+    for copy in go_loads:
+        copy.start()
+    for mask, (gu_ref, d_ref) in ((0, (sgu, sd)), (8, (xgu, xd)), (2, (zgu, zd)), (10, (xzgu, xzd))):
+        for j in range(8):
+            rel = mask + (j // 4) * 16 + ((j // 2) % 2) * 4 + j % 2
+            row = pl.ds(pl.multiple_of(flip(me, rel) * shard, shard), shard)
+            pltpu.make_async_copy(gu_ref.at[j, 0], wgu.at[row, pl.ds(0, width)], w_sem.at[0]).start()
+            pltpu.make_async_copy(gu_ref.at[j, 1], wgu.at[row, pl.ds(width, width)], w_sem.at[0]).start()
+            pltpu.make_async_copy(d_ref.at[j], wd.at[row], w_sem.at[1]).start()
+
+    pl.semaphore_wait(barrier, 4)
+    load_n.wait()
+
+    def push_n(slot, dst, device, send, recv):
+        return pltpu.make_async_remote_copy(
+            src_ref=nt.at[slot], dst_ref=nt.at[dst], send_sem=send, recv_sem=recv,
+            device_id=device, device_id_type=MESH,
+        )
+
+    first = [push_n(0, 2 * o, partner(o), n_send.at[o], n_recv.at[o]) for o in (1, 2, 3)]
+    for copy in first:
+        copy.start()
+    push_n(0, 1, core, f_send.at[0], f_recv.at[0]).start()
+    pltpu.make_async_copy(wgu, wgu, w_sem.at[0]).wait()
+    pltpu.make_async_copy(wd, wd, w_sem.at[1]).wait()
+    for copy in go_loads:
+        copy.wait()
+
+    def tile(slot):
+        gu = dot(nt[slot], wgu[...], ((1,), (0,)))
+        ga = dot(go[slot], wd[...], ((1,), (0,)))
+        gate, up = gu[:, :width], gu[:, width:]
+        sig = 1.0 / (1.0 + jnp.exp(-gate))
+        silu = gate * sig
+        act[slot] = (silu * up).astype(jnp.bfloat16)
+        ggu[slot, :, pl.ds(0, width)] = (ga * up * sig * (1.0 + gate * (1.0 - sig))).astype(jnp.bfloat16)
+        ggu[slot, :, pl.ds(width, width)] = (ga * silu).astype(jnp.bfloat16)
+        grad = dot(ggu[slot], wgu[...], ((1,), (1,)))
+        out = dot(act[slot], wd[...], ((1,), (1,)))
+        return (grad.astype(jnp.bfloat16), out.astype(jnp.bfloat16))
+
+    def cross(o):
+        return pltpu.make_async_remote_copy(
+            src_ref=csend, dst_ref=crecv.at[o % 2], send_sem=c_send, recv_sem=c_recv.at[o % 2],
+            device_id=core, device_id_type=MESH,
+        )
+
+    def final(o):
+        return pltpu.make_async_remote_copy(
+            src_ref=hpart.at[o], dst_ref=hr.at[o], send_sem=o_send.at[o], recv_sem=o_recv.at[o],
+            device_id=partner(o), device_id_type=MESH,
+        )
+
+    keep = pltpu.make_async_copy(hpart.at[0], hr.at[0], io_sem.at[0])
+
+    def combine(o):
+        cross(o).wait_recv()
+        total = hpart[o].astype(jnp.float32) + crecv[o % 2].astype(jnp.float32)
+        hpart[o] = total.astype(jnp.bfloat16)
+
+    def step(o, carry):
+        @pl.when(o > 0)
+        def _():
+            push_n(0, 2 * o, partner(o), n_send.at[o], n_recv.at[o]).wait_recv()
+            push_n(2 * o, 2 * o + 1, core, f_send.at[o], f_recv.at[o]).start()
+
+        grad, out = tile(2 * o)
+        hpart[o, 0] = grad
+        hpart[o, 1] = out
+
+        @pl.when(o > 0)
+        def _():
+            combine(o - 1)
+
+        @pl.when(o == 1)
+        def _():
+            keep.start()
+
+        @pl.when(o > 1)
+        def _():
+            final(o - 1).start()
+
+        push_n(2 * o, 2 * o + 1, core, f_send.at[o], f_recv.at[o]).wait_recv()
+        grad, out = tile(2 * o + 1)
+
+        @pl.when(o > 0)
+        def _():
+            cross(o).wait_send()
+
+        csend[0] = grad
+        csend[1] = out
+        cross(o).start()
+        return carry
+
+    lax.fori_loop(0, 4, step, 0)
+    combine(3)
+    final(3).start()
+
+    def stage_wait(slot):
+        pltpu.make_async_copy(stage.at[slot], stage.at[slot], st_sem.at[slot]).wait()
+
+    def weights(q, carry):
+        slot = q % 2
+
+        @pl.when(q > 1)
+        def _():
+            stage_wait(slot)
+
+        chunk = 8 * shard
+        cols = pl.ds(pl.multiple_of(q * chunk, chunk), chunk)
+        left = nt[:, :, cols].reshape(8 * rows, chunk)
+        for half in range(2):
+            part = pl.ds(half * width, width)
+            right = ggu[:, :, part].reshape(8 * rows, width)
+            stage[slot, :, part] = dot(left, right, ((0,), (0,))).astype(jnp.bfloat16)
+        left = go[:, :, cols].reshape(8 * rows, chunk)
+        right = act[...].reshape(8 * rows, width)
+        stage[slot, :, pl.ds(2 * width, width)] = dot(left, right, ((0,), (0,))).astype(jnp.bfloat16)
+        yr, xr = either(q // 2, y), either(q % 2, x)
+        for j in range(8):
+            cr, hrel, pr = either(j // 4, c), either((j // 2) % 2, h), either(j % 2, p)
+            block = yr * 4 + cr * 2 + pr
+            row = pl.ds(j * shard, shard)
+            for half in range(2):
+                pltpu.make_async_copy(
+                    stage.at[slot, row, pl.ds(half * width, width)], dgu.at[xr, hrel, block, half], st_sem.at[slot]
+                ).start()
+            pltpu.make_async_copy(
+                stage.at[slot, row, pl.ds(2 * width, width)], dd.at[xr, hrel, block], st_sem.at[slot]
+            ).start()
+        return carry
+
+    lax.fori_loop(0, 4, weights, 0)
+    stage_wait(0)
+    stage_wait(1)
+    keep.wait()
+    cross(3).wait_send()
+    for copy in first:
+        copy.wait_send()
+    for o in range(4):
+        push_n(2 * o, 2 * o + 1, core, f_send.at[o], f_recv.at[o]).wait_send()
+    for o in (1, 2, 3):
+        final(o).wait()
+
+
+def ffn_call(ctx_size, n_own, go_tiles, weights):
+    rows, model = n_own.shape
+    shard, width = weights[0].shape[2:]
+    low = jnp.bfloat16
+    return pl.pallas_call(
+        functools.partial(ffn_kernel, ctx_size),
+        out_shape=(
+            jax.ShapeDtypeStruct((4, 2, rows, model), low),
+            jax.ShapeDtypeStruct((2, 2, 8, 2, shard, width), low),
+            jax.ShapeDtypeStruct((2, 2, 8, shard, width), low),
+        ),
+        in_specs=[pl.BlockSpec(memory_space=pl.ANY)] * 14,
+        out_specs=[pl.BlockSpec(memory_space=pl.ANY)] * 3,
+        scratch_shapes=[
+            pltpu.VMEM((model, 2 * width), low),
+            pltpu.VMEM((model, width), low),
+            pltpu.VMEM((8, rows, model), low),
+            pltpu.VMEM((8, rows, model), low),
+            pltpu.VMEM((8, rows, 2 * width), low),
+            pltpu.VMEM((8, rows, width), low),
+            pltpu.VMEM((2, rows, model), low),
+            pltpu.VMEM((2, 2, rows, model), low),
+            pltpu.VMEM((4, 2, rows, model), low),
+            pltpu.VMEM((2, 8 * shard, 3 * width), low),
+            pltpu.SemaphoreType.DMA((2,)),
+            pltpu.SemaphoreType.DMA((9,)),
+            pltpu.SemaphoreType.DMA((4,)),
+            pltpu.SemaphoreType.DMA((4,)),
+            pltpu.SemaphoreType.DMA((4,)),
+            pltpu.SemaphoreType.DMA((4,)),
+            pltpu.SemaphoreType.DMA,
+            pltpu.SemaphoreType.DMA((2,)),
+            pltpu.SemaphoreType.DMA((4,)),
+            pltpu.SemaphoreType.DMA((4,)),
+            pltpu.SemaphoreType.DMA((2,)),
+        ],
+        compiler_params=pltpu.CompilerParams(
+            collective_id=1, has_side_effects=True, vmem_limit_bytes=63 << 20
+        ),
+        name="ffn",
+    )(n_own, *go_tiles, *weights)
+
+
+def permute(value, mask, size):
+    return lax.ppermute(value, ("dp", "ctx"), [(i, i ^ mask) for i in range(size)])
+
+
+def fits(mesh):
+    return mesh.shape["dp"] == 8 and mesh.shape["ctx"] == 4
+
+
+def fast_device(
+    hidden,
+    cotangent,
+    span_order,
+    attn_gain,
+    w_query,
+    b_query,
+    w_key,
+    b_key,
+    w_value,
+    b_value,
+    w_out,
+    ffn_gain,
+    w_gate,
+    w_up,
+    w_down,
+):
+    ctx_size = lax.axis_size("ctx")
+    ctx_rank = lax.axis_index("ctx")
+    size = lax.axis_size("dp") * ctx_size
+    me = lax.axis_index("dp") * ctx_size + ctx_rank
+    batches = hidden.shape[0]
+    length = hidden.shape[1]
+    span_len = length // 2
+    seq_len = length * ctx_size
+    row_count = batches * length
+    groups = HEADS // KV_HEADS
+    shard_rows = w_query.shape[0]
+    head_scale = HD ** (-0.5)
+    kv_width = KV_HEADS * HD
+    q_width = HEADS * HD
+    both = ("dp", "ctx")
+
+    hidden_units = w_gate.shape[1]
+    piece = -(-hidden_units // (8 * 128)) * 128
+    stacked = jnp.pad(jnp.stack([w_gate, w_up, w_down]), ((0, 0), (0, 0), (0, 8 * piece - hidden_units)))
+    pieces = stacked.reshape(3, shard_rows, 4, 2, piece).transpose(2, 3, 0, 1, 4)
+    y, core, p = me // 16, (me // 4) % 2, me % 2
+    mine = lax.dynamic_index_in_dim(pieces, core, 1, False)
+    other = lax.dynamic_index_in_dim(pieces, 1 - core, 1, False)
+    other = permute(other, 4, size)
+    col = 2 * y + p
+    sets = []
+    for mask in (0, 1, 16, 17):
+        want = jnp.bitwise_xor(col, (mask // 16) * 2 + mask % 2)
+        chosen = jnp.stack(
+            [lax.dynamic_index_in_dim(mine, want, 0, False), lax.dynamic_index_in_dim(other, want, 0, False)]
+        )
+        sets.append(permute(chosen, mask, size) if mask else chosen)
+    whole = jnp.stack(sets)
+    whole = whole.reshape(2, 2, 2, 3, shard_rows, piece).transpose(0, 2, 1, 3, 4, 5)
+    whole = whole.reshape(8, 3, shard_rows, piece)
+    own_gu, own_d = whole[:, :2], whole[:, 2]
+    z_gu = permute(own_gu, 2, size)
+    x_gu = permute(own_gu, 8, size)
+    x_d = permute(own_d, 8, size)
+    z_d = permute(own_d, 2, size)
+    xz_gu = permute(z_gu, 8, size)
+    xz_d = permute(z_d, 8, size)
+
+    grad_out = cotangent.reshape(row_count, D)
+    go_tiles = [grad_out] + [permute(grad_out, mask, size) for mask in (1, 16, 17)]
+    go_core = permute(jnp.stack(go_tiles), 4, size)
+
+    places = jnp.arange(seq_len, dtype=jnp.int32)
+    every_pos = jnp.repeat(span_order, span_len, axis=1) * span_len + places[None, :] % span_len
+    local_pos = lax.dynamic_slice_in_dim(every_pos, ctx_rank * length, length, 1)
+    cosine, sine = angles_for(local_pos.reshape(row_count), HD)
+    allowed = (every_pos[:, None, :] <= local_pos[:, :, None])[:, None, None]
+
+    gains = jnp.stack([attn_gain, b_query, ffn_gain], axis=1)
+    pair = jnp.pad(jnp.concatenate([b_key, b_value]), (0, shard_rows - 2 * b_key.shape[0]))
+    packed = jnp.concatenate(
+        [w_query, w_key, w_value, gains, pair[:, None], jnp.zeros((shard_rows, 124), jnp.bfloat16)], axis=1
+    )
+    packed = lax.all_gather(packed, both, axis=0, tiled=True)
+    out_full = lax.all_gather(w_out, both, axis=0, tiled=True)
+    proj_width = q_width + 2 * kv_width
+    proj_full = packed[:, :proj_width]
+    small = packed[:, proj_width : proj_width + 4].astype(jnp.float32)
+    gain_one = small[:, 0]
+    gain_two = small[:, 2]
+    biases = small[:, 3].reshape(size, shard_rows)
+    per = b_key.shape[0]
+    bias = jnp.concatenate([small[:, 1], biases[:, :per].reshape(-1), biases[:, per : 2 * per].reshape(-1)])
+
+    source = hidden.reshape(row_count, D).astype(jnp.float32)
+    attn_factor, normed = norm_forward(source, gain_one)
+    raw = plain_dot(normed, proj_full) + bias
+    query_raw, key_raw = raw[:, :q_width], raw[:, q_width : q_width + kv_width]
+    value_low = raw[:, q_width + kv_width :].astype(jnp.bfloat16)
+    query_rot = rotate(query_raw.reshape(row_count, HEADS, HD), cosine, sine).astype(jnp.bfloat16)
+    query_rot = query_rot.reshape(batches, length, KV_HEADS, groups, HD)
+    key_rot = rotate(key_raw.reshape(row_count, KV_HEADS, HD), cosine, sine).astype(jnp.bfloat16)
+    key_value = jnp.concatenate([key_rot.reshape(row_count, kv_width), value_low], axis=1)
+    key_value = lax.all_gather(key_value.reshape(batches, length, 2 * kv_width), "ctx", axis=1, tiled=True)
+    key_all = key_value[:, :, :kv_width].reshape(batches, seq_len, KV_HEADS, HD)
+    value_all = key_value[:, :, kv_width:].reshape(batches, seq_len, KV_HEADS, HD)
+    scores = (
+        jnp.einsum("bqkgd,bskd->bkgqs", query_rot, key_all, preferred_element_type=jnp.float32)
+        * head_scale
+    )
+    masked = jnp.where(allowed, scores, masked_fill)
+    row_max = jnp.max(masked, axis=-1, keepdims=True)
+    expo = jnp.exp(masked - row_max)
+    expo_sum = jnp.sum(expo, axis=-1, keepdims=True)
+    log_total = row_max + jnp.log(expo_sum)
+    attend = (expo / expo_sum).astype(jnp.bfloat16)
+    mixed = jnp.einsum("bkgqs,bskd->bqkgd", attend, value_all, preferred_element_type=jnp.float32)
+    mixed = mixed.reshape(row_count, q_width).astype(jnp.bfloat16)
+    resid = source + right_dot(mixed, out_full)
+    ffn_factor, normed_two = norm_forward(resid, gain_two)
+
+    tiles, gu_grad, d_grad = ffn_call(
+        ctx_size, normed_two, go_tiles + [go_core], [own_gu, own_d, x_gu, x_d, z_gu, z_d, xz_gu, xz_d]
+    )
+    sums = jnp.sum(tiles.astype(jnp.float32), axis=0)
+    grad_norm_two = sums[0]
+    result = (resid + sums[1]).astype(jnp.bfloat16).reshape(batches, length, D)
+
+    def fold(part):
+        high = permute(part[1, 1], 8, size)
+        low_part = permute(part[1, 0], 8, size)
+        far = (part[0, 1].astype(jnp.float32) + high.astype(jnp.float32)).astype(jnp.bfloat16)
+        far = permute(far, 2, size)
+        near = part[0, 0].astype(jnp.float32) + low_part.astype(jnp.float32)
+        return (near + far.astype(jnp.float32)).astype(jnp.bfloat16)
+
+    d_sum = fold(d_grad)
+    gu_sum = fold(gu_grad)
+    whole_grad = jnp.concatenate([gu_sum, d_sum[:, None]], axis=1)
+    whole_grad = whole_grad.reshape(2, 2, 2, 3, shard_rows, piece)
+    parts = []
+    for mask in (0, 1, 16, 17):
+        part = whole_grad[mask // 16, :, mask % 2]
+        parts.append(permute(part, mask, size) if mask else part)
+    parts = jnp.stack(parts)
+    theirs = permute(parts[:, 1], 4, size)
+    ordered = jnp.stack([parts[:, 0], theirs], axis=0)
+    ordered = ordered[jnp.bitwise_xor(jnp.arange(2), core)]
+    ordered = ordered[:, jnp.bitwise_xor(jnp.arange(4), col)]
+    flat = ordered.transpose(2, 3, 1, 0, 4).reshape(3, shard_rows, 8 * piece)[:, :, :hidden_units]
+    flat = flat.astype(jnp.float32)
+    w_gate_grad, w_up_grad, w_down_grad = flat[0], flat[1], flat[2]
+
+    grad_plain = grad_out.astype(jnp.float32)
+    resid_back, ffn_gain_part = norm_backward(resid, ffn_factor, gain_two, grad_norm_two)
+    grad_resid = grad_plain + resid_back
+    grad_attn = grad_resid.astype(jnp.bfloat16)
+    grad_mixed = plain_dot(grad_attn, out_full).astype(jnp.bfloat16)
+    grad_mixed = grad_mixed.reshape(batches, length, KV_HEADS, groups, HD)
+    scores = (
+        jnp.einsum("bqkgd,bskd->bkgqs", query_rot, key_all, preferred_element_type=jnp.float32)
+        * head_scale
+    )
+    masked = jnp.where(allowed, scores, masked_fill)
+    attend_full = jnp.exp(masked - log_total)
+    attend = attend_full.astype(jnp.bfloat16)
+    grad_attend = jnp.einsum(
+        "bqkgd,bskd->bkgqs", grad_mixed, value_all, preferred_element_type=jnp.float32
+    )
+    value_grad_all = jnp.einsum(
+        "bkgqs,bqkgd->bskd", attend, grad_mixed, preferred_element_type=jnp.float32
+    )
+    delta = jnp.sum(grad_attend * attend_full, axis=-1, keepdims=True)
+    grad_scores = (attend_full * (grad_attend - delta)).astype(jnp.bfloat16)
+    query_grad_rot = (
+        jnp.einsum("bkgqs,bskd->bqkgd", grad_scores, key_all, preferred_element_type=jnp.float32)
+        * head_scale
+    )
+    key_grad_all = (
+        jnp.einsum("bkgqs,bqkgd->bskd", grad_scores, query_rot, preferred_element_type=jnp.float32)
+        * head_scale
+    )
+    kv_grad = jnp.concatenate(
+        [key_grad_all.reshape(batches, seq_len, kv_width), value_grad_all.reshape(batches, seq_len, kv_width)],
+        axis=2,
+    ).astype(jnp.bfloat16)
+    kv_grad = lax.psum_scatter(kv_grad, "ctx", scatter_dimension=1, tiled=True).astype(jnp.float32)
+    key_grad_rot, value_grad = kv_grad[:, :, :kv_width], kv_grad[:, :, kv_width:]
+    query_grad = (
+        rotate_back(query_grad_rot.reshape(row_count, HEADS, HD), cosine, sine)
+        .reshape(row_count, q_width)
+        .astype(jnp.bfloat16)
+    )
+    key_grad = (
+        rotate_back(key_grad_rot.reshape(row_count, KV_HEADS, HD), cosine, sine)
+        .reshape(row_count, kv_width)
+        .astype(jnp.bfloat16)
+    )
+    value_grad = value_grad.reshape(row_count, kv_width).astype(jnp.bfloat16)
+    proj_grad = jnp.concatenate([query_grad, key_grad, value_grad], axis=1)
+    grad_norm_one = right_dot(proj_grad, proj_full)
+    source_back, attn_gain_part = norm_backward(source, attn_factor, gain_one, grad_norm_one)
+    hidden_grad = (grad_resid + source_back).reshape(batches, length, D)
+
+    bias_part = jnp.sum(proj_grad.astype(jnp.float32), axis=0)
+    kv_bias = bias_part[q_width:].reshape(2, size, per).transpose(1, 0, 2).reshape(size, 2 * per)
+    kv_bias = jnp.pad(kv_bias, ((0, 0), (0, shard_rows - 2 * per))).reshape(-1)
+    columns = jnp.stack([attn_gain_part, bias_part[:q_width], ffn_gain_part, kv_bias], axis=1)
+    part = jnp.concatenate(
+        [outer_add(normed, proj_grad), columns, jnp.zeros((D, 124), jnp.float32)], axis=1
+    ).astype(jnp.bfloat16)
+    proj_sum = lax.psum_scatter(part, both, scatter_dimension=0, tiled=True).astype(jnp.float32)
+    w_out_grad = lax.psum_scatter(
+        outer_add(grad_attn, mixed).astype(jnp.bfloat16), both, scatter_dimension=0, tiled=True
+    ).astype(jnp.float32)
+    w_query_grad = proj_sum[:, :q_width]
+    w_key_grad = proj_sum[:, q_width : q_width + kv_width]
+    w_value_grad = proj_sum[:, q_width + kv_width : proj_width]
+    small = proj_sum[:, proj_width : proj_width + 4]
+    return (
+        result,
+        hidden_grad,
+        small[:, 0],
+        w_query_grad,
+        small[:, 1],
+        w_key_grad,
+        small[:per, 3],
+        w_value_grad,
+        small[per : 2 * per, 3],
+        w_out_grad,
+        small[:, 2],
+        w_gate_grad,
+        w_up_grad,
+        w_down_grad,
+    )
+
+
+def general_device(
     hidden,
     cotangent,
     span_order,
@@ -345,7 +825,7 @@
         P(("dp", "ctx"), None),
     )
     return jax.shard_map(
-        per_device,
+        fast_device if fits(mesh) else general_device,
         mesh=mesh,
         in_specs=placed,
         out_specs=(

time: 2450 us -> 902 us (0.37)
  waiting for transfers between devices: 1870 us -> 506 us
  blocking collectives: 275 us -> 0 us
  matrix products: 211 us -> 51.8 us
  Pallas kernels: 0 us -> 126 us
  local copies, waits for them, and re-layouts: 43.7 us -> 109 us
  starting transfers between devices: 1.29 us -> 35 us
    all_gather x14 -> x3, waiting for transfers between devices: 1630 us -> 59.6 us  [the longest x1 59.5 us: fast_device(): packed = lax.all_gather(packed, both, axis=0, tiled=True)]
    ppermute x0 -> x24, waiting for transfers between devices: none -> 344 us  [permute(): lax.ppermute(value, ('dp', 'ctx'), [(i, i ^ mask) for i in range(size)])]
    all_gather x4 -> x0, blocking collectives: 194 us -> none  [the longest x1 80.5 us: per_device(): lax.all_gather(w_key, ('dp', 'ctx'), axis=0, tiled=True)]
    reduce_scatter x7 -> x3, waiting for transfers between devices: 231 us -> 102 us  [the longest x1 102 us: fast_device(): lax.psum_scatter(part, both, scatter_dimension=0, tiled=True)]
    pallas_call x0 -> x1, Pallas kernels: none -> 126 us  [ffn_call(): pl.pallas_call(functools.partial(ffn_kernel, ctx_size), out_shape=(jax.Sh...]
    unnamed x2 -> x0, blocking collectives: 81.8 us -> none
    dot_general x7 -> x2, matrix products: 65.8 us -> 6.89 us  [plain_dot(): return jnp.dot(left, weight, preferred_element_type=jnp.float32)]
    dot_general x5 -> x2, matrix products: 55.5 us -> 8.3 us  [outer_add(): jnp.einsum('rc,rf->cf', left, right, preferred_element_type=jnp.float32)]
  transfers between devices with their start and end apart: 21 -> 30, of which waited for: 17 -> 13; matrix products, arithmetic and copies ran while one was open for 8% -> 15% of each run, Pallas kernels for 0% -> 0%
where the time goes in v1:
time: 902 us; the launch traced here: 893 us
  waiting for transfers between devices  506 us (56%)
  Pallas kernels  126 us (14%)
  local copies, waits for them, and re-layouts  109 us (12%)
  matrix products  51.8 us (6%)
  other arithmetic  50.8 us (6%)
  starting transfers between devices  35 us (4%)
  between operations  15.3 us (2%)
    ppermute x24, waiting for transfers between devices, permute(): lax.ppermute(value, ('dp', 'ctx'), [(i, i ^ mask) for i in range(size)])  344 us
    pallas_call x1, Pallas kernels, ffn_call(): pl.pallas_call(functools.partial(ffn_kernel, ctx_size), out_shape=(jax.Sh...  126 us
    reduce_scatter x1, waiting for transfers between devices, fast_device(): lax.psum_scatter(part, both, scatter_dimension=0, tiled=True)  102 us
    all_gather x1, waiting for transfers between devices, fast_device(): packed = lax.all_gather(packed, both, axis=0, tiled=True)  59.5 us
    ppermute x24, starting transfers between devices, permute(): lax.ppermute(value, ('dp', 'ctx'), [(i, i ^ mask) for i in range(size)])  34.3 us
  transfers between devices with their start and end apart: 30, of which 13 were waited for; matrix products, arithmetic and copies ran while one was open for 15% of the time, Pallas kernels for 0%

profile of v1, /device:TPU:0, one launch (start us, length us, event | category | flops | bytes accessed | tf_op | source)
XLA Modules:
  0.0 892.9 jit_solution(9089141141425366120)
XLA Ops:
  12.2 2.9 fusion.26
  15.1 6.2 reshape.504
  26.5 59.5 %all-gather.5.cloned.1.call-done = bf16[1536,2176]{1,0:T(8,128)(2,1)} async-done(((bf16[48,2176]{1,0:T(8,128)(2,1)}), bf16[1536,2176]{1,0:T(8,128)(2,1)}) %all-gather.5.cloned.1.call-update) | async-done | bytes 6684688 | tf_op jit(solution)/shard_map/all_gather | solution.py:401
  91.3 4.6 fusion.22
  103.5 2.7 dynamic-slice_bitcast_fusion
  108.4 2.7 constant_dynamic-slice_fusion.7
  116.7 26.9 %collective-permute-done.5 = bf16[2,3,48,1152]{3,2,1,0:T(8,128)(2,1)S(1)} collective-permute-done((bf16[2,3,48,1152]{3,2,1,0:T(8,128)(2,1)S(1)}, bf16[2,3,48,1152]{3,2,1,0:T(8,128)(2,1)S(1)}, u32[]{:S(2)}, u32[]{:S(2)}) %collective-permute-start.5) | collective-permute-done | bytes 663584 | tf_op jit(solution)/shard_map/ppermute | solution.py:319
  143.6 15.0 %collective-permute-done.7 = bf16[2,3,48,1152]{3,2,1,0:T(8,128)(2,1)S(1)} collective-permute-done((bf16[2,3,48,1152]{3,2,1,0:T(8,128)(2,1)S(1)}, bf16[2,3,48,1152]{3,2,1,0:T(8,128)(2,1)S(1)}, u32[]{:S(2)}, u32[]{:S(2)}) %collective-permute-start.7) | collective-permute-done | bytes 663584 | tf_op jit(solution)/shard_map/ppermute | solution.py:319
  159.4 2.5 collective-permute-start.10
  163.3 83.7 %collective-permute-done.10 = bf16[8,2,48,1152]{3,2,0,1:T(8,128)(2,1)S(1)} collective-permute-done((bf16[8,2,48,1152]{3,2,0,1:T(8,128)(2,1)S(1)}, bf16[8,2,48,1152]{3,2,0,1:T(8,128)(2,1)S(1)}, u32[]{:S(2)}, u32[]{:S(2)}) %collective-permute-start.10) | collective-permute-done | bytes 1769504 | tf_op jit(solution)/shard_map/ppermute | solution.py:319
  249.2 2.9 collective-permute-start.2
  253.0 28.6 %collective-permute-done.go_p = bf16[256,1536]{1,0:T(8,128)(2,1)S(1)} collective-permute-done((bf16[256,1536]{1,0:T(8,128)(2,1)S(1)}, bf16[256,1536]{1,0:T(8,128)(2,1)S(1)}, u32[]{:S(2)}, u32[]{:S(2)}) %collective-permute-start) | collective-permute-done | bytes 786464 | tf_op jit(solution)/shard_map/ppermute | solution.py:319
  281.6 9.7 %collective-permute-start.11 = (bf16[8,48,1152]{2,1,0:T(8,128)(2,1)}, bf16[8,48,1152]{2,1,0:T(8,128)(2,1)}, u32[]{:S(2)}, u32[]{:S(2)}) collective-permute-start(bf16[8,48,1152]{2,1,0:T(8,128)(2,1)} %slice_bitcast_fusion.9.sd), channel_id=1, source_target_pairs={{0,2},{1,3},{2,0},{3,1},{4,6},{5,7},{6,4},{7,5},{8,10},{9,11},{10,... | collective-permute-start | bytes 2654216 | tf_op jit(solution)/shard_map/ppermute | solution.py:319
  291.6 19.3 %collective-permute-done.2.go_py = bf16[256,1536]{1,0:T(8,128)(2,1)S(1)} collective-permute-done((bf16[256,1536]{1,0:T(8,128)(2,1)S(1)}, bf16[256,1536]{1,0:T(8,128)(2,1)S(1)}, u32[]{:S(2)}, u32[]{:S(2)}) %collective-permute-start.2) | collective-permute-done | bytes 786464 | tf_op jit(solution)/shard_map/ppermute | solution.py:319
  314.7 6.9 collective-permute-done.11.zd
  333.1 2.3 fusion.83
  339.9 2.9 fusion.88
  344.6 2.8 copy-done
  347.4 2.6 fusion.45
  350.0 4.1 multiply_reduce_fusion.2
  356.4 125.5 %ffn.1 = (bf16[4,2,256,1536]{3,2,1,0:T(8,128)(2,1)}, bf16[2,2,8,2,48,1152]{5,4,3,2,1,0:T(8,128)(2,1)}, bf16[2,2,8,48,1152]{4,3,2,1,0:T(8,128)(2,1)}) custom-call(bf16[256,1536]{1,0:T(8,128)(2,1)} %multiply_convert_fusion.n_own, bf16[256,1536]{1,0:T(8,128)(2,1)} %bitcast.241, bf16[256,1536]{1,0:T(8,128)(2,1)} %copy-done.15, bf16[256,1536]{1,0:T(8,128)(2,1)} %copy-done.16, ...), custom_call_target="tpu_custom_call" | custom-call | tf_op jit(solution)/shard_map/ffn/pallas_call | solution.py:279
  482.0 4.2 convert_reduce_fusion
  488.9 2.3 convolution_convert_fusion.2
  492.6 10.4 %fusion = (f32[2,6,256]{2,1,0:T(8,128)S(1)}, f32[2,1024,256,6]{2,1,3,0:T(8,128)}) fusion(f32[1,2,6,256,1024]{3,4,2,1,0:T(8,128)} %copy-done, f32[2,6,256]{2,1,0:T(8,128)S(1)} %log_add_fusion, bf16[256,2,6,128]{0,3,2,1:T(8,128)(2,1)S(1)} %bitcast.249, bf16[1024,2,128,1]{2,1,0,3:T(2,128)(2,1)} %bitcast.261), kind=kOutput, calls=%fused_computation.5 | convolution fusion | flops 814740480 | bytes 26501120 | tf_op jit(solution)/shard_map/bqkgd,bskd->bkgqs/dot_general | solution.py:484
  503.0 7.0 fusion.52
  510.0 6.5 fusion.8
  516.6 2.4 fusion.55
  520.8 3.6 convolution_convert_fusion.1
  524.5 3.8 slice_bitcast_fusion.1
  528.3 2.5 slice_bitcast_fusion.11
  537.2 51.6 %collective-permute-done.18 = bf16[8,48,1152]{2,1,0:T(8,128)(2,1)S(1)} collective-permute-done((bf16[8,48,1152]{2,1,0:T(8,128)(2,1)S(1)}, bf16[8,48,1152]{2,1,0:T(8,128)(2,1)S(1)}, u32[]{:S(2)}, u32[]{:S(2)}) %collective-permute-start.18) | collective-permute-done | bytes 884768 | tf_op jit(solution)/shard_map/ppermute | solution.py:319
  588.8 2.3 fusion.31
  592.6 3.2 fusion.19
  611.1 6.2 fusion.40
  618.3 4.7 convolution_convert_fusion
  623.1 11.5 %concatenate.80 = bf16[1536,2176]{1,0:T(8,128)(2,1)} concatenate(bf16[1536,2048]{1,0:T(8,128)(2,1)} %convolution_convert_fusion, bf16[1536,1]{1,0:T(8,128)(2,1)} %stack.127, bf16[1536,1]{1,0:T(8,128)(2,1)} %stack.128, bf16[1536,1]{1,0:T(8,128)(2,1)} %stack.129, bf16[1536,1]{1,0:T(8,128)(2,1)} %stack_reshape.5, bf16[1536,124]{1,0:T(8,128)(2,1)S(1)} %broadcast_in_dim.29), dimensions={1} | concatenate | bytes 13369344 | tf_op jit(solution)/shard_map/concatenate | solution.py:526
  634.6 39.6 %collective-permute-done.19 = bf16[8,48,1152]{2,1,0:T(8,128)(2,1)} collective-permute-done((bf16[8,48,1152]{2,1,0:T(8,128)(2,1)}, bf16[8,48,1152]{2,1,0:T(8,128)(2,1)}, u32[]{:S(2)}, u32[]{:S(2)}) %collective-permute-start.19) | collective-permute-done | bytes 884768 | tf_op jit(solution)/shard_map/ppermute | solution.py:319
  676.3 35.7 %collective-permute-done.16 = bf16[8,2,48,1152]{3,2,1,0:T(8,128)(2,1)S(1)} collective-permute-done((bf16[8,2,48,1152]{3,2,1,0:T(8,128)(2,1)}, bf16[8,2,48,1152]{3,2,1,0:T(8,128)(2,1)S(1)}, u32[]{:S(2)}, u32[]{:S(2)}) %collective-permute-start.16) | collective-permute-done | bytes 1769504 | tf_op jit(solution)/shard_map/ppermute | solution.py:319
  712.0 2.6 fusion.21
  716.2 2.3 collective-permute-start.22
  718.5 20.4 %collective-permute-done.20 = bf16[2,3,48,1152]{3,2,1,0:T(8,128)(2,1)S(1)} collective-permute-done((bf16[2,3,48,1152]{3,2,1,0:T(8,128)(2,1)S(1)}, bf16[2,3,48,1152]{3,2,1,0:T(8,128)(2,1)S(1)}, u32[]{:S(2)}, u32[]{:S(2)}) %collective-permute-start.20) | collective-permute-done | bytes 663584 | tf_op jit(solution)/shard_map/ppermute | solution.py:319
  738.9 16.3 %collective-permute-done.22 = bf16[2,3,48,1152]{3,2,1,0:T(8,128)(2,1)S(1)} collective-permute-done((bf16[2,3,48,1152]{3,2,1,0:T(8,128)(2,1)S(1)}, bf16[2,3,48,1152]{3,2,1,0:T(8,128)(2,1)S(1)}, u32[]{:S(2)}, u32[]{:S(2)}) %collective-permute-start.22) | collective-permute-done | bytes 663584 | tf_op jit(solution)/shard_map/ppermute | solution.py:319
  759.3 2.4 gather_fusion
  761.7 2.7 gather_fusion.1
  764.4 3.6 copy.181
  768.1 5.8 reshape.517
  774.2 2.4 slice_bitcast_fusion.2
  778.3 102.1 %reduce-scatter.6.cloned.1.call-done = bf16[48,2176]{1,0:T(8,128)(2,1)} async-done(((bf16[1536,2176]{1,0:T(8,128)(2,1)}), bf16[48,2176]{1,0:T(8,128)(2,1)}) %reduce-scatter.6.cloned.1.call-update) | async-done | bytes 208912 | tf_op jit(solution)/shard_map/reduce_scatter | solution.py:529
  (241 shorter events, 105.0 us)
Async XLA Ops:
  7.2 78.9 %all-gather.5.cloned.1.call-start = ((), (), s32[]{:S(2)}) async-start(), calls=%async_computation.3 | async-start | bytes 6893568 | tf_op jit(solution)/shard_map/all_gather | solution.py:401
  12.1 321.0 %all-gather.9.cloned.1.call-start = ((), (), s32[]{:S(2)}) async-start(), calls=%async_computation.8 | async-start | bytes 1310720 | tf_op jit(solution)/shard_map/all_gather | solution.py:421
  15.1 10.6 %copy-start.6 = (bf16[1,256,1536]{2,1,0:T(8,128)(2,1)S(1)}, bf16[1,256,1536]{2,1,0:T(8,128)(2,1)}, u32[]{:S(2)}) copy-start(bf16[1,256,1536]{2,1,0:T(8,128)(2,1)} %param.15) | copy-start | bytes 2359300
  103.5 246.5 %all-gather.7.cloned.1.call-start = ((), (), s32[]{:S(2)}) async-start(), calls=%async_computation.4 | async-start | bytes 4866048 | tf_op jit(solution)/shard_map/all_gather | solution.py:402
  107.5 3.8 collective-permute-start.4
  107.8 489.5 %reduce-scatter.4.cloned.1.call-start = ((), (), s32[]{:S(2)}) async-start(), calls=%async_computation.5 | async-start | bytes 1310720 | tf_op jit(solution)/shard_map/reduce_scatter | solution.py:504
  112.8 30.9 %collective-permute-start.5 = (bf16[2,3,48,1152]{3,2,1,0:T(8,128)(2,1)S(1)}, bf16[2,3,48,1152]{3,2,1,0:T(8,128)(2,1)S(1)}, u32[]{:S(2)}, u32[]{:S(2)}) collective-permute-start(bf16[2,3,48,1152]{3,2,1,0:T(8,128)(2,1)S(1)} %pad_maximum_fusion.9), channel_id=1, source_target_pairs={{0,1},{1,0},{2,3},{3,2},{4,5},{5,4},{6,7},{7,6},{8,9},{9,8},{10,11... | collective-permute-start | bytes 1990664 | tf_op jit(solution)/shard_map/ppermute | solution.py:319
  114.4 29.2 %collective-permute-start.6 = (bf16[2,3,48,1152]{3,2,1,0:T(8,128)(2,1)S(1)}, bf16[2,3,48,1152]{3,2,1,0:T(8,128)(2,1)S(1)}, u32[]{:S(2)}, u32[]{:S(2)}) collective-permute-start(bf16[2,3,48,1152]{3,2,1,0:T(8,128)(2,1)S(1)} %pad_maximum_fusion.10), channel_id=1, source_target_pairs={{0,16},{1,17},{2,18},{3,19},{4,20},{5,21},{6,22},{7,23},{8,24},{9,... | collective-permute-start | bytes 1990664 | tf_op jit(solution)/shard_map/ppermute | solution.py:319
  116.0 42.6 %collective-permute-start.7 = (bf16[2,3,48,1152]{3,2,1,0:T(8,128)(2,1)S(1)}, bf16[2,3,48,1152]{3,2,1,0:T(8,128)(2,1)S(1)}, u32[]{:S(2)}, u32[]{:S(2)}) collective-permute-start(bf16[2,3,48,1152]{3,2,1,0:T(8,128)(2,1)S(1)} %pad_maximum_fusion.11), channel_id=1, source_target_pairs={{0,17},{1,16},{2,19},{3,18},{4,21},{5,20},{6,23},{7,22},{8,25},{9,... | collective-permute-start | bytes 1990664 | tf_op jit(solution)/shard_map/ppermute | solution.py:319
  159.2 89.3 %copy-start.7 = (bf16[1,256,1536]{2,1,0:T(8,128)(2,1)S(1)}, bf16[1,256,1536]{2,1,0:T(8,128)(2,1)}, u32[]{:S(2)}) copy-start(bf16[1,256,1536]{2,1,0:T(8,128)(2,1)} %param.16) | copy-start | bytes 2359300
  159.2 132.0 %copy-start.32 = (s32[8]{0:T(128)S(1)}, s32[8]{0:T(128)}, u32[]{:S(2)}) copy-start(s32[8]{0:T(128)} %copy-done.31) | copy-start | bytes 100
  159.3 132.1 %copy-start.30 = (s32[1,256]{1,0:T(1,128)S(1)}, s32[1,256]{1,0:T(1,128)}, u32[]{:S(2)}) copy-start(s32[1,256]{1,0:T(1,128)} %copy-done.29) | copy-start | bytes 3076
  159.4 87.6 %collective-permute-start.10 = (bf16[8,2,48,1152]{3,2,0,1:T(8,128)(2,1)S(1)}, bf16[8,2,48,1152]{3,2,0,1:T(8,128)(2,1)S(1)}, u32[]{:S(2)}, u32[]{:S(2)}) collective-permute-start(bf16[8,2,48,1152]{3,2,0,1:T(8,128)(2,1)S(1)} %slice.260), channel_id=1, source_target_pairs={{0,2},{1,3},{2,0},{3,1},{4,6},{5,7},{6,4},{7,5},{8,10},{9,11},{10,... | collective-permute-start | bytes 5308424 | tf_op jit(solution)/shard_map/ppermute | solution.py:319
  161.9 161.8 %collective-permute-start.8 = (bf16[8,2,48,1152]{3,2,0,1:T(8,128)(2,1)S(1)}, bf16[8,2,48,1152]{3,2,0,1:T(8,128)(2,1)S(1)}, u32[]{:S(2)}, u32[]{:S(2)}) collective-permute-start(bf16[8,2,48,1152]{3,2,0,1:T(8,128)(2,1)S(1)} %slice.260), channel_id=1, source_target_pairs={{0,8},{1,9},{2,10},{3,11},{4,12},{5,13},{6,14},{7,15},{8,0},{9,1},... | collective-permute-start | bytes 5308424 | tf_op jit(solution)/shard_map/ppermute | solution.py:319
  247.1 77.9 %collective-permute-start.12 = (bf16[8,2,48,1152]{3,2,0,1:T(8,128)(2,1)S(1)}, bf16[8,2,48,1152]{3,2,0,1:T(8,128)(2,1)S(1)}, u32[]{:S(2)}, u32[]{:S(2)}) collective-permute-start(bf16[8,2,48,1152]{3,2,0,1:T(8,128)(2,1)S(1)} %collective-permute-done.10), channel_id=1, source_target_pairs={{0,8},{1,9},{2,10},{3,11},{4,12},{5,13},{6,14},{7,15},{8,0},{9,1},... | collective-permute-start | bytes 5308424 | tf_op jit(solution)/shard_map/ppermute | solution.py:319
  248.5 33.1 %collective-permute-start = (bf16[256,1536]{1,0:T(8,128)(2,1)S(1)}, bf16[256,1536]{1,0:T(8,128)(2,1)S(1)}, u32[]{:S(2)}, u32[]{:S(2)}) collective-permute-start(bf16[256,1536]{1,0:T(8,128)(2,1)S(1)} %bitcast.242), channel_id=1, source_target_pairs={{0,1},{1,0},{2,3},{3,2},{4,5},{5,4},{6,7},{7,6},{8,9},{9,8},{10,11... | collective-permute-start | bytes 2359304 | tf_op jit(solution)/shard_map/ppermute | solution.py:319
  248.5 43.0 %collective-permute-start.1 = (bf16[256,1536]{1,0:T(8,128)(2,1)S(1)}, bf16[256,1536]{1,0:T(8,128)(2,1)S(1)}, u32[]{:S(2)}, u32[]{:S(2)}) collective-permute-start(bf16[256,1536]{1,0:T(8,128)(2,1)S(1)} %bitcast.243), channel_id=1, source_target_pairs={{0,16},{1,17},{2,18},{3,19},{4,20},{5,21},{6,22},{7,23},{8,24},{9,... | collective-permute-start | bytes 2359304 | tf_op jit(solution)/shard_map/ppermute | solution.py:319
  249.2 61.7 %collective-permute-start.2 = (bf16[256,1536]{1,0:T(8,128)(2,1)S(1)}, bf16[256,1536]{1,0:T(8,128)(2,1)S(1)}, u32[]{:S(2)}, u32[]{:S(2)}) collective-permute-start(bf16[256,1536]{1,0:T(8,128)(2,1)S(1)} %bitcast.244), channel_id=1, source_target_pairs={{0,17},{1,16},{2,19},{3,18},{4,21},{5,20},{6,23},{7,22},{8,25},{9,... | collective-permute-start | bytes 2359304 | tf_op jit(solution)/shard_map/ppermute | solution.py:319
  281.6 31.3 %copy-start.15 = (bf16[256,1536]{1,0:T(8,128)(2,1)}, bf16[256,1536]{1,0:T(8,128)(2,1)S(1)}, u32[]{:S(2)}) copy-start(bf16[256,1536]{1,0:T(8,128)(2,1)S(1)} %collective-permute-done.go_p) | copy-start | bytes 2359300
  281.6 40.0 %collective-permute-start.11 = (bf16[8,48,1152]{2,1,0:T(8,128)(2,1)}, bf16[8,48,1152]{2,1,0:T(8,128)(2,1)}, u32[]{:S(2)}, u32[]{:S(2)}) collective-permute-start(bf16[8,48,1152]{2,1,0:T(8,128)(2,1)} %slice_bitcast_fusion.9.sd), channel_id=1, source_target_pairs={{0,2},{1,3},{2,0},{3,1},{4,6},{5,7},{6,4},{7,5},{8,10},{9,11},{10,... | collective-permute-start | bytes 2654216 | tf_op jit(solution)/shard_map/ppermute | solution.py:319
  291.6 21.3 %copy-start.16 = (bf16[256,1536]{1,0:T(8,128)(2,1)}, bf16[256,1536]{1,0:T(8,128)(2,1)S(1)}, u32[]{:S(2)}) copy-start(bf16[256,1536]{1,0:T(8,128)(2,1)S(1)} %collective-permute-done.1.go_y) | copy-start | bytes 2359300
  312.9 43.5 %collective-permute-start.3 = (bf16[4,256,1536]{2,1,0:T(8,128)(2,1)}, bf16[4,256,1536]{2,1,0:T(8,128)(2,1)}, u32[]{:S(2)}, u32[]{:S(2)}) collective-permute-start(bf16[4,256,1536]{2,1,0:T(8,128)(2,1)} %pad_maximum_fusion), channel_id=1, source_target_pairs={{0,4},{1,5},{2,6},{3,7},{4,0},{5,1},{6,2},{7,3},{8,12},{9,13},{10,... | collective-permute-start | bytes 9437192 | tf_op jit(solution)/shard_map/ppermute | solution.py:319
  314.3 42.1 %collective-permute-start.9 = (bf16[8,48,1152]{2,1,0:T(8,128)(2,1)}, bf16[8,48,1152]{2,1,0:T(8,128)(2,1)}, u32[]{:S(2)}, u32[]{:S(2)}) collective-permute-start(bf16[8,48,1152]{2,1,0:T(8,128)(2,1)} %slice_bitcast_fusion.9.sd), channel_id=1, source_target_pairs={{0,8},{1,9},{2,10},{3,11},{4,12},{5,13},{6,14},{7,15},{8,0},{9,1},... | collective-permute-start | bytes 2654216 | tf_op jit(solution)/shard_map/ppermute | solution.py:319
  321.6 34.8 %collective-permute-start.13 = (bf16[8,48,1152]{2,1,0:T(8,128)(2,1)}, bf16[8,48,1152]{2,1,0:T(8,128)(2,1)}, u32[]{:S(2)}, u32[]{:S(2)}) collective-permute-start(bf16[8,48,1152]{2,1,0:T(8,128)(2,1)} %collective-permute-done.11.zd), channel_id=1, source_target_pairs={{0,8},{1,9},{2,10},{3,11},{4,12},{5,13},{6,14},{7,15},{8,0},{9,1},... | collective-permute-start | bytes 2654216 | tf_op jit(solution)/shard_map/ppermute | solution.py:319
  332.7 7.2 copy-start.9
  333.1 9.7 %copy-start.11 = (bf16[256,12,64]{2,0,1:T(8,128)(2,1)}, bf16[256,12,64]{2,0,1:T(8,128)(2,1)S(1)}, u32[]{:S(2)}) copy-start(bf16[256,12,64]{2,0,1:T(8,128)(2,1)S(1)} %copy.149) | copy-start | bytes 1179652
  488.6 31.7 %copy-start.2 = (f32[256,1536]{1,0:T(8,128)}, f32[256,1536]{1,0:T(8,128)S(1)}, u32[]{:S(2)}) copy-start(f32[256,1536]{1,0:T(8,128)S(1)} %get-tuple-element.38) | copy-start | bytes 4718596
  492.6 17.4 %slice-start = ((s8[12582912]{0:T(1024)(128)(4,1)}), s8[4194304]{0:T(1024)(128)(4,1)S(1)}, s32[]{:S(2)}) async-start(s8[12582912]{0:T(1024)(128)(4,1)} %bitcast.233), calls=%async_computation.9 | async-start | bytes 8388608
  492.6 17.4 %slice-start.1 = ((s8[12582912]{0:T(1024)(128)(4,1)}), s8[4194304]{0:T(1024)(128)(4,1)S(1)}, s32[]{:S(2)}) async-start(s8[12582912]{0:T(1024)(128)(4,1)} %bitcast.233), calls=%async_computation.10 | async-start | bytes 8388608
  503.0 7.0 slice-start.2
  520.3 256.3 %reduce-scatter.8.cloned.1.call-start = ((), (), s32[]{:S(2)}) async-start(), calls=%async_computation.7 | async-start | bytes 4866048 | tf_op jit(solution)/shard_map/reduce_scatter | solution.py:530
  524.4 11.5 %slice-start.3 = ((s8[6291456]{0:T(1024)(128)(4,1)}), s8[2097152]{0:T(1024)(128)(4,1)S(1)}, s32[]{:S(2)}) async-start(s8[6291456]{0:T(1024)(128)(4,1)} %bitcast.235), calls=%async_computation.12 | async-start | bytes 4194304
  524.4 356.0 %reduce-scatter.6.cloned.1.call-start = ((), (), s32[]{:S(2)}) async-start(), calls=%async_computation.6 | async-start | bytes 6893568 | tf_op jit(solution)/shard_map/reduce_scatter | solution.py:529
  524.5 11.4 %slice-start.4 = ((s8[6291456]{0:T(1024)(128)(4,1)}), s8[4194304]{0:T(1024)(128)(4,1)S(1)}, s32[]{:S(2)}) async-start(s8[6291456]{0:T(1024)(128)(4,1)} %bitcast.235), calls=%async_computation.13 | async-start | bytes 8388608
  528.3 7.6 copy-start.14
  528.3 64.3 %collective-permute-start.15 = (bf16[8,2,48,1152]{3,2,1,0:T(8,128)(2,1)S(1)}, bf16[8,2,48,1152]{3,2,1,0:T(8,128)(2,1)S(1)}, u32[]{:S(2)}, u32[]{:S(2)}) collective-permute-start(bf16[8,2,48,1152]{3,2,1,0:T(8,128)(2,1)S(1)} %get-tuple-element.34), channel_id=1, source_target_pairs={{0,8},{1,9},{2,10},{3,11},{4,12},{5,13},{6,14},{7,15},{8,0},{9,1},... | collective-permute-start | bytes 5308424 | tf_op jit(solution)/shard_map/ppermute | solution.py:319
  530.9 58.0 %collective-permute-start.18 = (bf16[8,48,1152]{2,1,0:T(8,128)(2,1)S(1)}, bf16[8,48,1152]{2,1,0:T(8,128)(2,1)S(1)}, u32[]{:S(2)}, u32[]{:S(2)}) collective-permute-start(bf16[8,48,1152]{2,1,0:T(8,128)(2,1)S(1)} %get-tuple-element.41), channel_id=1, source_target_pairs={{0,8},{1,9},{2,10},{3,11},{4,12},{5,13},{6,14},{7,15},{8,0},{9,1},... | collective-permute-start | bytes 2654216 | tf_op jit(solution)/shard_map/ppermute | solution.py:319
  532.8 101.8 %collective-permute-start.17 = (bf16[8,48,1152]{2,1,0:T(8,128)(2,1)}, bf16[8,48,1152]{2,1,0:T(8,128)(2,1)}, u32[]{:S(2)}, u32[]{:S(2)}) collective-permute-start(bf16[8,48,1152]{2,1,0:T(8,128)(2,1)} %get-tuple-element.40), channel_id=1, source_target_pairs={{0,8},{1,9},{2,10},{3,11},{4,12},{5,13},{6,14},{7,15},{8,0},{9,1},... | collective-permute-start | bytes 2654216 | tf_op jit(solution)/shard_map/ppermute | solution.py:319
  532.9 143.4 %collective-permute-start.14 = (bf16[8,2,48,1152]{3,2,1,0:T(8,128)(2,1)}, bf16[8,2,48,1152]{3,2,1,0:T(8,128)(2,1)}, u32[]{:S(2)}, u32[]{:S(2)}) collective-permute-start(bf16[8,2,48,1152]{3,2,1,0:T(8,128)(2,1)} %get-tuple-element.33), channel_id=1, source_target_pairs={{0,8},{1,9},{2,10},{3,11},{4,12},{5,13},{6,14},{7,15},{8,0},{9,1},... | collective-permute-start | bytes 5308424 | tf_op jit(solution)/shard_map/ppermute | solution.py:319
  591.2 83.1 %collective-permute-start.19 = (bf16[8,48,1152]{2,1,0:T(8,128)(2,1)}, bf16[8,48,1152]{2,1,0:T(8,128)(2,1)}, u32[]{:S(2)}, u32[]{:S(2)}) collective-permute-start(bf16[8,48,1152]{2,1,0:T(8,128)(2,1)} %fusion.31), channel_id=1, source_target_pairs={{0,2},{1,3},{2,0},{3,1},{4,6},{5,7},{6,4},{7,5},{8,10},{9,11},{10,... | collective-permute-start | bytes 2654216 | tf_op jit(solution)/shard_map/ppermute | solution.py:319
  595.9 15.2 %copy-start.28 = (f32[256]{0:T(256)S(1)}, f32[256]{0:T(256)}, u32[]{:S(2)}) copy-start(f32[256]{0:T(256)} %add_rsqrt_fusion.1) | copy-start | bytes 3076
  595.9 116.1 %collective-permute-start.16 = (bf16[8,2,48,1152]{3,2,1,0:T(8,128)(2,1)}, bf16[8,2,48,1152]{3,2,1,0:T(8,128)(2,1)S(1)}, u32[]{:S(2)}, u32[]{:S(2)}) collective-permute-start(bf16[8,2,48,1152]{3,2,1,0:T(8,128)(2,1)} %fusion.19), channel_id=1, source_target_pairs={{0,2},{1,3},{2,0},{3,1},{4,6},{5,7},{6,4},{7,5},{8,10},{9,11},{10,... | collective-permute-start | bytes 5308424 | tf_op jit(solution)/shard_map/ppermute | solution.py:319
  611.1 7.2 copy-start.22
  611.1 7.2 copy-start.23
  714.9 24.0 %collective-permute-start.20 = (bf16[2,3,48,1152]{3,2,1,0:T(8,128)(2,1)S(1)}, bf16[2,3,48,1152]{3,2,1,0:T(8,128)(2,1)S(1)}, u32[]{:S(2)}, u32[]{:S(2)}) collective-permute-start(bf16[2,3,48,1152]{3,2,1,0:T(8,128)(2,1)S(1)} %get-tuple-element.45), channel_id=1, source_target_pairs={{0,1},{1,0},{2,3},{3,2},{4,5},{5,4},{6,7},{7,6},{8,9},{9,8},{10,11... | collective-permute-start | bytes 1990664 | tf_op jit(solution)/shard_map/ppermute | solution.py:319
  715.0 23.9 %collective-permute-start.21 = (bf16[2,3,48,1152]{3,2,1,0:T(8,128)(2,1)S(1)}, bf16[2,3,48,1152]{3,2,1,0:T(8,128)(2,1)S(1)}, u32[]{:S(2)}, u32[]{:S(2)}) collective-permute-start(bf16[2,3,48,1152]{3,2,1,0:T(8,128)(2,1)S(1)} %get-tuple-element.47), channel_id=1, source_target_pairs={{0,16},{1,17},{2,18},{3,19},{4,20},{5,21},{6,22},{7,23},{8,24},{9,... | collective-permute-start | bytes 1990664 | tf_op jit(solution)/shard_map/ppermute | solution.py:319
  716.2 39.0 %collective-permute-start.22 = (bf16[2,3,48,1152]{3,2,1,0:T(8,128)(2,1)S(1)}, bf16[2,3,48,1152]{3,2,1,0:T(8,128)(2,1)S(1)}, u32[]{:S(2)}, u32[]{:S(2)}) collective-permute-start(bf16[2,3,48,1152]{3,2,1,0:T(8,128)(2,1)S(1)} %get-tuple-element.46), channel_id=1, source_target_pairs={{0,17},{1,16},{2,19},{3,18},{4,21},{5,20},{6,23},{7,22},{8,25},{9,... | collective-permute-start | bytes 1990664 | tf_op jit(solution)/shard_map/ppermute | solution.py:319
  755.8 3.3 collective-permute-start.23
  (23 other events, 66.7 us)
Sparse Core Ops, SparseCore 0:
  12.2 73.7 all-gather.4
  103.6 35.7 all-gather.8
  142.2 139.0 all-gather.6
  520.4 26.1 reduce-scatter.3
  552.8 205.4 reduce-scatter.7
  763.9 116.4 reduce-scatter.5

commit v2 on v1

--- a/solution.py
+++ b/solution.py
@@ -95,7 +95,7 @@
 
 
 def ffn_kernel(
-    ctx_size, n_own, go_own, go_p, go_y, go_py, go_core, sgu, sd, xgu, xd, zgu, zd, xzgu, xzd,
+    ctx_size, n_own, go_all, big,
     hr, dgu, dd,
     wgu, wd, nt, go, ggu, act, csend, crecv, hpart, stage,
     w_sem, io_sem, n_send, n_recv, f_send, f_recv, c_send, c_recv, o_send, o_recv, st_sem,
@@ -106,7 +106,7 @@
     y, x, c = dp // 4, (dp // 2) % 2, dp % 2
     h, p = ctx // 2, ctx % 2
     width = wd.shape[1]
-    shard = sgu.shape[2]
+    shard = dgu.shape[4]
     rows, model = n_own.shape
 
     def at(index):
@@ -123,19 +123,12 @@
 
     load_n = pltpu.make_async_copy(n_own, nt.at[0], io_sem.at[0])
     load_n.start()
-    go_loads = []
-    for o, ref in enumerate((go_own, go_p, go_y, go_py)):
-        go_loads.append(pltpu.make_async_copy(ref, go.at[2 * o], io_sem.at[1 + o]))
-        go_loads.append(pltpu.make_async_copy(go_core.at[o], go.at[2 * o + 1], io_sem.at[5 + o]))
-    for copy in go_loads:
-        copy.start()
-    for mask, (gu_ref, d_ref) in ((0, (sgu, sd)), (8, (xgu, xd)), (2, (zgu, zd)), (10, (xzgu, xzd))):
-        for j in range(8):
-            rel = mask + (j // 4) * 16 + ((j // 2) % 2) * 4 + j % 2
-            row = pl.ds(pl.multiple_of(flip(me, rel) * shard, shard), shard)
-            pltpu.make_async_copy(gu_ref.at[j, 0], wgu.at[row, pl.ds(0, width)], w_sem.at[0]).start()
-            pltpu.make_async_copy(gu_ref.at[j, 1], wgu.at[row, pl.ds(width, width)], w_sem.at[0]).start()
-            pltpu.make_async_copy(d_ref.at[j], wd.at[row], w_sem.at[1]).start()
+    load_go = pltpu.make_async_copy(go_all, go, io_sem.at[1])
+    load_go.start()
+    load_gu = pltpu.make_async_copy(big.at[:, pl.ds(0, 2 * width)], wgu, w_sem.at[0])
+    load_gu.start()
+    load_d = pltpu.make_async_copy(big.at[:, pl.ds(2 * width, width)], wd, w_sem.at[1])
+    load_d.start()
 
     pl.semaphore_wait(barrier, 4)
     load_n.wait()
@@ -150,10 +143,9 @@
     for copy in first:
         copy.start()
     push_n(0, 1, core, f_send.at[0], f_recv.at[0]).start()
-    pltpu.make_async_copy(wgu, wgu, w_sem.at[0]).wait()
-    pltpu.make_async_copy(wd, wd, w_sem.at[1]).wait()
-    for copy in go_loads:
-        copy.wait()
+    load_gu.wait()
+    load_d.wait()
+    load_go.wait()
 
     def tile(slot):
         gu = dot(nt[slot], wgu[...], ((1,), (0,)))
@@ -272,9 +264,9 @@
         final(o).wait()
 
 
-def ffn_call(ctx_size, n_own, go_tiles, weights):
+def ffn_call(ctx_size, shard, n_own, go_all, big):
     rows, model = n_own.shape
-    shard, width = weights[0].shape[2:]
+    width = big.shape[1] // 3
     low = jnp.bfloat16
     return pl.pallas_call(
         functools.partial(ffn_kernel, ctx_size),
@@ -283,7 +275,7 @@
             jax.ShapeDtypeStruct((2, 2, 8, 2, shard, width), low),
             jax.ShapeDtypeStruct((2, 2, 8, shard, width), low),
         ),
-        in_specs=[pl.BlockSpec(memory_space=pl.ANY)] * 14,
+        in_specs=[pl.BlockSpec(memory_space=pl.ANY)] * 3,
         out_specs=[pl.BlockSpec(memory_space=pl.ANY)] * 3,
         scratch_shapes=[
             pltpu.VMEM((model, 2 * width), low),
@@ -297,7 +289,7 @@
             pltpu.VMEM((4, 2, rows, model), low),
             pltpu.VMEM((2, 8 * shard, 3 * width), low),
             pltpu.SemaphoreType.DMA((2,)),
-            pltpu.SemaphoreType.DMA((9,)),
+            pltpu.SemaphoreType.DMA((2,)),
             pltpu.SemaphoreType.DMA((4,)),
             pltpu.SemaphoreType.DMA((4,)),
             pltpu.SemaphoreType.DMA((4,)),
@@ -312,7 +304,308 @@
             collective_id=1, has_side_effects=True, vmem_limit_bytes=63 << 20
         ),
         name="ffn",
-    )(n_own, *go_tiles, *weights)
+    )(n_own, go_all, big)
+
+
+def turn(values, cosine, sine):
+    return values * cosine + pltpu.roll(values, HD // 2, 1) * sine
+
+
+def front_kernel(
+    ctx_size, hidden, cosine, sine, pos_q, pos_k, spread, packed, w_out, w_gate, w_up, w_down, grad_out,
+    normed_o, query_o, kv_o, total_o, mixed_o, resid_o, normed_two_o, small_o, proj_o, out_o, big, go,
+    proj, out_w, source, query, kv, mixed, total,
+    load_sem, ag_send, ag_recv, core_send, core_recv, big_send, big_recv, go_send, go_recv, kv_send, kv_recv, back_sem,
+):
+    dp = lax.axis_index("dp")
+    ctx = lax.axis_index("ctx")
+    me = dp * ctx_size + ctx
+    shard, wide = packed.shape
+    rows, model = hidden.shape
+    width = big.shape[1] // 3
+    kv_width = KV_HEADS * HD
+    q_width = HEADS * HD
+    proj_width = q_width + 2 * kv_width
+    groups = HEADS // KV_HEADS
+
+    def at(index):
+        return (index // ctx_size, index % ctx_size)
+
+    def block(mask, count=1):
+        base = flip(me, mask) // count * count
+        return pl.ds(pl.multiple_of(base * shard, shard), shard * count)
+
+    def remote(src, dst, send, recv, mask):
+        return pltpu.make_async_remote_copy(
+            src_ref=src, dst_ref=dst, send_sem=send, recv_sem=recv, device_id=at(flip(me, mask)), device_id_type=MESH
+        )
+
+    def drain(ref, sem):
+        pltpu.make_async_copy(ref, ref, sem).wait()
+
+    barrier = pltpu.get_barrier_semaphore()
+    partners = (1, 2, 4, 5, 8, 16, 17, 20, 21)
+    for mask in partners:
+        pl.semaphore_signal(barrier, inc=1, device_id=at(flip(me, mask)), device_id_type=MESH)
+
+    own = (
+        pltpu.make_async_copy(packed, proj.at[block(0)], load_sem.at[0]),
+        pltpu.make_async_copy(w_out, out_w.at[block(0)], load_sem.at[1]),
+    )
+    for copy in own:
+        copy.start()
+    hidden_units = w_gate.shape[1]
+    cuts = []
+    for k in range(8):
+        size = min(width, hidden_units - k * width)
+        for n, ref in enumerate((w_gate, w_up, w_down)):
+            cuts.append((ref.at[:, pl.ds(k * width, size)], source.at[k, :, pl.ds(n * width, size)]))
+            if size < width:
+                source[k, :, pl.ds(n * width + size, width - size)] = jnp.zeros((shard, width - size), source.dtype)
+    cuts = [pltpu.make_async_copy(a, b, load_sem.at[2 + i]) for i, (a, b) in enumerate(cuts)]
+    for copy in cuts:
+        copy.start()
+    pl.semaphore_wait(barrier, len(partners))
+    for copy in own:
+        copy.wait()
+
+    pair = ((proj, 0), (out_w, 1))
+
+    def ag(mask, over):
+        for ref, n in pair:
+            remote(ref.at[block(mask)], ref.at[block(mask)], ag_send.at[n], ag_recv.at[n, mask | over], over).start()
+
+    def ag_wait(mask):
+        for ref, n in pair:
+            remote(ref.at[block(mask)], ref.at[block(mask)], ag_send.at[n], ag_recv.at[n, mask], 1).wait_recv()
+
+    def group(mask):
+        return [
+            remote(ref.at[block(mask, 4)], ref.at[block(mask, 4)], core_send.at[n, mask // 8], core_recv.at[n, mask // 8], 4)
+            for ref, n in pair
+        ]
+
+    def group_wait(mask, n):
+        ref = pair[n][0]
+        remote(ref.at[block(mask | 4, 4)], ref.at[block(mask | 4, 4)], core_send.at[n, mask // 8], core_recv.at[n, mask // 8], 4).wait_recv()
+
+    for over in (2, 1, 8, 16):
+        ag(0, over)
+
+    for copy in cuts:
+        copy.wait()
+    y, x, c = dp // 4, (dp // 2) % 2, dp % 2
+    h, p = ctx // 2, ctx % 2
+
+    def column(mask):
+        return either(y, mask // 16) * 4 + either(p, mask % 2) * 2 + either(c, (mask // 4) % 2)
+
+    own_big = pltpu.make_async_copy(source.at[column(0)], big.at[block(0)], load_sem.at[0])
+    own_big.start()
+    for mask in (4, 1, 16, 5, 20, 17, 21):
+        remote(source.at[column(mask)], big.at[block(0)], big_send.at[0], big_recv.at[mask], mask).start()
+    first_z = remote(source.at[column(0)], big.at[block(0)], big_send.at[0], big_recv.at[2], 2)
+    first_z.start()
+
+    def big_forward(mask, over):
+        remote(big.at[block(mask)], big.at[block(mask)], big_send.at[0], big_recv.at[mask | over], over).start()
+
+    def big_wait(mask):
+        remote(big.at[block(mask)], big.at[block(mask)], big_send.at[0], big_recv.at[mask], 1).wait_recv()
+
+    ag_wait(1)
+    for over in (8, 16):
+        ag(1, over)
+    ag_wait(8)
+    ag(8, 16)
+    ag_wait(2)
+    for over in (1, 8, 16):
+        ag(2, over)
+    ag_wait(9)
+    ag(9, 16)
+    big_wait(4)
+    big_forward(4, 2)
+    big_wait(1)
+    big_forward(1, 2)
+    ag_wait(3)
+    for over in (8, 16):
+        ag(3, over)
+    for copy in group(0):
+        copy.start()
+    ag_wait(10)
+    ag(10, 16)
+    ag_wait(11)
+    ag(11, 16)
+    for copy in group(8):
+        copy.start()
+    remote(source.at[column(0)], big.at[block(0)], big_send.at[0], big_recv.at[8], 8).start()
+    for mask in (16, 5, 20, 17, 21):
+        big_wait(mask)
+        big_forward(mask, 2)
+    for mask in (4, 1, 16, 5):
+        big_forward(mask, 8)
+    for mask in (16, 17, 18, 19):
+        ag_wait(mask)
+    for copy in group(16):
+        copy.start()
+    for mask in (24, 25, 26, 27):
+        ag_wait(mask)
+    for copy in group(24):
+        copy.start()
+    for mask in (20, 17, 21):
+        big_forward(mask, 8)
+    own_go = pltpu.make_async_copy(grad_out, go.at[0], load_sem.at[1])
+    own_go.start()
+    for o, mask in ((1, 1), (2, 16), (3, 17)):
+        remote(grad_out, go.at[2 * o], go_send.at[o], go_recv.at[2 * o], mask).start()
+    remote(grad_out, go.at[1], go_send.at[0], go_recv.at[1], 4).start()
+    for mask in (0, 8, 16, 24):
+        group_wait(mask, 0)
+
+    small = jnp.transpose(proj[:, proj_width:].astype(jnp.float32))
+    small_o[...] = small[:8]
+    kv_bias = dot(small[:8].astype(jnp.bfloat16), spread[...], ((1,), (0,)))[3:4]
+    values = hidden[...].astype(jnp.float32)
+    factor = lax.rsqrt(jnp.mean(values * values, axis=-1, keepdims=True) + norm_eps)
+    normed_o[...] = (values * factor * small[0:1]).astype(jnp.bfloat16)
+    cos, sin = cosine[...], sine[...]
+    raw = dot(normed_o[...], proj[:, q_width:proj_width], ((1,), (0,))) + kv_bias
+    mine = block(0)
+    for g in range(KV_HEADS):
+        kv[ctx, :, pl.ds(g * HD, HD)] = turn(raw[:, g * HD : (g + 1) * HD], cos, sin).astype(jnp.bfloat16)
+    kv[ctx, :, pl.ds(kv_width, kv_width)] = raw[:, kv_width:].astype(jnp.bfloat16)
+
+    def kv_push(mask, over):
+        slot = flip(ctx, mask)
+        return remote(kv.at[slot], kv.at[slot], kv_send.at[mask | over], kv_recv.at[mask | over], over)
+
+    kv_push(0, 2).start()
+    kv_push(0, 1).start()
+    for half in range(2):
+        part = half * (q_width // 2)
+        raw = dot(normed_o[...], proj[:, part : part + q_width // 2], ((1,), (0,)))
+        raw = raw + small[1:2, part : part + q_width // 2]
+        for i in range(HEADS // 2):
+            query[half * (HEADS // 2) + i] = turn(raw[:, i * HD : (i + 1) * HD], cos, sin).astype(jnp.bfloat16)
+    big_wait(2)
+    big_forward(2, 8)
+    kv_push(0, 2).wait_recv()
+    kv_push(2, 1).start()
+    for mask in (6, 3):
+        big_wait(mask)
+        big_forward(mask, 8)
+    kv_push(0, 1).wait_recv()
+    kv_push(2, 1).wait_recv()
+    query_back = pltpu.make_async_copy(query, query_o, back_sem.at[0])
+    query_back.start()
+    kv_back = pltpu.make_async_copy(kv, kv_o, back_sem.at[1])
+    kv_back.start()
+
+    def head(n, carry):
+        g = n // groups
+        keys = kv[:, :, pl.ds(pl.multiple_of(g * HD, HD), HD)].reshape(ctx_size * rows, HD)
+        vals = kv[:, :, pl.ds(pl.multiple_of(kv_width + g * HD, HD), HD)].reshape(ctx_size * rows, HD)
+        scores = dot(query[n], keys, ((1,), (1,))) * HD ** (-0.5)
+        scores = jnp.where(pos_k[...] <= pos_q[...], scores, masked_fill)
+        top = jnp.max(scores, axis=-1, keepdims=True)
+        expo = jnp.exp(scores - top)
+        expo_sum = jnp.sum(expo, axis=-1, keepdims=True)
+        attend = (expo / expo_sum).astype(jnp.bfloat16)
+        mixed[:, pl.ds(pl.multiple_of(n * HD, HD), HD)] = dot(attend, vals, ((1,), (0,))).astype(jnp.bfloat16)
+        total[n] = jnp.broadcast_to(top + jnp.log(expo_sum), (rows, HD))
+        return carry
+
+    lax.fori_loop(0, HEADS // 2, head, 0)
+    for o, mask in ((1, 1), (2, 16), (3, 17)):
+        remote(grad_out, go.at[2 * o], go_send.at[o], go_recv.at[2 * o], mask).wait_recv()
+        remote(go.at[2 * o], go.at[2 * o + 1], go_send.at[3 + o], go_recv.at[2 * o + 1], 4).start()
+    big_wait(18)
+    big_forward(18, 8)
+    lax.fori_loop(HEADS // 2, HEADS, head, 0)
+    mixed_back = pltpu.make_async_copy(mixed, mixed_o, back_sem.at[2])
+    mixed_back.start()
+    total_back = pltpu.make_async_copy(total, total_o, back_sem.at[3])
+    total_back.start()
+    for mask in (0, 8, 16, 24):
+        group_wait(mask, 1)
+    proj_back = pltpu.make_async_copy(proj, proj_o, back_sem.at[4])
+    proj_back.start()
+    out_back = pltpu.make_async_copy(out_w, out_o, back_sem.at[5])
+    out_back.start()
+    resid = hidden[...].astype(jnp.float32) + dot(mixed[...], out_w[...], ((1,), (1,)))
+    resid_o[...] = resid
+    factor = lax.rsqrt(jnp.mean(resid * resid, axis=-1, keepdims=True) + norm_eps)
+    normed_two_o[...] = (resid * factor * small_o[2:3]).astype(jnp.bfloat16)
+    for mask in (7, 22, 19, 23):
+        big_wait(mask)
+        big_forward(mask, 8)
+
+    for mask in (8, 12, 9, 24, 13, 28, 25, 29, 10, 14, 11, 26, 15, 30, 27, 31):
+        big_wait(mask)
+    own_big.wait()
+    own_go.wait()
+    sent = 7 + 8 + 8 + 8
+    drain(big.at[pl.ds(0, sent * shard)], big_send.at[0])
+    for ref, n in pair:
+        drain(ref.at[pl.ds(0, 15 * shard)], ag_send.at[n])
+        for mask in (0, 8, 16, 24):
+            group(mask)[n].wait_send()
+    remote(grad_out, go.at[1], go_send.at[0], go_recv.at[1], 4).wait()
+    for o, mask in ((1, 1), (2, 16), (3, 17)):
+        remote(grad_out, go.at[2 * o], go_send.at[o], go_recv.at[2 * o], mask).wait_send()
+        remote(go.at[2 * o], go.at[2 * o + 1], go_send.at[3 + o], go_recv.at[2 * o + 1], 4).wait()
+    kv_push(0, 2).wait_send()
+    kv_push(0, 1).wait_send()
+    kv_push(2, 1).wait_send()
+    for copy in (query_back, kv_back, mixed_back, total_back, proj_back, out_back):
+        copy.wait()
+
+
+def front_call(ctx_size, hidden, cosine, sine, pos_q, pos_k, spread, packed, w_out, w_gate, w_up, w_down, grad_out):
+    rows, model = hidden.shape
+    shard, wide = packed.shape
+    kv_width = KV_HEADS * HD
+    q_width = HEADS * HD
+    width = -(-w_gate.shape[1] // (8 * 128)) * 128
+    low, full = jnp.bfloat16, jnp.float32
+    vmem = pl.BlockSpec(memory_space=pltpu.VMEM)
+    anywhere = pl.BlockSpec(memory_space=pl.ANY)
+    shapes = (
+        ((rows, model), low, vmem),
+        ((HEADS, rows, HD), low, anywhere),
+        ((ctx_size, rows, 2 * kv_width), low, anywhere),
+        ((HEADS, rows, HD), full, anywhere),
+        ((rows, q_width), low, anywhere),
+        ((rows, model), full, vmem),
+        ((rows, model), low, vmem),
+        ((8, model), full, vmem),
+        ((model, wide), low, anywhere),
+        ((model, q_width), low, anywhere),
+        ((model, 3 * width), low, anywhere),
+        ((8, rows, model), low, anywhere),
+    )
+    sem = pltpu.SemaphoreType.DMA
+    return pl.pallas_call(
+        functools.partial(front_kernel, ctx_size),
+        out_shape=tuple(jax.ShapeDtypeStruct(shape, kind) for shape, kind, _ in shapes),
+        in_specs=[vmem] * 6 + [anywhere] * 6,
+        out_specs=tuple(spec for _, _, spec in shapes),
+        scratch_shapes=[
+            pltpu.VMEM((model, wide), low),
+            pltpu.VMEM((model, q_width), low),
+            pltpu.VMEM((8, shard, 3 * width), low),
+            pltpu.VMEM((HEADS, rows, HD), low),
+            pltpu.VMEM((ctx_size, rows, 2 * kv_width), low),
+            pltpu.VMEM((rows, q_width), low),
+            pltpu.VMEM((HEADS, rows, HD), full),
+            sem((26,)), sem((2,)), sem((2, 32)), sem((2, 4)), sem((2, 4)), sem((1,)), sem((32,)),
+            sem((7,)), sem((8,)), sem((4,)), sem((4,)), sem((6,)),
+        ],
+        compiler_params=pltpu.CompilerParams(
+            collective_id=0, has_side_effects=True, vmem_limit_bytes=56 << 20
+        ),
+        name="front",
+    )(hidden, cosine, sine, pos_q, pos_k, spread, packed, w_out, w_gate, w_up, w_down, grad_out)
 
 
 def permute(value, mask, size):
@@ -355,90 +648,46 @@
     kv_width = KV_HEADS * HD
     q_width = HEADS * HD
     both = ("dp", "ctx")
-
+    piece = -(-w_gate.shape[1] // (8 * 128)) * 128
     hidden_units = w_gate.shape[1]
-    piece = -(-hidden_units // (8 * 128)) * 128
-    stacked = jnp.pad(jnp.stack([w_gate, w_up, w_down]), ((0, 0), (0, 0), (0, 8 * piece - hidden_units)))
-    pieces = stacked.reshape(3, shard_rows, 4, 2, piece).transpose(2, 3, 0, 1, 4)
-    y, core, p = me // 16, (me // 4) % 2, me % 2
-    mine = lax.dynamic_index_in_dim(pieces, core, 1, False)
-    other = lax.dynamic_index_in_dim(pieces, 1 - core, 1, False)
-    other = permute(other, 4, size)
-    col = 2 * y + p
-    sets = []
-    for mask in (0, 1, 16, 17):
-        want = jnp.bitwise_xor(col, (mask // 16) * 2 + mask % 2)
-        chosen = jnp.stack(
-            [lax.dynamic_index_in_dim(mine, want, 0, False), lax.dynamic_index_in_dim(other, want, 0, False)]
-        )
-        sets.append(permute(chosen, mask, size) if mask else chosen)
-    whole = jnp.stack(sets)
-    whole = whole.reshape(2, 2, 2, 3, shard_rows, piece).transpose(0, 2, 1, 3, 4, 5)
-    whole = whole.reshape(8, 3, shard_rows, piece)
-    own_gu, own_d = whole[:, :2], whole[:, 2]
-    z_gu = permute(own_gu, 2, size)
-    x_gu = permute(own_gu, 8, size)
-    x_d = permute(own_d, 8, size)
-    z_d = permute(own_d, 2, size)
-    xz_gu = permute(z_gu, 8, size)
-    xz_d = permute(z_d, 8, size)
-
+
+    col = 2 * (me // 16) + me % 2
+    core = (me // 4) % 2
     grad_out = cotangent.reshape(row_count, D)
-    go_tiles = [grad_out] + [permute(grad_out, mask, size) for mask in (1, 16, 17)]
-    go_core = permute(jnp.stack(go_tiles), 4, size)
-
     places = jnp.arange(seq_len, dtype=jnp.int32)
     every_pos = jnp.repeat(span_order, span_len, axis=1) * span_len + places[None, :] % span_len
     local_pos = lax.dynamic_slice_in_dim(every_pos, ctx_rank * length, length, 1)
     cosine, sine = angles_for(local_pos.reshape(row_count), HD)
-    allowed = (every_pos[:, None, :] <= local_pos[:, :, None])[:, None, None]
+    cos_full = jnp.concatenate([cosine[:, 0], cosine[:, 0]], axis=1)
+    sin_full = jnp.concatenate([-sine[:, 0], sine[:, 0]], axis=1)
+    allowed = every_pos.reshape(1, seq_len) <= local_pos.reshape(length, 1)
 
     gains = jnp.stack([attn_gain, b_query, ffn_gain], axis=1)
-    pair = jnp.pad(jnp.concatenate([b_key, b_value]), (0, shard_rows - 2 * b_key.shape[0]))
+    per = b_key.shape[0]
+    pair = jnp.pad(jnp.concatenate([b_key, b_value]), (0, shard_rows - 2 * per))
     packed = jnp.concatenate(
         [w_query, w_key, w_value, gains, pair[:, None], jnp.zeros((shard_rows, 124), jnp.bfloat16)], axis=1
     )
-    packed = lax.all_gather(packed, both, axis=0, tiled=True)
-    out_full = lax.all_gather(w_out, both, axis=0, tiled=True)
     proj_width = q_width + 2 * kv_width
-    proj_full = packed[:, :proj_width]
-    small = packed[:, proj_width : proj_width + 4].astype(jnp.float32)
-    gain_one = small[:, 0]
-    gain_two = small[:, 2]
-    biases = small[:, 3].reshape(size, shard_rows)
-    per = b_key.shape[0]
-    bias = jnp.concatenate([small[:, 1], biases[:, :per].reshape(-1), biases[:, per : 2 * per].reshape(-1)])
-
-    source = hidden.reshape(row_count, D).astype(jnp.float32)
-    attn_factor, normed = norm_forward(source, gain_one)
-    raw = plain_dot(normed, proj_full) + bias
-    query_raw, key_raw = raw[:, :q_width], raw[:, q_width : q_width + kv_width]
-    value_low = raw[:, q_width + kv_width :].astype(jnp.bfloat16)
-    query_rot = rotate(query_raw.reshape(row_count, HEADS, HD), cosine, sine).astype(jnp.bfloat16)
-    query_rot = query_rot.reshape(batches, length, KV_HEADS, groups, HD)
-    key_rot = rotate(key_raw.reshape(row_count, KV_HEADS, HD), cosine, sine).astype(jnp.bfloat16)
-    key_value = jnp.concatenate([key_rot.reshape(row_count, kv_width), value_low], axis=1)
-    key_value = lax.all_gather(key_value.reshape(batches, length, 2 * kv_width), "ctx", axis=1, tiled=True)
-    key_all = key_value[:, :, :kv_width].reshape(batches, seq_len, KV_HEADS, HD)
-    value_all = key_value[:, :, kv_width:].reshape(batches, seq_len, KV_HEADS, HD)
-    scores = (
-        jnp.einsum("bqkgd,bskd->bkgqs", query_rot, key_all, preferred_element_type=jnp.float32)
-        * head_scale
-    )
-    masked = jnp.where(allowed, scores, masked_fill)
-    row_max = jnp.max(masked, axis=-1, keepdims=True)
-    expo = jnp.exp(masked - row_max)
-    expo_sum = jnp.sum(expo, axis=-1, keepdims=True)
-    log_total = row_max + jnp.log(expo_sum)
-    attend = (expo / expo_sum).astype(jnp.bfloat16)
-    mixed = jnp.einsum("bkgqs,bskd->bqkgd", attend, value_all, preferred_element_type=jnp.float32)
-    mixed = mixed.reshape(row_count, q_width).astype(jnp.bfloat16)
-    resid = source + right_dot(mixed, out_full)
-    ffn_factor, normed_two = norm_forward(resid, gain_two)
-
-    tiles, gu_grad, d_grad = ffn_call(
-        ctx_size, normed_two, go_tiles + [go_core], [own_gu, own_d, x_gu, x_d, z_gu, z_d, xz_gu, xz_d]
-    )
+    unit = jnp.arange(2 * kv_width)
+    unit = unit % kv_width // per * shard_rows + unit // kv_width * per + unit % per
+    spread = (jnp.arange(D)[:, None] == unit[None, :]).astype(jnp.bfloat16)
+    source = hidden.reshape(row_count, D)
+    normed, query_heads, key_value, log_total, mixed, resid, normed_two, small, proj_full, out_full, big, go_all = front_call(
+        ctx_size, source, cos_full, sin_full, local_pos.reshape(length, 1), every_pos.reshape(1, seq_len), spread,
+        packed, w_out, w_gate, w_up, w_down, grad_out,
+    )
+    source = source.astype(jnp.float32)
+    gain_one, gain_two = small[0], small[2]
+    attn_factor = lax.rsqrt(jnp.mean(source * source, axis=-1, keepdims=True) + norm_eps)
+    ffn_factor = lax.rsqrt(jnp.mean(resid * resid, axis=-1, keepdims=True) + norm_eps)
+    proj_full = proj_full[:, :proj_width]
+    query_heads = query_heads.reshape(KV_HEADS, groups, length, HD)
+    log_total = log_total[:, :, :1].reshape(KV_HEADS, groups, length, 1)
+    key_value = key_value.reshape(seq_len, 2, KV_HEADS, HD)
+    key_all, value_all = key_value[:, 0], key_value[:, 1]
+
+    tiles, gu_grad, d_grad = ffn_call(ctx_size, shard_rows, normed_two, go_all, big)
     sums = jnp.sum(tiles.astype(jnp.float32), axis=0)
     grad_norm_two = sums[0]
     result = (resid + sums[1]).astype(jnp.bfloat16).reshape(batches, length, D)
@@ -473,29 +722,22 @@
     grad_resid = grad_plain + resid_back
     grad_attn = grad_resid.astype(jnp.bfloat16)
     grad_mixed = plain_dot(grad_attn, out_full).astype(jnp.bfloat16)
-    grad_mixed = grad_mixed.reshape(batches, length, KV_HEADS, groups, HD)
+    grad_mixed = grad_mixed.reshape(length, KV_HEADS, groups, HD).transpose(1, 2, 0, 3)
     scores = (
-        jnp.einsum("bqkgd,bskd->bkgqs", query_rot, key_all, preferred_element_type=jnp.float32)
-        * head_scale
+        jnp.einsum("kgqd,skd->kgqs", query_heads, key_all, preferred_element_type=jnp.float32) * head_scale
     )
     masked = jnp.where(allowed, scores, masked_fill)
     attend_full = jnp.exp(masked - log_total)
     attend = attend_full.astype(jnp.bfloat16)
-    grad_attend = jnp.einsum(
-        "bqkgd,bskd->bkgqs", grad_mixed, value_all, preferred_element_type=jnp.float32
-    )
-    value_grad_all = jnp.einsum(
-        "bkgqs,bqkgd->bskd", attend, grad_mixed, preferred_element_type=jnp.float32
-    )
+    grad_attend = jnp.einsum("kgqd,skd->kgqs", grad_mixed, value_all, preferred_element_type=jnp.float32)
+    value_grad_all = jnp.einsum("kgqs,kgqd->skd", attend, grad_mixed, preferred_element_type=jnp.float32)
     delta = jnp.sum(grad_attend * attend_full, axis=-1, keepdims=True)
     grad_scores = (attend_full * (grad_attend - delta)).astype(jnp.bfloat16)
     query_grad_rot = (
-        jnp.einsum("bkgqs,bskd->bqkgd", grad_scores, key_all, preferred_element_type=jnp.float32)
-        * head_scale
+        jnp.einsum("kgqs,skd->qkgd", grad_scores, key_all, preferred_element_type=jnp.float32) * head_scale
     )
     key_grad_all = (
-        jnp.einsum("bkgqs,bqkgd->bskd", grad_scores, query_rot, preferred_element_type=jnp.float32)
-        * head_scale
+        jnp.einsum("kgqs,kgqd->skd", grad_scores, query_heads, preferred_element_type=jnp.float32) * head_scale
     )
     kv_grad = jnp.concatenate(
         [key_grad_all.reshape(batches, seq_len, kv_width), value_grad_all.reshape(batches, seq_len, kv_width)],

time: 902 us -> 740 us (0.82)
  waiting for transfers between devices: 506 us -> 223 us
  Pallas kernels: 126 us -> 342 us
  local copies, waits for them, and re-layouts: 109 us -> 59.7 us
  matrix products: 51.8 us -> 34 us
  starting transfers between devices: 35 us -> 18.3 us
  other arithmetic: 50.8 us -> 41.1 us
    pallas_call x0 -> x1, Pallas kernels: none -> 220 us  [front_call(): pl.pallas_call(functools.partial(front_kernel, ctx_size), out_shape=tuple...]
    ppermute x24 -> x10, waiting for transfers between devices: 344 us -> 147 us  [permute(): lax.ppermute(value, ('dp', 'ctx'), [(i, i ^ mask) for i in range(size)])]
    all_gather x3 -> x0, waiting for transfers between devices: 59.6 us -> none  [the longest x1 59.5 us: fast_device(): packed = lax.all_gather(packed, both, axis=0, tiled=True)]
    reduce_scatter x1, waiting for transfers between devices: 102 us -> 76.4 us  [fast_device(): lax.psum_scatter(part, both, scatter_dimension=0, tiled=True)]
    ppermute x24 -> x10, starting transfers between devices: 34.3 us -> 18 us  [permute(): lax.ppermute(value, ('dp', 'ctx'), [(i, i ^ mask) for i in range(size)])]
    another operation x12 -> x2, other arithmetic: 16.2 us -> 1.63 us
    unnamed x90 -> x41, local copies, waits for them, and re-layouts: 13.4 us -> 3.27 us
    dot_general x6 -> x5, matrix products: 26.3 us -> 17.5 us  [the longest x1 7.2 us: fast_device(): jnp.einsum('kgqd,skd->kgqs', grad_mixed, value_all, preferred_element_typ...]
  transfers between devices with their start and end apart: 30 -> 13, of which waited for: 13 -> 8; matrix products, arithmetic and copies ran while one was open for 15% -> 11% of each run, Pallas kernels for 0% -> 0%
where the time goes in v2:
time: 740 us; the launch traced here: 733 us
  Pallas kernels  342 us (46%)
  waiting for transfers between devices  223 us (30%)
  local copies, waits for them, and re-layouts  59.7 us (8%)
  other arithmetic  41.1 us (6%)
  matrix products  34 us (5%)
  starting transfers between devices  18.3 us (2%)
  between operations  14.5 us (2%)
    pallas_call x1, Pallas kernels, front_call(): pl.pallas_call(functools.partial(front_kernel, ctx_size), out_shape=tuple...  220 us
    ppermute x10, waiting for transfers between devices, permute(): lax.ppermute(value, ('dp', 'ctx'), [(i, i ^ mask) for i in range(size)])  147 us
    pallas_call x1, Pallas kernels, ffn_call(): pl.pallas_call(functools.partial(ffn_kernel, ctx_size), out_shape=(jax.Sh...  121 us
    reduce_scatter x1, waiting for transfers between devices, fast_device(): lax.psum_scatter(part, both, scatter_dimension=0, tiled=True)  76.4 us
    ppermute x10, starting transfers between devices, permute(): lax.ppermute(value, ('dp', 'ctx'), [(i, i ^ mask) for i in range(size)])  18 us
  transfers between devices with their start and end apart: 13, of which 8 were waited for; matrix products, arithmetic and copies ran while one was open for 11% of the time, Pallas kernels for 0%

profile of v2, /device:TPU:0, one launch (start us, length us, event | category | flops | bytes accessed | tf_op | source)
XLA Modules:
  0.0 732.5 jit_solution(16208920635216775049)
XLA Ops:
  9.0 1.8 fusion.9.spread
  16.1 220.3 %front.1 = (bf16[256,1536]{1,0:T(8,128)(2,1)}, bf16[12,256,128]{2,1,0:T(8,128)(2,1)}, bf16[4,256,512]{2,1,0:T(8,128)(2,1)}, f32[12,256,128]{2,1,0:T(8,128)}, bf1...) custom-call(bf16[256,1536]{1,0:T(8,128)(2,1)} %bitcast.168, ...), custom_call_target="tpu_custom_call" | custom-call | tf_op jit(solution)/shard_map/front/pallas_call | solution.py:588
  237.8 1.5 fusion.77
  239.3 121.3 %ffn.1 = (bf16[4,2,256,1536]{3,2,1,0:T(8,128)(2,1)}, bf16[2,2,8,2,48,1152]{5,4,3,2,1,0:T(8,128)(2,1)}, bf16[2,2,8,48,1152]{4,3,2,1,0:T(8,128)(2,1)}) custom-call(bf16[256,1536]{1,0:T(8,128)(2,1)} %get-tuple-element.30.n_own, bf16[8,256,1536]{2,1,0:T(8,128)(2,1)} %get-tuple-element.31.go_all, bf16[1536,3456]{1,0:T(8,128)(2,1)} %get-tuple-element.32.big), custom_call_target="tpu_custom_call" | custom-call | tf_op jit(solution)/shard_map/ffn/pallas_call | solution.py:271
  360.6 4.2 convert_reduce_fusion
  366.5 1.4 multiply_add_fusion
  368.6 2.3 convolution_convert_fusion.2
  370.9 2.4 copy.83
  373.3 1.9 slice_reduce_fusion
  375.4 1.8 fusion.43
  377.2 4.1 fusion.30
  381.3 7.2 multiply_reduce_fusion
  388.5 6.7 multiply_convert_fusion
  396.4 1.5 copy-done
  399.4 3.6 convolution_convert_fusion.1
  403.3 3.0 slice_bitcast_fusion.10
  408.3 4.2 slice_bitcast_fusion.1
  414.5 3.4 convolution_multiply_fusion
  418.3 1.6 add_convert_fusion
  420.2 9.0 %collective-permute-done.4 = bf16[8,48,1152]{2,1,0:T(8,128)(2,1)} collective-permute-done((bf16[8,48,1152]{2,1,0:T(8,128)(2,1)}, bf16[8,48,1152]{2,1,0:T(8,128)(2,1)}, u32[]{:S(2)}, u32[]{:S(2)}) %collective-permute-start.4) | collective-permute-done | bytes 884768 | tf_op jit(solution)/shard_map/ppermute | solution.py:612
  429.2 2.6 fusion.13
  431.7 3.9 collective-permute-start.5
  435.7 52.0 %collective-permute-done.1 = bf16[8,2,48,1152]{3,2,1,0:T(8,128)(2,1)} collective-permute-done((bf16[8,2,48,1152]{3,2,1,0:T(8,128)(2,1)}, bf16[8,2,48,1152]{3,2,1,0:T(8,128)(2,1)}, u32[]{:S(2)}, u32[]{:S(2)}) %collective-permute-start.1) | collective-permute-done | bytes 1769504 | tf_op jit(solution)/shard_map/ppermute | solution.py:612
  487.7 3.7 fusion.6
  491.4 6.5 collective-permute-start.2
  500.3 6.1 fusion.21
  506.7 4.5 convolution_convert_fusion
  511.3 11.4 %concatenate.61 = bf16[1536,2176]{1,0:T(8,128)(2,1)} concatenate(bf16[1536,2048]{1,0:T(8,128)(2,1)} %convolution_convert_fusion, bf16[1536,1]{1,0:T(8,128)(2,1)S(1)} %stack.51, bf16[1536,1]{1,0:T(8,128)(2,1)S(1)} %stack.52, bf16[1536,1]{1,0:T(8,128)(2,1)S(1)} %stack.53, bf16[1536,1]{1,0:T(8,128)(2,1)S(1)} %stack_reshape.5, bf16[1536,124]{1,0:T(8,128)(2,1)S(1)} %broadcast_in_dim.21), dimensions={1} | concatenate | bytes 13369344 | tf_op jit(solution)/shard_map/concatenate | solution.py:768
  522.7 2.0 fusion.15
  524.8 4.1 collective-permute-done
  528.8 51.2 %collective-permute-done.2 = bf16[8,2,48,1152]{3,2,1,0:T(8,128)(2,1)} collective-permute-done((bf16[8,2,48,1152]{3,2,1,0:T(8,128)(2,1)}, bf16[8,2,48,1152]{3,2,1,0:T(8,128)(2,1)}, u32[]{:S(2)}, u32[]{:S(2)}) %collective-permute-start.2) | collective-permute-done | bytes 1769504 | tf_op jit(solution)/shard_map/ppermute | solution.py:612
  580.0 3.2 fusion.8
  583.6 1.6 collective-permute-start.7
  585.2 1.9 collective-permute-start.8
  587.1 16.5 %collective-permute-done.6 = bf16[2,3,48,1152]{3,2,1,0:T(8,128)(2,1)S(1)} collective-permute-done((bf16[2,3,48,1152]{3,2,1,0:T(8,128)(2,1)S(1)}, bf16[2,3,48,1152]{3,2,1,0:T(8,128)(2,1)S(1)}, u32[]{:S(2)}, u32[]{:S(2)}) %collective-permute-start.6) | collective-permute-done | bytes 663584 | tf_op jit(solution)/shard_map/ppermute | solution.py:612
  603.5 14.0 %collective-permute-done.8 = bf16[2,3,48,1152]{3,2,1,0:T(8,128)(2,1)S(1)} collective-permute-done((bf16[2,3,48,1152]{3,2,1,0:T(8,128)(2,1)S(1)}, bf16[2,3,48,1152]{3,2,1,0:T(8,128)(2,1)S(1)}, u32[]{:S(2)}, u32[]{:S(2)}) %collective-permute-start.8) | collective-permute-done | bytes 663584 | tf_op jit(solution)/shard_map/ppermute | solution.py:612
  617.9 1.7 slice_bitcast_fusion.8
  620.1 3.1 fusion.20
  623.3 1.6 pad_maximum_fusion.1
  624.9 2.4 gather_fusion
  627.3 2.8 gather_fusion.1
  630.1 3.6 copy.103
  633.6 5.8 reshape.379
  639.8 2.4 slice_bitcast_fusion.2
  642.3 1.6 convert_element_type.146
  643.9 76.4 %reduce-scatter.6.cloned.1.call-done = bf16[48,2176]{1,0:T(8,128)(2,1)} async-done(((bf16[1536,2176]{1,0:T(8,128)(2,1)}), bf16[48,2176]{1,0:T(8,128)(2,1)}) %reduce-scatter.6.cloned.1.call-update) | async-done | bytes 208912 | tf_op jit(solution)/shard_map/reduce_scatter | solution.py:771
  722.7 1.6 slice.203
  724.4 1.4 fusion.79
  (119 shorter events, 25.3 us)
Async XLA Ops:
  7.2 8.1 %copy-start.12 = (bf16[48,1536]{1,0:T(8,128)(2,1)S(1)}, bf16[48,1536]{1,0:T(8,128)(2,1)}, u32[]{:S(2)}) copy-start(bf16[48,1536]{1,0:T(8,128)(2,1)} %param.19) | copy-start | bytes 442372
  7.2 8.1 %copy-start.14 = (bf16[48,256]{1,0:T(8,128)(2,1)S(1)}, bf16[48,256]{1,0:T(8,128)(2,1)}, u32[]{:S(2)}) copy-start(bf16[48,256]{1,0:T(8,128)(2,1)} %param.21) | copy-start | bytes 73732
  7.2 8.1 %copy-start.15 = (bf16[48,256]{1,0:T(8,128)(2,1)S(1)}, bf16[48,256]{1,0:T(8,128)(2,1)}, u32[]{:S(2)}) copy-start(bf16[48,256]{1,0:T(8,128)(2,1)} %param.23) | copy-start | bytes 73732
  7.2 490.7 %reduce-scatter.4.cloned.1.call-start = ((), (), s32[]{:S(2)}) async-start(), calls=%async_computation.3 | async-start | bytes 1310720 | tf_op jit(solution)/shard_map/reduce_scatter | solution.py:746
  8.0 8.1 %copy-start.13 = (s32[1,1024]{1,0:T(1,128)}, s32[1,1024]{1,0:T(1,128)S(1)}, u32[]{:S(2)}) copy-start(s32[1,1024]{1,0:T(1,128)S(1)} %fusion.55.pos_k) | copy-start | bytes 12292
  360.6 4.2 copy-start.4
  364.8 1.6 copy-start.8
  365.9 2.5 slice-start.2
  366.4 2.2 slice-start.3
  367.8 31.2 %copy-start.1 = (f32[256,1536]{1,0:T(8,128)}, f32[256,1536]{1,0:T(8,128)S(1)}, u32[]{:S(2)}) copy-start(f32[256,1536]{1,0:T(8,128)S(1)} %get-tuple-element.60) | copy-start | bytes 4718596
  370.9 4.5 copy-start.3
  375.4 1.8 copy-start.7
  377.2 4.1 copy-start.9
  395.3 2.6 copy-start
  397.9 1.5 copy-start.11
  399.0 243.3 %reduce-scatter.8.cloned.1.call-start = ((), (), s32[]{:S(2)}) async-start(), calls=%async_computation.5 | async-start | bytes 4866048 | tf_op jit(solution)/shard_map/reduce_scatter | solution.py:772
  403.0 11.4 %slice-start = ((s8[6291456]{0:T(1024)(128)(4,1)}), s8[2097152]{0:T(1024)(128)(4,1)S(1)}, s32[]{:S(2)}) async-start(s8[6291456]{0:T(1024)(128)(4,1)} %bitcast.163), calls=%async_computation.6 | async-start | bytes 4194304
  403.1 317.3 %reduce-scatter.6.cloned.1.call-start = ((), (), s32[]{:S(2)}) async-start(), calls=%async_computation.4 | async-start | bytes 6893568 | tf_op jit(solution)/shard_map/reduce_scatter | solution.py:771
  403.3 11.2 %slice-start.1 = ((s8[6291456]{0:T(1024)(128)(4,1)}), s8[4194304]{0:T(1024)(128)(4,1)S(1)}, s32[]{:S(2)}) async-start(s8[6291456]{0:T(1024)(128)(4,1)} %bitcast.163), calls=%async_computation.7 | async-start | bytes 8388608
  406.3 22.9 %collective-permute-start.4 = (bf16[8,48,1152]{2,1,0:T(8,128)(2,1)}, bf16[8,48,1152]{2,1,0:T(8,128)(2,1)}, u32[]{:S(2)}, u32[]{:S(2)}) collective-permute-start(bf16[8,48,1152]{2,1,0:T(8,128)(2,1)} %get-tuple-element.63), channel_id=1, source_target_pairs={{0,8},{1,9},{2,10},{3,11},{4,12},{5,13},{6,14},{7,15},{8,0},{9,1},... | collective-permute-start | bytes 2654216 | tf_op jit(solution)/shard_map/ppermute | solution.py:612
  407.1 115.6 %collective-permute-start.3 = (bf16[8,48,1152]{2,1,0:T(8,128)(2,1)}, bf16[8,48,1152]{2,1,0:T(8,128)(2,1)}, u32[]{:S(2)}, u32[]{:S(2)}) collective-permute-start(bf16[8,48,1152]{2,1,0:T(8,128)(2,1)} %get-tuple-element.62), channel_id=1, source_target_pairs={{0,8},{1,9},{2,10},{3,11},{4,12},{5,13},{6,14},{7,15},{8,0},{9,1},... | collective-permute-start | bytes 2654216 | tf_op jit(solution)/shard_map/ppermute | solution.py:612
  412.4 75.3 %collective-permute-start.1 = (bf16[8,2,48,1152]{3,2,1,0:T(8,128)(2,1)}, bf16[8,2,48,1152]{3,2,1,0:T(8,128)(2,1)}, u32[]{:S(2)}, u32[]{:S(2)}) collective-permute-start(bf16[8,2,48,1152]{3,2,1,0:T(8,128)(2,1)} %get-tuple-element.56), channel_id=1, source_target_pairs={{0,8},{1,9},{2,10},{3,11},{4,12},{5,13},{6,14},{7,15},{8,0},{9,1},... | collective-permute-start | bytes 5308424 | tf_op jit(solution)/shard_map/ppermute | solution.py:612
  413.3 115.5 %collective-permute-start = (bf16[8,2,48,1152]{3,2,1,0:T(8,128)(2,1)}, bf16[8,2,48,1152]{3,2,1,0:T(8,128)(2,1)}, u32[]{:S(2)}, u32[]{:S(2)}) collective-permute-start(bf16[8,2,48,1152]{3,2,1,0:T(8,128)(2,1)} %get-tuple-element.55), channel_id=1, source_target_pairs={{0,8},{1,9},{2,10},{3,11},{4,12},{5,13},{6,14},{7,15},{8,0},{9,1},... | collective-permute-start | bytes 5308424 | tf_op jit(solution)/shard_map/ppermute | solution.py:612
  417.8 2.1 copy-start.5
  431.7 91.0 %collective-permute-start.5 = (bf16[8,48,1152]{2,1,0:T(8,128)(2,1)}, bf16[8,48,1152]{2,1,0:T(8,128)(2,1)}, u32[]{:S(2)}, u32[]{:S(2)}) collective-permute-start(bf16[8,48,1152]{2,1,0:T(8,128)(2,1)} %fusion.13), channel_id=1, source_target_pairs={{0,2},{1,3},{2,0},{3,1},{4,6},{5,7},{6,4},{7,5},{8,10},{9,11},{10,... | collective-permute-start | bytes 2654216 | tf_op jit(solution)/shard_map/ppermute | solution.py:612
  491.4 88.6 %collective-permute-start.2 = (bf16[8,2,48,1152]{3,2,1,0:T(8,128)(2,1)}, bf16[8,2,48,1152]{3,2,1,0:T(8,128)(2,1)}, u32[]{:S(2)}, u32[]{:S(2)}) collective-permute-start(bf16[8,2,48,1152]{3,2,1,0:T(8,128)(2,1)} %fusion.6), channel_id=1, source_target_pairs={{0,2},{1,3},{2,0},{3,1},{4,6},{5,7},{6,4},{7,5},{8,10},{9,11},{10,... | collective-permute-start | bytes 5308424 | tf_op jit(solution)/shard_map/ppermute | solution.py:612
  500.3 6.4 copy-start.10
  583.5 20.0 %collective-permute-start.6 = (bf16[2,3,48,1152]{3,2,1,0:T(8,128)(2,1)S(1)}, bf16[2,3,48,1152]{3,2,1,0:T(8,128)(2,1)S(1)}, u32[]{:S(2)}, u32[]{:S(2)}) collective-permute-start(bf16[2,3,48,1152]{3,2,1,0:T(8,128)(2,1)S(1)} %get-tuple-element.67), channel_id=1, source_target_pairs={{0,1},{1,0},{2,3},{3,2},{4,5},{5,4},{6,7},{7,6},{8,9},{9,8},{10,11... | collective-permute-start | bytes 1990664 | tf_op jit(solution)/shard_map/ppermute | solution.py:612
  583.6 20.0 %collective-permute-start.7 = (bf16[2,3,48,1152]{3,2,1,0:T(8,128)(2,1)S(1)}, bf16[2,3,48,1152]{3,2,1,0:T(8,128)(2,1)S(1)}, u32[]{:S(2)}, u32[]{:S(2)}) collective-permute-start(bf16[2,3,48,1152]{3,2,1,0:T(8,128)(2,1)S(1)} %get-tuple-element.69), channel_id=1, source_target_pairs={{0,16},{1,17},{2,18},{3,19},{4,20},{5,21},{6,22},{7,23},{8,24},{9,... | collective-permute-start | bytes 1990664 | tf_op jit(solution)/shard_map/ppermute | solution.py:612
  585.2 32.4 %collective-permute-start.8 = (bf16[2,3,48,1152]{3,2,1,0:T(8,128)(2,1)S(1)}, bf16[2,3,48,1152]{3,2,1,0:T(8,128)(2,1)S(1)}, u32[]{:S(2)}, u32[]{:S(2)}) collective-permute-start(bf16[2,3,48,1152]{3,2,1,0:T(8,128)(2,1)S(1)} %get-tuple-element.68), channel_id=1, source_target_pairs={{0,17},{1,16},{2,19},{3,18},{4,21},{5,20},{6,23},{7,22},{8,25},{9,... | collective-permute-start | bytes 1990664 | tf_op jit(solution)/shard_map/ppermute | solution.py:612
  617.9 2.1 copy-start.2
  619.6 3.6 collective-permute-start.9
  620.1 3.2 copy-start.6
Sparse Core Ops, SparseCore 0:
  399.1 28.8 reduce-scatter.3
  434.4 162.7 reduce-scatter.7
  602.8 117.4 reduce-scatter.5

commit v3 on v2

--- a/solution.py
+++ b/solution.py
@@ -96,7 +96,7 @@
 
 def ffn_kernel(
     ctx_size, n_own, go_all, big,
-    hr, dgu, dd,
+    hr, grads,
     wgu, wd, nt, go, ggu, act, csend, crecv, hpart, stage,
     w_sem, io_sem, n_send, n_recv, f_send, f_recv, c_send, c_recv, o_send, o_recv, st_sem,
 ):
@@ -106,7 +106,7 @@
     y, x, c = dp // 4, (dp // 2) % 2, dp % 2
     h, p = ctx // 2, ctx % 2
     width = wd.shape[1]
-    shard = dgu.shape[4]
+    shard = grads.shape[3]
     rows, model = n_own.shape
 
     def at(index):
@@ -242,13 +242,7 @@
             cr, hrel, pr = either(j // 4, c), either((j // 2) % 2, h), either(j % 2, p)
             block = yr * 4 + cr * 2 + pr
             row = pl.ds(j * shard, shard)
-            for half in range(2):
-                pltpu.make_async_copy(
-                    stage.at[slot, row, pl.ds(half * width, width)], dgu.at[xr, hrel, block, half], st_sem.at[slot]
-                ).start()
-            pltpu.make_async_copy(
-                stage.at[slot, row, pl.ds(2 * width, width)], dd.at[xr, hrel, block], st_sem.at[slot]
-            ).start()
+            pltpu.make_async_copy(stage.at[slot, row], grads.at[xr, hrel, block], st_sem.at[slot]).start()
         return carry
 
     lax.fori_loop(0, 4, weights, 0)
@@ -272,11 +266,10 @@
         functools.partial(ffn_kernel, ctx_size),
         out_shape=(
             jax.ShapeDtypeStruct((4, 2, rows, model), low),
-            jax.ShapeDtypeStruct((2, 2, 8, 2, shard, width), low),
-            jax.ShapeDtypeStruct((2, 2, 8, shard, width), low),
+            jax.ShapeDtypeStruct((2, 2, 8, shard, 3 * width), low),
         ),
         in_specs=[pl.BlockSpec(memory_space=pl.ANY)] * 3,
-        out_specs=[pl.BlockSpec(memory_space=pl.ANY)] * 3,
+        out_specs=[pl.BlockSpec(memory_space=pl.ANY)] * 2,
         scratch_shapes=[
             pltpu.VMEM((model, 2 * width), low),
             pltpu.VMEM((model, width), low),
@@ -314,7 +307,7 @@
 def front_kernel(
     ctx_size, hidden, cosine, sine, pos_q, pos_k, spread, packed, w_out, w_gate, w_up, w_down, grad_out,
     normed_o, query_o, kv_o, total_o, mixed_o, resid_o, normed_two_o, small_o, proj_o, out_o, big, go,
-    proj, out_w, source, query, kv, mixed, total,
+    proj, out_w, source, query, kv, mixed,
     load_sem, ag_send, ag_recv, core_send, core_recv, big_send, big_recv, go_send, go_recv, kv_send, kv_recv, back_sem,
 ):
     dp = lax.axis_index("dp")
@@ -371,26 +364,29 @@
 
     pair = ((proj, 0), (out_w, 1))
 
-    def ag(mask, over):
-        for ref, n in pair:
-            remote(ref.at[block(mask)], ref.at[block(mask)], ag_send.at[n], ag_recv.at[n, mask | over], over).start()
-
-    def ag_wait(mask):
-        for ref, n in pair:
-            remote(ref.at[block(mask)], ref.at[block(mask)], ag_send.at[n], ag_recv.at[n, mask], 1).wait_recv()
-
-    def group(mask):
-        return [
-            remote(ref.at[block(mask, 4)], ref.at[block(mask, 4)], core_send.at[n, mask // 8], core_recv.at[n, mask // 8], 4)
-            for ref, n in pair
-        ]
+    def ag(n, mask, over):
+        ref = pair[n][0]
+        remote(ref.at[block(mask)], ref.at[block(mask)], ag_send.at[n], ag_recv.at[n, mask | over], over).start()
+
+    def ag_pass(n, mask, *overs):
+        ref = pair[n][0]
+        remote(ref.at[block(mask)], ref.at[block(mask)], ag_send.at[n], ag_recv.at[n, mask], 1).wait_recv()
+        for over in overs:
+            ag(n, mask, over)
+
+    def group(n, mask):
+        ref = pair[n][0]
+        part = ref.at[block(mask, 4)]
+        return remote(part, part, core_send.at[n, mask // 8], core_recv.at[n, mask // 8], 4)
 
     def group_wait(mask, n):
         ref = pair[n][0]
         remote(ref.at[block(mask | 4, 4)], ref.at[block(mask | 4, 4)], core_send.at[n, mask // 8], core_recv.at[n, mask // 8], 4).wait_recv()
 
     for over in (2, 1, 8, 16):
-        ag(0, over)
+        ag(0, 0, over)
+    for over in (2, 1, 8):
+        ag(1, 0, over)
 
     for copy in cuts:
         copy.wait()
@@ -402,63 +398,45 @@
 
     own_big = pltpu.make_async_copy(source.at[column(0)], big.at[block(0)], load_sem.at[0])
     own_big.start()
-    for mask in (4, 1, 16, 5, 20, 17, 21):
+    def cut(mask):
         remote(source.at[column(mask)], big.at[block(0)], big_send.at[0], big_recv.at[mask], mask).start()
-    first_z = remote(source.at[column(0)], big.at[block(0)], big_send.at[0], big_recv.at[2], 2)
-    first_z.start()
 
     def big_forward(mask, over):
         remote(big.at[block(mask)], big.at[block(mask)], big_send.at[0], big_recv.at[mask | over], over).start()
 
-    def big_wait(mask):
+    def big_pass(mask, *overs):
         remote(big.at[block(mask)], big.at[block(mask)], big_send.at[0], big_recv.at[mask], 1).wait_recv()
-
-    ag_wait(1)
-    for over in (8, 16):
-        ag(1, over)
-    ag_wait(8)
-    ag(8, 16)
-    ag_wait(2)
-    for over in (1, 8, 16):
-        ag(2, over)
-    ag_wait(9)
-    ag(9, 16)
-    big_wait(4)
-    big_forward(4, 2)
-    big_wait(1)
-    big_forward(1, 2)
-    ag_wait(3)
-    for over in (8, 16):
-        ag(3, over)
-    for copy in group(0):
-        copy.start()
-    ag_wait(10)
-    ag(10, 16)
-    ag_wait(11)
-    ag(11, 16)
-    for copy in group(8):
-        copy.start()
+        for over in overs:
+            big_forward(mask, over)
+
+    for mask in (4, 1, 5):
+        cut(mask)
+    remote(source.at[column(0)], big.at[block(0)], big_send.at[0], big_recv.at[2], 2).start()
+
+    ag_pass(0, 1, 8, 16)
+    ag_pass(0, 8, 16)
+    ag_pass(0, 2, 1, 8, 16)
+    ag_pass(0, 9, 16)
+    ag_pass(0, 3, 8, 16)
+    group(0, 0).start()
+    big_pass(4, 2)
+    ag_pass(0, 10, 16)
+    ag_pass(0, 11, 16)
+    group(0, 8).start()
+    for mask in (16, 20, 17, 21):
+        cut(mask)
+    ag_pass(1, 1, 8)
+    ag_pass(1, 2, 1, 8)
     remote(source.at[column(0)], big.at[block(0)], big_send.at[0], big_recv.at[8], 8).start()
-    for mask in (16, 5, 20, 17, 21):
-        big_wait(mask)
-        big_forward(mask, 2)
-    for mask in (4, 1, 16, 5):
-        big_forward(mask, 8)
+    big_forward(4, 8)
     for mask in (16, 17, 18, 19):
-        ag_wait(mask)
-    for copy in group(16):
-        copy.start()
+        ag_pass(0, mask)
+    group(0, 16).start()
+    ag_pass(1, 3, 8)
+    big_pass(1, 2, 8)
     for mask in (24, 25, 26, 27):
-        ag_wait(mask)
-    for copy in group(24):
-        copy.start()
-    for mask in (20, 17, 21):
-        big_forward(mask, 8)
-    own_go = pltpu.make_async_copy(grad_out, go.at[0], load_sem.at[1])
-    own_go.start()
-    for o, mask in ((1, 1), (2, 16), (3, 17)):
-        remote(grad_out, go.at[2 * o], go_send.at[o], go_recv.at[2 * o], mask).start()
-    remote(grad_out, go.at[1], go_send.at[0], go_recv.at[1], 4).start()
+        ag_pass(0, mask)
+    group(0, 24).start()
     for mask in (0, 8, 16, 24):
         group_wait(mask, 0)
 
@@ -481,19 +459,29 @@
 
     kv_push(0, 2).start()
     kv_push(0, 1).start()
+    big_pass(5, 2, 8)
+    big_pass(16, 2, 8)
+    for mask in (0, 1, 2, 3):
+        ag(1, mask, 16)
+    group(1, 0).start()
+    for mask in (8, 9, 10, 11):
+        ag_pass(1, mask, 16)
+    group(1, 8).start()
     for half in range(2):
         part = half * (q_width // 2)
         raw = dot(normed_o[...], proj[:, part : part + q_width // 2], ((1,), (0,)))
         raw = raw + small[1:2, part : part + q_width // 2]
         for i in range(HEADS // 2):
             query[half * (HEADS // 2) + i] = turn(raw[:, i * HD : (i + 1) * HD], cos, sin).astype(jnp.bfloat16)
-    big_wait(2)
-    big_forward(2, 8)
     kv_push(0, 2).wait_recv()
     kv_push(2, 1).start()
-    for mask in (6, 3):
-        big_wait(mask)
-        big_forward(mask, 8)
+    for mask in (20, 17, 21):
+        big_pass(mask, 2, 8)
+    for o, mask in ((1, 1), (2, 16), (3, 17)):
+        remote(grad_out, go.at[2 * o], go_send.at[o], go_recv.at[2 * o], mask).start()
+    remote(grad_out, go.at[1], go_send.at[0], go_recv.at[1], 4).start()
+    for mask in (2, 6):
+        big_pass(mask, 8)
     kv_push(0, 1).wait_recv()
     kv_push(2, 1).wait_recv()
     query_back = pltpu.make_async_copy(query, query_o, back_sem.at[0])
@@ -512,20 +500,22 @@
         expo_sum = jnp.sum(expo, axis=-1, keepdims=True)
         attend = (expo / expo_sum).astype(jnp.bfloat16)
         mixed[:, pl.ds(pl.multiple_of(n * HD, HD), HD)] = dot(attend, vals, ((1,), (0,))).astype(jnp.bfloat16)
-        total[n] = jnp.broadcast_to(top + jnp.log(expo_sum), (rows, HD))
+        lane = lax.broadcasted_iota(jnp.int32, (rows, HD), 1)
+        total_o[...] = jnp.where(lane == n, top + jnp.log(expo_sum), total_o[...])
         return carry
 
-    lax.fori_loop(0, HEADS // 2, head, 0)
-    for o, mask in ((1, 1), (2, 16), (3, 17)):
-        remote(grad_out, go.at[2 * o], go_send.at[o], go_recv.at[2 * o], mask).wait_recv()
-        remote(go.at[2 * o], go.at[2 * o + 1], go_send.at[3 + o], go_recv.at[2 * o + 1], 4).start()
-    big_wait(18)
-    big_forward(18, 8)
-    lax.fori_loop(HEADS // 2, HEADS, head, 0)
+    total_o[...] = jnp.zeros_like(total_o)
+    lax.fori_loop(0, HEADS, head, 0)
+    own_go = pltpu.make_async_copy(grad_out, go.at[0], load_sem.at[1])
+    own_go.start()
     mixed_back = pltpu.make_async_copy(mixed, mixed_o, back_sem.at[2])
     mixed_back.start()
-    total_back = pltpu.make_async_copy(total, total_o, back_sem.at[3])
-    total_back.start()
+    for mask in (3, 7):
+        big_pass(mask, 8)
+    for n, mask in enumerate((16, 17, 18, 19, 24, 25, 26, 27)):
+        ag_pass(1, mask)
+        if n % 4 == 3:
+            group(1, mask & 24).start()
     for mask in (0, 8, 16, 24):
         group_wait(mask, 1)
     proj_back = pltpu.make_async_copy(proj, proj_o, back_sem.at[4])
@@ -536,12 +526,14 @@
     resid_o[...] = resid
     factor = lax.rsqrt(jnp.mean(resid * resid, axis=-1, keepdims=True) + norm_eps)
     normed_two_o[...] = (resid * factor * small_o[2:3]).astype(jnp.bfloat16)
-    for mask in (7, 22, 19, 23):
-        big_wait(mask)
-        big_forward(mask, 8)
+    for o, mask in ((1, 1), (2, 16), (3, 17)):
+        remote(grad_out, go.at[2 * o], go_send.at[o], go_recv.at[2 * o], mask).wait_recv()
+        remote(go.at[2 * o], go.at[2 * o + 1], go_send.at[3 + o], go_recv.at[2 * o + 1], 4).start()
+    for mask in (18, 22, 19, 23):
+        big_pass(mask, 8)
 
     for mask in (8, 12, 9, 24, 13, 28, 25, 29, 10, 14, 11, 26, 15, 30, 27, 31):
-        big_wait(mask)
+        big_pass(mask)
     own_big.wait()
     own_go.wait()
     sent = 7 + 8 + 8 + 8
@@ -549,7 +541,7 @@
     for ref, n in pair:
         drain(ref.at[pl.ds(0, 15 * shard)], ag_send.at[n])
         for mask in (0, 8, 16, 24):
-            group(mask)[n].wait_send()
+            group(n, mask).wait_send()
     remote(grad_out, go.at[1], go_send.at[0], go_recv.at[1], 4).wait()
     for o, mask in ((1, 1), (2, 16), (3, 17)):
         remote(grad_out, go.at[2 * o], go_send.at[o], go_recv.at[2 * o], mask).wait_send()
@@ -557,7 +549,7 @@
     kv_push(0, 2).wait_send()
     kv_push(0, 1).wait_send()
     kv_push(2, 1).wait_send()
-    for copy in (query_back, kv_back, mixed_back, total_back, proj_back, out_back):
+    for copy in (query_back, kv_back, mixed_back, proj_back, out_back):
         copy.wait()
 
 
@@ -574,7 +566,7 @@
         ((rows, model), low, vmem),
         ((HEADS, rows, HD), low, anywhere),
         ((ctx_size, rows, 2 * kv_width), low, anywhere),
-        ((HEADS, rows, HD), full, anywhere),
+        ((rows, HD), full, vmem),
         ((rows, q_width), low, anywhere),
         ((rows, model), full, vmem),
         ((rows, model), low, vmem),
@@ -597,7 +589,6 @@
             pltpu.VMEM((HEADS, rows, HD), low),
             pltpu.VMEM((ctx_size, rows, 2 * kv_width), low),
             pltpu.VMEM((rows, q_width), low),
-            pltpu.VMEM((HEADS, rows, HD), full),
             sem((26,)), sem((2,)), sem((2, 32)), sem((2, 4)), sem((2, 4)), sem((1,)), sem((32,)),
             sem((7,)), sem((8,)), sem((4,)), sem((4,)), sem((6,)),
         ],
@@ -608,8 +599,425 @@
     )(hidden, cosine, sine, pos_q, pos_k, spread, packed, w_out, w_gate, w_up, w_down, grad_out)
 
 
-def permute(value, mask, size):
-    return lax.ppermute(value, ("dp", "ctx"), [(i, i ^ mask) for i in range(size)])
+def back_kernel(
+    ctx_size, grad_two, resid, hidden, grad_out, normed, mixed, query, kv, total, cosine, sine, pos_q, pos_k, small, spread,
+    proj, out_w, grads,
+    hidden_o, query_o, key_o, outw_o, gate_o, up_o, down_o,
+    weight, turned, left_n, left_a, right_b, right_p, side, side_in, g_b, g_q, g_k,
+    y_b, y_q, y_k, x_b, x_q, x_k, p_b, p_q, p_k, h_b, h_q, h_k,
+    own, far, zin, fin, stage, heads_g, lse, dkv, kv_out, kv_p, kv_h, grad_resid,
+    load_sem, xs, xr, zs, zr, fs, fr, cs, cr, rs, rr, ks, kr, st_sem,
+):
+    dp = lax.axis_index("dp")
+    ctx = lax.axis_index("ctx")
+    me = dp * ctx_size + ctx
+    y, x, c = dp // 4, (dp // 2) % 2, dp % 2
+    h, p = ctx // 2, ctx % 2
+    rows, model = resid.shape
+    shard = grads.shape[3]
+    width = grads.shape[4] // 3
+    hidden_units = gate_o.shape[1]
+    kv_width = KV_HEADS * HD
+    q_width = HEADS * HD
+    groups = HEADS // KV_HEADS
+    low, full = jnp.bfloat16, jnp.float32
+    span = ctx_size * shard
+
+    def at(index):
+        return (index // ctx_size, index % ctx_size)
+
+    def remote(src, dst, send, recv, mask):
+        return pltpu.make_async_remote_copy(
+            src_ref=src, dst_ref=dst, send_sem=send, recv_sem=recv, device_id=at(flip(me, mask)), device_id_type=MESH
+        )
+
+    def group_rows(mask):
+        return pl.ds(pl.multiple_of(flip(dp, mask // 4) * span, span), span)
+
+    def mask_of(j):
+        return (j // 4) * 16 + ((j // 2) % 2) * 4 + j % 2
+
+    barrier = pltpu.get_barrier_semaphore()
+    partners = (1, 2, 4, 5, 8, 16, 17, 20, 21)
+    for mask in partners:
+        pl.semaphore_signal(barrier, inc=1, device_id=at(flip(me, mask)), device_id_type=MESH)
+    load_w = pltpu.make_async_copy(out_w, weight.at[:, pl.ds(0, q_width)], load_sem.at[0])
+    load_w.start()
+    load_own = [pltpu.make_async_copy(grads.at[0, 1], own, load_sem.at[1]), pltpu.make_async_copy(grads.at[0, 0], own, load_sem.at[2])]
+    load_own[0].start()
+    pl.semaphore_wait(barrier, len(partners))
+
+    def far_push(half, j):
+        return remote(grads.at[1, half, j], far.at[half, j], xs.at[half, j], xr.at[half, j], 8)
+
+    for j in range(8):
+        far_push(1, j).start()
+
+    def transposed(value, left, n):
+        turned[n] = jnp.transpose(value)
+        for i, mask in enumerate((0, 8, 16, 24)):
+            left[i, :, pl.ds(0, rows)] = turned[n, group_rows(mask)]
+            cross_left(left, n, i, mask).start()
+
+    def cross_left(left, n, i, mask):
+        return remote(turned.at[n, group_rows(mask | 4)], left.at[i, :, pl.ds(rows, rows)], cs.at[n, i], cr.at[n, i], 4)
+
+    def cross(src, dst, n, i):
+        return remote(src, dst, cs.at[n, i], cr.at[n, i], 4)
+
+    transposed(normed[...], left_n, 0)
+    right_b[pl.ds(0, rows)] = mixed[...]
+    cross_mixed = cross(mixed, right_b.at[pl.ds(rows, rows)], 2, 0)
+    cross_mixed.start()
+
+    value = resid[...]
+    factor = lax.rsqrt(jnp.mean(value * value, axis=-1, keepdims=True) + norm_eps)
+    unit = value * factor
+    scaled = grad_two[...] * small[2:3]
+    ffn_row = jnp.sum(grad_two[...] * unit, axis=0, keepdims=True)
+    grad_resid[...] = grad_out[...].astype(full) + factor * (
+        scaled - unit * jnp.mean(scaled * unit, axis=-1, keepdims=True)
+    )
+    grad_attn = grad_resid[...].astype(low)
+    transposed(grad_attn, left_a, 1)
+    lse[...] = jnp.transpose(total[...])
+    load_w.wait()
+    for half in range(2):
+        part = half * (q_width // 2)
+        moved = dot(grad_attn, weight[:, part : part + q_width // 2], ((1,), (0,))).astype(low)
+        for i in range(HEADS // 2):
+            heads_g[half * (HEADS // 2) + i] = moved[:, i * HD : (i + 1) * HD]
+    load_p = pltpu.make_async_copy(proj, weight, load_sem.at[0])
+    load_p.start()
+
+    streams = ((g_b, y_b, x_b, p_b, h_b), (g_q, y_q, x_q, p_q, h_q), (g_k, y_k, x_k, p_k, h_k))
+
+    def add(ref, other):
+        ref[...] = (ref[...].astype(full) + other[...].astype(full)).astype(low)
+
+    def y_push(s, k):
+        g, yy = streams[s][:2]
+        return remote(g.at[2 + k], yy.at[k], rs.at[s, k], rr.at[s, k], 16)
+
+    def x_push(s):
+        g, xx = streams[s][0], streams[s][2]
+        return remote(g.at[1], xx, rs.at[s, 2], rr.at[s, 2], 8)
+
+    def block_of(hr, other):
+        z = 2 * either(h, hr) + either(p, other)
+        return pl.ds(pl.multiple_of(z * shard, shard), shard)
+
+    def p_push(s, hr):
+        g, pp = streams[s][0], streams[s][3]
+        return remote(g.at[0, block_of(hr, 1)], pp.at[hr], rs.at[s, 3 + hr], rr.at[s, 3 + hr], 1)
+
+    def h_push(s):
+        g, hh = streams[s][0], streams[s][4]
+        return remote(g.at[0, block_of(1, 0)], hh, rs.at[s, 5], rr.at[s, 5], 2)
+
+    def y_pass(s):
+        g, yy = streams[s][:2]
+        y_push(s, 1).wait_recv()
+        add(g.at[1], yy.at[1])
+        x_push(s).start()
+        y_push(s, 0).wait_recv()
+        add(g.at[0], yy.at[0])
+
+    def x_pass(s):
+        x_push(s).wait_recv()
+        add(streams[s][0].at[0], streams[s][2])
+        p_push(s, 1).start()
+        p_push(s, 0).start()
+
+    def p_pass(s):
+        g, pp = streams[s][0], streams[s][3]
+        p_push(s, 1).wait_recv()
+        add(g.at[0, block_of(1, 0)], pp.at[1])
+        h_push(s).start()
+        p_push(s, 0).wait_recv()
+        add(g.at[0, block_of(0, 0)], pp.at[0])
+
+    def h_pass(s, out):
+        h_push(s).wait_recv()
+        out[...] = streams[s][0][0, block_of(0, 0)].astype(full) + streams[s][4][...].astype(full)
+
+    for i, mask in enumerate((0, 8, 16, 24)):
+        cross_left(left_a, 1, i, mask).wait_recv()
+    cross_mixed.wait_recv()
+    for i in (3, 2, 1, 0):
+        g_b[i] = dot(left_a[i], right_b[...], ((1,), (0,))).astype(low)
+        if i > 1:
+            y_push(0, i - 2).start()
+
+    def z_push(j):
+        return remote(far.at[1, j], zin.at[j], zs.at[j], zr.at[j], 2)
+
+    def far_step(j):
+        far_push(1, j).wait_recv()
+        far[1, j] = (far[1, j].astype(full) + own[j].astype(full)).astype(low)
+        z_push(j).start()
+
+    load_own[0].wait()
+
+    def head(n, carry):
+        g = n // groups
+        k_cols = pl.ds(pl.multiple_of(g * HD, HD), HD)
+        v_cols = pl.ds(pl.multiple_of(kv_width + g * HD, HD), HD)
+        keys = kv[:, :, k_cols].reshape(ctx_size * rows, HD)
+        vals = kv[:, :, v_cols].reshape(ctx_size * rows, HD)
+        scores = dot(keys, query[n], ((1,), (1,))) * HD ** (-0.5)
+        scores = jnp.where(pos_k[...] <= pos_q[...], scores, masked_fill)
+        attend = jnp.exp(scores - lse[pl.ds(n, 1), :])
+        grad_attend = dot(vals, heads_g[n], ((1,), (1,)))
+        delta = jnp.sum(grad_attend * attend, axis=0, keepdims=True)
+        grad_scores = (attend * (grad_attend - delta)).astype(low)
+        dkv[:, k_cols] += dot(grad_scores, query[n], ((1,), (0,)))
+        dkv[:, v_cols] += dot(attend.astype(low), heads_g[n], ((1,), (0,)))
+        back = dot(grad_scores, keys, ((0,), (0,))) * HD ** (-0.5)
+        back = turn(back, cosine[...], -sine[...]).astype(low)
+        right_p[pl.ds(0, rows), pl.ds(pl.multiple_of(n * HD, HD), HD)] = back
+        return carry
+
+    dkv[...] = jnp.zeros_like(dkv)
+    lax.fori_loop(0, HEADS // 2, head, 0)
+    far_step(0)
+    lax.fori_loop(HEADS // 2, HEADS, head, 0)
+    far_step(1)
+
+    for z in range(ctx_size):
+        part = dkv[pl.ds(z * rows, rows)]
+        kv_out[z, :, pl.ds(0, kv_width)] = (part[:, :kv_width] * HD ** (-0.5)).astype(low)
+        kv_out[z, :, pl.ds(kv_width, kv_width)] = part[:, kv_width:].astype(low)
+
+    def kv_push(hr):
+        return remote(kv_out.at[2 * either(h, hr) + 1 - p], kv_p.at[hr], ks.at[hr], kr.at[hr], 1)
+
+    def kv_cross():
+        return remote(kv_out.at[2 * (1 - h) + p], kv_h, ks.at[2], kr.at[2], 2)
+
+    kv_push(1).start()
+    kv_push(0).start()
+    cross_q = cross(
+        right_p.at[pl.ds(0, rows), pl.ds(0, q_width)], right_p.at[pl.ds(rows, rows), pl.ds(0, q_width)], 2, 1
+    )
+    cross_q.start()
+    y_pass(0)
+    kv_push(1).wait_recv()
+    add(kv_out.at[2 * (1 - h) + p], kv_p.at[1])
+    kv_cross().start()
+    kv_push(0).wait_recv()
+    add(kv_out.at[2 * h + p], kv_p.at[0])
+    far_step(2)
+    for i, mask in enumerate((0, 8, 16, 24)):
+        cross_left(left_n, 0, i, mask).wait_recv()
+    cross_q.wait_recv()
+    for i in (3, 2, 1, 0):
+        g_q[i] = dot(left_n[i], right_p[:, pl.ds(0, q_width)], ((1,), (0,))).astype(low)
+        if i > 1:
+            y_push(1, i - 2).start()
+    load_p.wait()
+    hidden_o[...] = dot(right_p[pl.ds(0, rows), pl.ds(0, q_width)], weight[:, pl.ds(0, q_width)], ((1,), (1,)))
+    far_step(3)
+    far_step(4)
+    kv_cross().wait_recv()
+    final = kv_out[2 * h + p].astype(full) + kv_h[...].astype(full)
+    for g in range(KV_HEADS):
+        right_p[pl.ds(0, rows), pl.ds(q_width + g * HD, HD)] = turn(
+            final[:, g * HD : (g + 1) * HD], cosine[...], -sine[...]
+        ).astype(low)
+    right_p[pl.ds(0, rows), pl.ds(q_width + kv_width, kv_width)] = final[:, kv_width:].astype(low)
+    cross_kv = cross(
+        right_p.at[pl.ds(0, rows), pl.ds(q_width, 2 * kv_width)],
+        right_p.at[pl.ds(rows, rows), pl.ds(q_width, 2 * kv_width)], 2, 2,
+    )
+    cross_kv.start()
+    grad_one = hidden_o[...] + dot(
+        right_p[pl.ds(0, rows), pl.ds(q_width, 2 * kv_width)], weight[:, pl.ds(q_width, 2 * kv_width)], ((1,), (1,))
+    )
+    value = hidden[...].astype(full)
+    factor = lax.rsqrt(jnp.mean(value * value, axis=-1, keepdims=True) + norm_eps)
+    unit = value * factor
+    scaled = grad_one * small[0:1]
+    attn_row = jnp.sum(grad_one * unit, axis=0, keepdims=True)
+    hidden_o[...] = grad_resid[...] + factor * (scaled - unit * jnp.mean(scaled * unit, axis=-1, keepdims=True))
+    bias = jnp.sum(right_p[pl.ds(0, rows)].astype(full), axis=0, keepdims=True)
+    kv_bias = jnp.broadcast_to(bias[:, q_width:], (8, 2 * kv_width)).astype(low)
+    kv_row = dot(kv_bias, spread[...], ((1,), (1,)))[:1]
+    table = jnp.concatenate([attn_row, bias[:, :q_width], ffn_row, kv_row, jnp.zeros((124, model), full)], axis=0)
+    side[...] = jnp.transpose(table).astype(low)
+
+    def cross_side(i, mask):
+        return cross(side.at[group_rows(mask | 4)], side_in.at[i], 3, i)
+
+    for i, mask in enumerate((0, 8, 16, 24)):
+        cross_side(i, mask).start()
+    cross_kv.wait_recv()
+    for i, mask in ((3, 24), (2, 16), (1, 8), (0, 0)):
+        g_k[i, :, pl.ds(0, 2 * kv_width)] = dot(
+            left_n[i], right_p[:, pl.ds(q_width, 2 * kv_width)], ((1,), (0,))
+        ).astype(low)
+        cross_side(i, mask).wait_recv()
+        g_k[i, :, pl.ds(2 * kv_width, HD)] = (
+            side[group_rows(mask)].astype(full) + side_in[i].astype(full)
+        ).astype(low)
+        if i > 1:
+            y_push(2, i - 2).start()
+    x_pass(0)
+    far_step(5)
+    y_pass(1)
+    far_step(6)
+    y_pass(2)
+    far_step(7)
+    p_pass(0)
+    for j in range(8):
+        far_push(0, j).start()
+    load_own[1].start()
+    x_pass(1)
+    x_pass(2)
+    h_pass(0, outw_o)
+    p_pass(1)
+    p_pass(2)
+    load_own[1].wait()
+
+    def fin_push(j):
+        return remote(own.at[j], fin.at[j], fs.at[j], fr.at[j], mask_of(j))
+
+    def total_step(j):
+        far_push(0, j).wait_recv()
+        z_push(j).wait_recv()
+        own[j] = (own[j].astype(full) + far[0, j].astype(full) + zin[j].astype(full)).astype(low)
+
+    outs = (gate_o, up_o, down_o)
+    last = hidden_units - 7 * width
+
+    def store(j, ref):
+        slot = j % 2
+        stage[slot] = ref[...].astype(full)
+        mask = mask_of(j)
+        k = either(y, mask // 16) * 4 + either(p, mask % 2) * 2 + either(c, (mask // 4) % 2)
+
+        @pl.when(k < 7)
+        def _():
+            for n in range(3):
+                pltpu.make_async_copy(
+                    stage.at[slot, :, pl.ds(n * width, width)],
+                    outs[n].at[:, pl.ds(pl.multiple_of(k * width, HD), width)], st_sem.at[slot],
+                ).start()
+            pltpu.make_async_copy(stage.at[slot], stage.at[slot], st_sem.at[slot]).wait()
+
+        @pl.when(k == 7)
+        def _():
+            for n in range(3):
+                pltpu.make_async_copy(
+                    stage.at[slot, :, pl.ds(n * width, last)], outs[n].at[:, pl.ds(7 * width, last)], st_sem.at[slot]
+                ).start()
+            part = stage.at[slot, :, pl.ds(0, 3 * last)]
+            pltpu.make_async_copy(part, part, st_sem.at[slot]).wait()
+
+    total_step(0)
+    store(0, own.at[0])
+    for j in range(1, 8):
+        total_step(j)
+        fin_push(j).start()
+    h_pass(1, query_o)
+    h_pass(2, key_o)
+    for j in range(1, 8):
+        fin_push(j).wait_recv()
+        store(j, fin.at[j])
+
+    for j in range(8):
+        far_push(0, j).wait_send()
+        far_push(1, j).wait_send()
+        z_push(j).wait_send()
+        if j:
+            fin_push(j).wait_send()
+    for i, mask in enumerate((0, 8, 16, 24)):
+        cross_left(left_n, 0, i, mask).wait_send()
+        cross_left(left_a, 1, i, mask).wait_send()
+        cross_side(i, mask).wait_send()
+    for copy in (cross_mixed, cross_q, cross_kv):
+        copy.wait_send()
+    for s in range(3):
+        for k in range(2):
+            y_push(s, k).wait_send()
+            p_push(s, k).wait_send()
+        x_push(s).wait_send()
+        h_push(s).wait_send()
+    kv_push(0).wait_send()
+    kv_push(1).wait_send()
+    kv_cross().wait_send()
+
+
+def back_call(
+    ctx_size, hidden_units, grad_two, resid, hidden, grad_out, normed, mixed, query, kv, total, cosine, sine, pos_q, pos_k,
+    small, spread, proj, out_w, grads,
+):
+    rows, model = resid.shape
+    shard, wide = grads.shape[3:]
+    kv_width = KV_HEADS * HD
+    q_width = HEADS * HD
+    k_cols = 2 * kv_width + HD
+    span = ctx_size * shard
+    low, full = jnp.bfloat16, jnp.float32
+    vmem = pl.BlockSpec(memory_space=pltpu.VMEM)
+    anywhere = pl.BlockSpec(memory_space=pl.ANY)
+    shapes = (
+        ((rows, model), vmem),
+        ((shard, q_width), vmem),
+        ((shard, k_cols), vmem),
+        ((shard, q_width), vmem),
+        ((shard, hidden_units), anywhere),
+        ((shard, hidden_units), anywhere),
+        ((shard, hidden_units), anywhere),
+    )
+    sem = pltpu.SemaphoreType.DMA
+    cols = (q_width, q_width, k_cols)
+
+    def each(*lead):
+        return [pltpu.VMEM(lead + (n,), low) for n in cols]
+
+    return pl.pallas_call(
+        functools.partial(back_kernel, ctx_size),
+        out_shape=tuple(jax.ShapeDtypeStruct(shape, full) for shape, _ in shapes),
+        in_specs=[vmem] * 15 + [anywhere] * 3,
+        out_specs=tuple(spec for _, spec in shapes),
+        scratch_shapes=[
+            pltpu.VMEM(proj.shape, low),
+            pltpu.VMEM((2, model, rows), low),
+            pltpu.VMEM((4, span, 2 * rows), low),
+            pltpu.VMEM((4, span, 2 * rows), low),
+            pltpu.VMEM((2 * rows, q_width), low),
+            pltpu.VMEM((2 * rows, q_width + 2 * kv_width), low),
+            pltpu.VMEM((model, HD), low),
+            pltpu.VMEM((4, span, HD), low),
+            *each(4, span),
+            *each(2, span),
+            *each(span),
+            *each(2, shard),
+            *each(shard),
+            pltpu.VMEM((8, shard, wide), low),
+            pltpu.VMEM((2, 8, shard, wide), low),
+            pltpu.VMEM((8, shard, wide), low),
+            pltpu.VMEM((8, shard, wide), low),
+            pltpu.VMEM((2, shard, wide), full),
+            pltpu.VMEM((HEADS, rows, HD), low),
+            pltpu.VMEM((HD, rows), full),
+            pltpu.VMEM((ctx_size * rows, 2 * kv_width), full),
+            pltpu.VMEM((ctx_size, rows, 2 * kv_width), low),
+            pltpu.VMEM((2, rows, 2 * kv_width), low),
+            pltpu.VMEM((rows, 2 * kv_width), low),
+            pltpu.VMEM((rows, model), full),
+            sem((3,)), sem((2, 8)), sem((2, 8)), sem((8,)), sem((8,)), sem((8,)), sem((8,)),
+            sem((4, 4)), sem((4, 4)), sem((3, 6)), sem((3, 6)), sem((3,)), sem((3,)), sem((2,)),
+        ],
+        compiler_params=pltpu.CompilerParams(
+            collective_id=2, has_side_effects=True, vmem_limit_bytes=63 << 20
+        ),
+        name="back",
+    )(
+        grad_two, resid, hidden, grad_out, normed, mixed, query, kv, total, cosine, sine, pos_q, pos_k, small, spread,
+        proj, out_w, grads,
+    )
 
 
 def fits(mesh):
@@ -635,24 +1043,15 @@
 ):
     ctx_size = lax.axis_size("ctx")
     ctx_rank = lax.axis_index("ctx")
-    size = lax.axis_size("dp") * ctx_size
-    me = lax.axis_index("dp") * ctx_size + ctx_rank
     batches = hidden.shape[0]
     length = hidden.shape[1]
     span_len = length // 2
     seq_len = length * ctx_size
     row_count = batches * length
-    groups = HEADS // KV_HEADS
     shard_rows = w_query.shape[0]
-    head_scale = HD ** (-0.5)
     kv_width = KV_HEADS * HD
     q_width = HEADS * HD
-    both = ("dp", "ctx")
-    piece = -(-w_gate.shape[1] // (8 * 128)) * 128
-    hidden_units = w_gate.shape[1]
-
-    col = 2 * (me // 16) + me % 2
-    core = (me // 4) % 2
+
     grad_out = cotangent.reshape(row_count, D)
     places = jnp.arange(seq_len, dtype=jnp.int32)
     every_pos = jnp.repeat(span_order, span_len, axis=1) * span_len + places[None, :] % span_len
@@ -660,7 +1059,6 @@
     cosine, sine = angles_for(local_pos.reshape(row_count), HD)
     cos_full = jnp.concatenate([cosine[:, 0], cosine[:, 0]], axis=1)
     sin_full = jnp.concatenate([-sine[:, 0], sine[:, 0]], axis=1)
-    allowed = every_pos.reshape(1, seq_len) <= local_pos.reshape(length, 1)
 
     gains = jnp.stack([attn_gain, b_query, ffn_gain], axis=1)
     per = b_key.shape[0]
@@ -668,7 +1066,6 @@
     packed = jnp.concatenate(
         [w_query, w_key, w_value, gains, pair[:, None], jnp.zeros((shard_rows, 124), jnp.bfloat16)], axis=1
     )
-    proj_width = q_width + 2 * kv_width
     unit = jnp.arange(2 * kv_width)
     unit = unit % kv_width // per * shard_rows + unit // kv_width * per + unit % per
     spread = (jnp.arange(D)[:, None] == unit[None, :]).astype(jnp.bfloat16)
@@ -677,117 +1074,27 @@
         ctx_size, source, cos_full, sin_full, local_pos.reshape(length, 1), every_pos.reshape(1, seq_len), spread,
         packed, w_out, w_gate, w_up, w_down, grad_out,
     )
-    source = source.astype(jnp.float32)
-    gain_one, gain_two = small[0], small[2]
-    attn_factor = lax.rsqrt(jnp.mean(source * source, axis=-1, keepdims=True) + norm_eps)
-    ffn_factor = lax.rsqrt(jnp.mean(resid * resid, axis=-1, keepdims=True) + norm_eps)
-    proj_full = proj_full[:, :proj_width]
-    query_heads = query_heads.reshape(KV_HEADS, groups, length, HD)
-    log_total = log_total[:, :, :1].reshape(KV_HEADS, groups, length, 1)
-    key_value = key_value.reshape(seq_len, 2, KV_HEADS, HD)
-    key_all, value_all = key_value[:, 0], key_value[:, 1]
-
-    tiles, gu_grad, d_grad = ffn_call(ctx_size, shard_rows, normed_two, go_all, big)
+    tiles, grads = ffn_call(ctx_size, shard_rows, normed_two, go_all, big)
     sums = jnp.sum(tiles.astype(jnp.float32), axis=0)
-    grad_norm_two = sums[0]
     result = (resid + sums[1]).astype(jnp.bfloat16).reshape(batches, length, D)
-
-    def fold(part):
-        high = permute(part[1, 1], 8, size)
-        low_part = permute(part[1, 0], 8, size)
-        far = (part[0, 1].astype(jnp.float32) + high.astype(jnp.float32)).astype(jnp.bfloat16)
-        far = permute(far, 2, size)
-        near = part[0, 0].astype(jnp.float32) + low_part.astype(jnp.float32)
-        return (near + far.astype(jnp.float32)).astype(jnp.bfloat16)
-
-    d_sum = fold(d_grad)
-    gu_sum = fold(gu_grad)
-    whole_grad = jnp.concatenate([gu_sum, d_sum[:, None]], axis=1)
-    whole_grad = whole_grad.reshape(2, 2, 2, 3, shard_rows, piece)
-    parts = []
-    for mask in (0, 1, 16, 17):
-        part = whole_grad[mask // 16, :, mask % 2]
-        parts.append(permute(part, mask, size) if mask else part)
-    parts = jnp.stack(parts)
-    theirs = permute(parts[:, 1], 4, size)
-    ordered = jnp.stack([parts[:, 0], theirs], axis=0)
-    ordered = ordered[jnp.bitwise_xor(jnp.arange(2), core)]
-    ordered = ordered[:, jnp.bitwise_xor(jnp.arange(4), col)]
-    flat = ordered.transpose(2, 3, 1, 0, 4).reshape(3, shard_rows, 8 * piece)[:, :, :hidden_units]
-    flat = flat.astype(jnp.float32)
-    w_gate_grad, w_up_grad, w_down_grad = flat[0], flat[1], flat[2]
-
-    grad_plain = grad_out.astype(jnp.float32)
-    resid_back, ffn_gain_part = norm_backward(resid, ffn_factor, gain_two, grad_norm_two)
-    grad_resid = grad_plain + resid_back
-    grad_attn = grad_resid.astype(jnp.bfloat16)
-    grad_mixed = plain_dot(grad_attn, out_full).astype(jnp.bfloat16)
-    grad_mixed = grad_mixed.reshape(length, KV_HEADS, groups, HD).transpose(1, 2, 0, 3)
-    scores = (
-        jnp.einsum("kgqd,skd->kgqs", query_heads, key_all, preferred_element_type=jnp.float32) * head_scale
-    )
-    masked = jnp.where(allowed, scores, masked_fill)
-    attend_full = jnp.exp(masked - log_total)
-    attend = attend_full.astype(jnp.bfloat16)
-    grad_attend = jnp.einsum("kgqd,skd->kgqs", grad_mixed, value_all, preferred_element_type=jnp.float32)
-    value_grad_all = jnp.einsum("kgqs,kgqd->skd", attend, grad_mixed, preferred_element_type=jnp.float32)
-    delta = jnp.sum(grad_attend * attend_full, axis=-1, keepdims=True)
-    grad_scores = (attend_full * (grad_attend - delta)).astype(jnp.bfloat16)
-    query_grad_rot = (
-        jnp.einsum("kgqs,skd->qkgd", grad_scores, key_all, preferred_element_type=jnp.float32) * head_scale
-    )
-    key_grad_all = (
-        jnp.einsum("kgqs,kgqd->skd", grad_scores, query_heads, preferred_element_type=jnp.float32) * head_scale
-    )
-    kv_grad = jnp.concatenate(
-        [key_grad_all.reshape(batches, seq_len, kv_width), value_grad_all.reshape(batches, seq_len, kv_width)],
-        axis=2,
-    ).astype(jnp.bfloat16)
-    kv_grad = lax.psum_scatter(kv_grad, "ctx", scatter_dimension=1, tiled=True).astype(jnp.float32)
-    key_grad_rot, value_grad = kv_grad[:, :, :kv_width], kv_grad[:, :, kv_width:]
-    query_grad = (
-        rotate_back(query_grad_rot.reshape(row_count, HEADS, HD), cosine, sine)
-        .reshape(row_count, q_width)
-        .astype(jnp.bfloat16)
-    )
-    key_grad = (
-        rotate_back(key_grad_rot.reshape(row_count, KV_HEADS, HD), cosine, sine)
-        .reshape(row_count, kv_width)
-        .astype(jnp.bfloat16)
-    )
-    value_grad = value_grad.reshape(row_count, kv_width).astype(jnp.bfloat16)
-    proj_grad = jnp.concatenate([query_grad, key_grad, value_grad], axis=1)
-    grad_norm_one = right_dot(proj_grad, proj_full)
-    source_back, attn_gain_part = norm_backward(source, attn_factor, gain_one, grad_norm_one)
-    hidden_grad = (grad_resid + source_back).reshape(batches, length, D)
-
-    bias_part = jnp.sum(proj_grad.astype(jnp.float32), axis=0)
-    kv_bias = bias_part[q_width:].reshape(2, size, per).transpose(1, 0, 2).reshape(size, 2 * per)
-    kv_bias = jnp.pad(kv_bias, ((0, 0), (0, shard_rows - 2 * per))).reshape(-1)
-    columns = jnp.stack([attn_gain_part, bias_part[:q_width], ffn_gain_part, kv_bias], axis=1)
-    part = jnp.concatenate(
-        [outer_add(normed, proj_grad), columns, jnp.zeros((D, 124), jnp.float32)], axis=1
-    ).astype(jnp.bfloat16)
-    proj_sum = lax.psum_scatter(part, both, scatter_dimension=0, tiled=True).astype(jnp.float32)
-    w_out_grad = lax.psum_scatter(
-        outer_add(grad_attn, mixed).astype(jnp.bfloat16), both, scatter_dimension=0, tiled=True
-    ).astype(jnp.float32)
-    w_query_grad = proj_sum[:, :q_width]
-    w_key_grad = proj_sum[:, q_width : q_width + kv_width]
-    w_value_grad = proj_sum[:, q_width + kv_width : proj_width]
-    small = proj_sum[:, proj_width : proj_width + 4]
+    hidden_grad, w_query_grad, kv_sum, w_out_grad, w_gate_grad, w_up_grad, w_down_grad = back_call(
+        ctx_size, w_gate.shape[1], sums[0], resid, source, grad_out, normed, mixed, query_heads, key_value, log_total,
+        cos_full, sin_full, local_pos.reshape(1, length), every_pos.reshape(seq_len, 1), small, spread,
+        proj_full, out_full, grads,
+    )
+    sides = kv_sum[:, 2 * kv_width : 2 * kv_width + 4]
     return (
         result,
-        hidden_grad,
-        small[:, 0],
+        hidden_grad.reshape(batches, length, D),
+        sides[:, 0],
         w_query_grad,
-        small[:, 1],
-        w_key_grad,
-        small[:per, 3],
-        w_value_grad,
-        small[per : 2 * per, 3],
+        sides[:, 1],
+        kv_sum[:, :kv_width],
+        sides[:per, 3],
+        kv_sum[:, kv_width : 2 * kv_width],
+        sides[per : 2 * per, 3],
         w_out_grad,
-        small[:, 2],
+        sides[:, 2],
         w_gate_grad,
         w_up_grad,
         w_down_grad,

time: 740 us -> 585 us (0.79)
  waiting for transfers between devices: 223 us -> 0 us
  Pallas kernels: 342 us -> 547 us
  local copies, waits for them, and re-layouts: 59.7 us -> 17.8 us
  matrix products: 34 us -> 0 us
  other arithmetic: 41.1 us -> 12.1 us
  starting transfers between devices: 18.3 us -> 0 us
  between operations: 14.5 us -> 1.29 us
    pallas_call x0 -> x1, Pallas kernels: none -> 193 us  [back_call(): pl.pallas_call(functools.partial(back_kernel, ctx_size), out_shape=tuple(...]
    ppermute x10 -> x0, waiting for transfers between devices: 147 us -> none  [permute(): lax.ppermute(value, ('dp', 'ctx'), [(i, i ^ mask) for i in range(size)])]
    reduce_scatter x3 -> x0, waiting for transfers between devices: 76.4 us -> none  [the longest x1 76.4 us: fast_device(): lax.psum_scatter(part, both, scatter_dimension=0, tiled=True)]
    dot_general x9 -> x0, matrix products: 34 us -> none  [the longest x2 8.16 us: outer_add(): jnp.einsum('rc,rf->cf', left, right, preferred_element_type=jnp.float32)]
    convert_element_type x8 -> x0, other arithmetic: 21.2 us -> none  [the longest x1 6.75 us: fast_device(): grad_scores = (attend_full * (grad_attend - delta)).astype(jnp.bfloat16)]
    pallas_call x1, Pallas kernels: 121 us -> 141 us  [ffn_call(): pl.pallas_call(functools.partial(ffn_kernel, ctx_size), out_shape=(jax.Sh...]
    ppermute x10 -> x0, starting transfers between devices: 18 us -> none  [permute(): lax.ppermute(value, ('dp', 'ctx'), [(i, i ^ mask) for i in range(size)])]
    concatenate x1 -> x0, local copies, waits for them, and re-layouts: 11.4 us -> none  [fast_device(): jnp.concatenate([outer_add(normed, proj_grad), columns, jnp.zeros((D, 124...]
  transfers between devices with their start and end apart: 13 -> 0, of which waited for: 8 -> 0; matrix products, arithmetic and copies ran while one was open for 11% -> 0% of each run, Pallas kernels for 0% -> 0%
where the time goes in v3:
time: 585 us; the launch traced here: 579 us
  Pallas kernels  547 us (94%)
  local copies, waits for them, and re-layouts  17.8 us (3%)
  other arithmetic  12.1 us (2%)
    pallas_call x1, Pallas kernels, front_call(): pl.pallas_call(functools.partial(front_kernel, ctx_size), out_shape=tuple...  214 us
    pallas_call x1, Pallas kernels, back_call(): pl.pallas_call(functools.partial(back_kernel, ctx_size), out_shape=tuple(...  193 us
    pallas_call x1, Pallas kernels, ffn_call(): pl.pallas_call(functools.partial(ffn_kernel, ctx_size), out_shape=(jax.Sh...  141 us

profile of v3, /device:TPU:0, one launch (start us, length us, event | category | flops | bytes accessed | tf_op | source)
XLA Modules:
  0.0 578.6 jit_solution(336898872982866773)
XLA Ops:
  0.6 0.0 copy-start.16
  0.7 0.0 copy-start.15
  0.7 0.0 copy-start.12
  0.7 0.0 copy-start.13
  0.7 0.0 copy-start.14
  0.7 0.0 copy-start.7
  0.7 0.0 copy-start.8
  0.7 0.0 copy-start.9
  0.7 0.7 multiply_bitcast_fusion
  1.5 0.1 broadcast_in_dim.6
  1.6 0.0 copy-start.11
  1.6 0.5 fusion.8
  2.2 0.8 pad_maximum_fusion
  3.0 0.8 copy.37.pos_q
  3.8 1.9 fusion.spread
  5.7 0.0 copy-done.16
  5.7 0.0 copy-done.15
  5.7 0.1 fusion.29
  5.7 0.1 copy.36
  5.8 0.0 copy-done.12
  5.8 0.1 copy.33
  6.0 0.0 copy-done.13
  6.0 0.1 copy.34
  6.1 0.0 copy-done.14
  6.1 0.1 copy.35
  6.2 0.8 concatenate.15.packed
  7.0 213.5 %front.1 = (bf16[256,1536]{1,0:T(8,128)(2,1)}, bf16[12,256,128]{2,1,0:T(8,128)(2,1)}, bf16[4,256,512]{2,1,0:T(8,128)(2,1)}, f32[256,128]{1,0:T(8,128)}, bf16[256...) custom-call(bf16[256,1536]{1,0:T(8,128)(2,1)} %bitcast.26, ...), custom_call_target="tpu_custom_call" | custom-call | tf_op jit(solution)/shard_map/front/pallas_call | solution.py:580
  220.5 141.2 %ffn.1 = (bf16[4,2,256,1536]{3,2,1,0:T(8,128)(2,1)}, bf16[2,2,8,48,3456]{4,3,2,1,0:T(8,128)(2,1)}) custom-call(bf16[256,1536]{1,0:T(8,128)(2,1)} %get-tuple-element.36.n_own, bf16[8,256,1536]{2,1,0:T(8,128)(2,1)} %get-tuple-element.37.go_all, bf16[1536,3456]{1,0:T(8,128)(2,1)} %get-tuple-element.38.big), custom_call_target="tpu_custom_call" | custom-call | tf_op jit(solution)/shard_map/ffn/pallas_call | solution.py:265
  361.7 4.1 convert_reduce_fusion
  365.8 1.8 copy-done
  367.6 1.2 slice_bitcast_fusion.grad_two
  368.8 0.2 copy.38
  369.1 0.9 fusion.4.pos_k
  369.9 192.7 %back.1 = (f32[256,1536]{1,0:T(8,128)}, f32[48,1536]{1,0:T(8,128)}, f32[48,640]{1,0:T(8,128)}, f32[48,1536]{1,0:T(8,128)}, f32[48,8960]{1,0:T(8,128)}, /*index=5*/f32[48,8960]{1,0:T(8,128)}, f32[48,8960]{1,0:T(8,128)}) custom-call(f32[256,1536]{1,0:T(8,128)} %slice_bitcast_fusion.grad_two, f32[256,1536]{1,0:T(8,128)} %get-tuple-element.35.resid, ...), custom_call_target="tpu_custom_call" | custom-call | tf_op jit(solution)/shard_map/back/pallas_call | solution.py:979
  562.7 1.5 fusion.31
  564.1 1.6 slice_reduce_fusion
  565.7 1.4 slice_reduce_fusion.3
  567.1 3.1 fusion.3
  570.2 0.0 copy-done.4
  570.2 1.1 copy.45
  571.4 0.7 copy.46
  572.1 0.7 copy.47
  572.8 0.0 copy-done.3
  572.8 1.2 copy.48
  574.0 0.9 copy-done.2
  574.9 1.2 copy.49
  576.1 0.9 copy-done.1
  577.0 1.2 copy.50
  (20 shorter events, 0.1 us)
Async XLA Ops:
  0.6 5.0 copy-start.16
  0.7 5.0 copy-start.15
  0.7 5.2 copy-start.12
  0.7 5.3 copy-start.13
  0.7 5.4 copy-start.14
  0.7 5.5 copy-start.7
  0.7 5.5 copy-start.8
  0.7 5.5 copy-start.9
  1.6 5.4 copy-start.10
  1.6 218.9 %copy-start.11 = (s32[1,256]{1,0:T(1,128)}, s32[1,256]{1,0:T(1,128)S(1)}, u32[]{:S(2)}) copy-start(s32[1,256]{1,0:T(1,128)S(1)} %get-tuple-element.62.pos_q) | copy-start | bytes 3076
  365.8 1.8 copy-start
  567.1 3.1 copy-start.4
  570.2 1.2 copy-start.6
  570.2 1.9 copy-start.5
  570.2 2.6 copy-start.3
  572.8 2.1 copy-start.2
  574.9 2.1 copy-start.1

commit v4 on v3

--- a/solution.py
+++ b/solution.py
@@ -94,210 +94,325 @@
     return lax.dot_general(a, b, (dims, ((), ())), preferred_element_type=jnp.float32)
 
 
+def widths(hidden_units):
+    width = -(-hidden_units // (8 * 128)) * 128
+    first = width // 384 * 256
+    return (first, width - first)
+
+
 def ffn_kernel(
-    ctx_size, n_own, go_all, big,
-    hr, grads,
-    wgu, wd, nt, go, ggu, act, csend, crecv, hpart, stage,
-    w_sem, io_sem, n_send, n_recv, f_send, f_recv, c_send, c_recv, o_send, o_recv, st_sem,
+    ctx_size, n_own, go_all, big, big_two,
+    grad_two, r_part, grads, grads_two, near, zin,
+    w_one, w_two, nt, go, ggu, act, crecv, part, h_in, h_mid, stage, own, far,
+    io_sem, n_send, n_recv, f_send, f_recv, c_send, c_recv, o_send, o_recv, st_sem, w_send, w_recv, l_sem, x_send, x_recv, z_send, z_recv, d_sem,
 ):
     dp = lax.axis_index("dp")
     ctx = lax.axis_index("ctx")
     me = dp * ctx_size + ctx
     y, x, c = dp // 4, (dp // 2) % 2, dp % 2
     h, p = ctx // 2, ctx % 2
-    width = wd.shape[1]
+    one, two = w_one.shape[1] // 3, w_two.shape[1] // 3
     shard = grads.shape[3]
     rows, model = n_own.shape
+    low, full = jnp.bfloat16, jnp.float32
 
     def at(index):
         return (index // ctx_size, index % ctx_size)
 
-    core = at(flip(me, 4))
-
-    def partner(o):
-        return (dp + (o // 2) * 4 * (1 - 2 * y), ctx + (o % 2) * (1 - 2 * p))
+    def remote(src, dst, send, recv, mask):
+        return pltpu.make_async_remote_copy(
+            src_ref=src, dst_ref=dst, send_sem=send, recv_sem=recv, device_id=at(flip(me, mask)), device_id_type=MESH
+        )
+
+    def block(mask):
+        return pl.ds(pl.multiple_of(flip(me, mask) * shard, shard), shard)
 
     barrier = pltpu.get_barrier_semaphore()
-    for device in (core, partner(1), partner(2), partner(3)):
-        pl.semaphore_signal(barrier, inc=1, device_id=device, device_id_type=MESH)
-
+    partners = (1, 2, 4, 8, 16)
+    for mask in partners:
+        pl.semaphore_signal(barrier, inc=1, device_id=at(flip(me, mask)), device_id_type=MESH)
     load_n = pltpu.make_async_copy(n_own, nt.at[0], io_sem.at[0])
-    load_n.start()
-    load_go = pltpu.make_async_copy(go_all, go, io_sem.at[1])
-    load_go.start()
-    load_gu = pltpu.make_async_copy(big.at[:, pl.ds(0, 2 * width)], wgu, w_sem.at[0])
-    load_gu.start()
-    load_d = pltpu.make_async_copy(big.at[:, pl.ds(2 * width, width)], wd, w_sem.at[1])
-    load_d.start()
-
-    pl.semaphore_wait(barrier, 4)
+    load_w = pltpu.make_async_copy(big, w_one, io_sem.at[1])
+    load_go = pltpu.make_async_copy(go_all, go, io_sem.at[2])
+    held = (0, 4, 1, 5, 16, 20, 17, 21)
+    load_l = [
+        pltpu.make_async_copy(big_two.at[block(mask)], w_two.at[block(mask)], l_sem.at[i]) for i, mask in enumerate(held)
+    ]
+    for copy in (load_n, load_w, load_go, *load_l):
+        copy.start()
+    pl.semaphore_wait(barrier, len(partners))
+
+    def spread_two(mask, over):
+        remote(big_two.at[block(mask)], w_two.at[block(mask)], w_send.at[0], w_recv.at[mask | over], over).start()
+
+    def w_wait(mask):
+        remote(w_two.at[block(mask)], w_two.at[block(mask)], w_send.at[0], w_recv.at[mask], 1).wait_recv()
+
+    def w_pass(mask):
+        w_wait(mask)
+        remote(w_two.at[block(mask)], w_two.at[block(mask)], w_send.at[0], w_recv.at[mask | 8], 8).start()
+
+    def n_core(slot):
+        return remote(nt.at[slot], nt.at[slot + 1], f_send.at[slot // 2], f_recv.at[slot // 2], 4)
+
+    def n_push(o):
+        src = nt.at[2] if o == 3 else nt.at[0]
+        return remote(src, nt.at[2 * o], n_send.at[o], n_recv.at[o], (0, 1, 16, 16)[o])
+
     load_n.wait()
-
-    def push_n(slot, dst, device, send, recv):
-        return pltpu.make_async_remote_copy(
-            src_ref=nt.at[slot], dst_ref=nt.at[dst], send_sem=send, recv_sem=recv,
-            device_id=device, device_id_type=MESH,
-        )
-
-    first = [push_n(0, 2 * o, partner(o), n_send.at[o], n_recv.at[o]) for o in (1, 2, 3)]
-    for copy in first:
-        copy.start()
-    push_n(0, 1, core, f_send.at[0], f_recv.at[0]).start()
-    load_gu.wait()
-    load_d.wait()
+    n_push(1).start()
+    n_push(2).start()
+    n_core(0).start()
+    for mask in held:
+        spread_two(mask, 2)
+    for mask in held:
+        spread_two(mask, 8)
+    load_w.wait()
     load_go.wait()
 
-    def tile(slot):
-        gu = dot(nt[slot], wgu[...], ((1,), (0,)))
-        ga = dot(go[slot], wd[...], ((1,), (0,)))
-        gate, up = gu[:, :width], gu[:, width:]
+    def first(slot):
+        gu = dot(nt[slot], w_one[:, : 2 * one], ((1,), (0,)))
+        ga = dot(go[slot], w_one[:, 2 * one :], ((1,), (0,)))
+        finish(slot, gu[:, :one], gu[:, one:], ga, 0, 0)
+
+    def finish(slot, gate, up, ga, at_gu, at_act):
+        size = gate.shape[1]
         sig = 1.0 / (1.0 + jnp.exp(-gate))
         silu = gate * sig
-        act[slot] = (silu * up).astype(jnp.bfloat16)
-        ggu[slot, :, pl.ds(0, width)] = (ga * up * sig * (1.0 + gate * (1.0 - sig))).astype(jnp.bfloat16)
-        ggu[slot, :, pl.ds(width, width)] = (ga * silu).astype(jnp.bfloat16)
-        grad = dot(ggu[slot], wgu[...], ((1,), (1,)))
-        out = dot(act[slot], wd[...], ((1,), (1,)))
-        return (grad.astype(jnp.bfloat16), out.astype(jnp.bfloat16))
-
-    def cross(o):
-        return pltpu.make_async_remote_copy(
-            src_ref=csend, dst_ref=crecv.at[o % 2], send_sem=c_send, recv_sem=c_recv.at[o % 2],
-            device_id=core, device_id_type=MESH,
-        )
-
-    def final(o):
-        return pltpu.make_async_remote_copy(
-            src_ref=hpart.at[o], dst_ref=hr.at[o], send_sem=o_send.at[o], recv_sem=o_recv.at[o],
-            device_id=partner(o), device_id_type=MESH,
-        )
-
-    keep = pltpu.make_async_copy(hpart.at[0], hr.at[0], io_sem.at[0])
-
-    def combine(o):
-        cross(o).wait_recv()
-        total = hpart[o].astype(jnp.float32) + crecv[o % 2].astype(jnp.float32)
-        hpart[o] = total.astype(jnp.bfloat16)
-
-    def step(o, carry):
-        @pl.when(o > 0)
-        def _():
-            push_n(0, 2 * o, partner(o), n_send.at[o], n_recv.at[o]).wait_recv()
-            push_n(2 * o, 2 * o + 1, core, f_send.at[o], f_recv.at[o]).start()
-
-        grad, out = tile(2 * o)
-        hpart[o, 0] = grad
-        hpart[o, 1] = out
-
-        @pl.when(o > 0)
-        def _():
-            combine(o - 1)
-
+        act[slot, :, pl.ds(at_act, size)] = (silu * up).astype(low)
+        ggu[slot, :, pl.ds(at_gu, size)] = (ga * up * sig * (1.0 + gate * (1.0 - sig))).astype(low)
+        ggu[slot, :, pl.ds(at_gu + size, size)] = (ga * silu).astype(low)
+
+    def second(slot):
+        gu = dot(nt[slot], w_two[:, : 2 * two], ((1,), (0,)))
+        ga = dot(go[slot], w_two[:, 2 * two :], ((1,), (0,)))
+        finish(slot, gu[:, :two], gu[:, two:], ga, 2 * one, one)
+        grad = dot(ggu[slot, :, : 2 * one], w_one[:, : 2 * one], ((1,), (1,)))
+        grad = grad + dot(ggu[slot, :, 2 * one :], w_two[:, : 2 * two], ((1,), (1,)))
+        out = dot(act[slot, :, :one], w_one[:, 2 * one :], ((1,), (1,)))
+        out = out + dot(act[slot, :, one:], w_two[:, 2 * two :], ((1,), (1,)))
+        return (grad.astype(low), out.astype(low))
+
+    def early(o, carry):
         @pl.when(o == 1)
         def _():
-            keep.start()
-
-        @pl.when(o > 1)
+            n_push(1).wait_recv()
+            n_push(3).start()
+            n_core(2).start()
+            n_push(2).wait_recv()
+            n_core(4).start()
+
+        @pl.when(o == 3)
         def _():
-            final(o - 1).start()
-
-        push_n(2 * o, 2 * o + 1, core, f_send.at[o], f_recv.at[o]).wait_recv()
-        grad, out = tile(2 * o + 1)
-
-        @pl.when(o > 0)
+            n_push(3).wait_recv()
+            n_core(6).start()
+
+        first(2 * o)
+
+        @pl.when(o == 1)
         def _():
-            cross(o).wait_send()
-
-        csend[0] = grad
-        csend[1] = out
-        cross(o).start()
+            for mask in (2, 6, 3):
+                w_pass(mask)
+
+        @pl.when(o == 2)
+        def _():
+            for mask in (7, 18, 22):
+                w_pass(mask)
+
+        n_core(2 * o).wait_recv()
+        first(2 * o + 1)
         return carry
 
-    lax.fori_loop(0, 4, step, 0)
-    combine(3)
-    final(3).start()
-
-    def stage_wait(slot):
-        pltpu.make_async_copy(stage.at[slot], stage.at[slot], st_sem.at[slot]).wait()
-
-    def weights(q, carry):
+    lax.fori_loop(0, 4, early, 0)
+    for mask in (19, 23):
+        w_pass(mask)
+    def stage_wait(slot, size):
+        part_of = stage.at[slot, :, pl.ds(0, size)]
+        pltpu.make_async_copy(part_of, part_of, st_sem.at[slot]).wait()
+
+    def weights(size, start_gu, start_act, to, q, carry):
         slot = q % 2
 
         @pl.when(q > 1)
         def _():
-            stage_wait(slot)
+            stage_wait(slot, 3 * size)
 
         chunk = 8 * shard
         cols = pl.ds(pl.multiple_of(q * chunk, chunk), chunk)
-        left = nt[:, :, cols].reshape(8 * rows, chunk)
-        for half in range(2):
-            part = pl.ds(half * width, width)
-            right = ggu[:, :, part].reshape(8 * rows, width)
-            stage[slot, :, part] = dot(left, right, ((0,), (0,))).astype(jnp.bfloat16)
-        left = go[:, :, cols].reshape(8 * rows, chunk)
-        right = act[...].reshape(8 * rows, width)
-        stage[slot, :, pl.ds(2 * width, width)] = dot(left, right, ((0,), (0,))).astype(jnp.bfloat16)
+
+        def product(left, right, start, count, at_col):
+            left = left[:, :, cols].reshape(8 * rows, chunk)
+            right = right[:, :, pl.ds(start, count)].reshape(8 * rows, count)
+            stage[slot, :, pl.ds(at_col, count)] = dot(left, right, ((0,), (0,))).astype(low)
+
+        for start in range(0, 2 * size, one):
+            count = min(one, 2 * size - start)
+            product(nt, ggu, start_gu + start, count, start)
+        product(go, act, start_act, size, 2 * size)
         yr, xr = either(q // 2, y), either(q % 2, x)
         for j in range(8):
             cr, hrel, pr = either(j // 4, c), either((j // 2) % 2, h), either(j % 2, p)
-            block = yr * 4 + cr * 2 + pr
-            row = pl.ds(j * shard, shard)
-            pltpu.make_async_copy(stage.at[slot, row], grads.at[xr, hrel, block], st_sem.at[slot]).start()
+            pltpu.make_async_copy(
+                stage.at[slot, pl.ds(j * shard, shard), pl.ds(0, 3 * size)],
+                to.at[xr, hrel, yr * 4 + cr * 2 + pr], st_sem.at[slot],
+            ).start()
         return carry
 
-    lax.fori_loop(0, 4, weights, 0)
-    stage_wait(0)
-    stage_wait(1)
-    keep.wait()
-    cross(3).wait_send()
-    for copy in first:
-        copy.wait_send()
+    def all_weights(size, start_gu, start_act, to):
+        lax.fori_loop(0, 4, functools.partial(weights, size, start_gu, start_act, to), 0)
+        stage_wait(0, 3 * size)
+        stage_wait(1, 3 * size)
+
+    def far_push(j):
+        return remote(grads.at[1, 1, j], far.at[j], x_send.at[j], x_recv.at[j], 8)
+
+    def z_push(j):
+        return remote(far.at[j], zin.at[j], z_send.at[j], z_recv.at[j], 2)
+
+    def load_own(k):
+        return pltpu.make_async_copy(grads.at[0, 1, pl.ds(4 * k, 4)], own, d_sem.at[0])
+
+    keep_near = pltpu.make_async_copy(far, near, d_sem.at[0])
+
+    def far_pass(*blocks):
+        for j in blocks:
+            far_push(j).wait_recv()
+            far[j] = (far[j].astype(full) + own[j % 4].astype(full)).astype(low)
+            if j < 4:
+                z_push(j).start()
+
+    all_weights(one, 0, 0, grads)
+    for j in range(8):
+        far_push(j).start()
+    load_own(0).start()
+
+    for mask in (8, 12, 9, 13, 24, 28, 25, 29, 10, 14, 11, 15, 26, 30, 27, 31):
+        w_wait(mask)
+    for copy in load_l:
+        copy.wait()
+
+    def cross(o):
+        return remote(stage.at[:, pl.ds(0, rows), pl.ds(0, model)], crecv.at[o % 2], c_send, c_recv.at[o % 2], 4)
+
+    def final(o):
+        dst = h_mid if o == 3 else h_in.at[o - 1]
+        return remote(part.at[o, 0], dst, o_send.at[o], o_recv.at[o], (0, 1, 16, 16)[o])
+
+    def keep(o):
+        return pltpu.make_async_copy(part.at[o, 1], r_part.at[o], io_sem.at[o])
+
+    def combine(o):
+        cross(o).wait_recv()
+        part[o] = (part[o].astype(full) + crecv[o % 2].astype(full)).astype(low)
+        keep(o).start()
+
+    def late(n, carry):
+        o = 3 - n
+        grad, out = second(2 * o)
+        part[o, 0] = grad
+        part[o, 1] = out
+
+        @pl.when(n > 0)
+        def _():
+            combine(o + 1)
+
+        @pl.when(n == 1)
+        def _():
+            final(3).start()
+            load_own(0).wait()
+            far_pass(0, 1)
+
+        @pl.when(n == 2)
+        def _():
+            final(2).start()
+            far_pass(2, 3)
+            load_own(1).start()
+
+        @pl.when(n == 3)
+        def _():
+            final(3).wait_recv()
+            part[1, 0] = (part[1, 0].astype(full) + h_mid[...].astype(full)).astype(low)
+            final(1).start()
+            load_own(1).wait()
+            far_pass(4, 5)
+
+        grad, out = second(2 * o + 1)
+
+        @pl.when(n > 0)
+        def _():
+            cross(o).wait_send()
+
+        stage[0, pl.ds(0, rows), pl.ds(0, model)] = grad
+        stage[1, pl.ds(0, rows), pl.ds(0, model)] = out
+        cross(o).start()
+        return carry
+
+    lax.fori_loop(0, 4, late, 0)
+
+    far_pass(6, 7)
+    keep_near.start()
+    cross(0).wait_send()
+    all_weights(two, 2 * one, one, grads_two)
+    combine(0)
+    grad_two[...] = part[0, 0].astype(full)
+    for o in (1, 2):
+        final(o).wait_recv()
+        grad_two[...] += h_in[o - 1].astype(full)
+    keep_near.wait()
+    for j in range(8):
+        far_push(j).wait_send()
+        if j < 4:
+            z_push(j).wait()
     for o in range(4):
-        push_n(2 * o, 2 * o + 1, core, f_send.at[o], f_recv.at[o]).wait_send()
+        keep(o).wait()
+        n_core(2 * o).wait_send()
     for o in (1, 2, 3):
-        final(o).wait()
-
-
-def ffn_call(ctx_size, shard, n_own, go_all, big):
+        n_push(o).wait_send()
+        final(o).wait_send()
+    sent = w_two.at[pl.ds(0, 24 * shard)]
+    pltpu.make_async_copy(sent, sent, w_send.at[0]).wait()
+
+
+def ffn_call(ctx_size, shard, n_own, go_all, big, big_two):
     rows, model = n_own.shape
-    width = big.shape[1] // 3
+    one, two = big.shape[1] // 3, big_two.shape[1] // 3
     low = jnp.bfloat16
+    anywhere = pl.BlockSpec(memory_space=pl.ANY)
+    sem = pltpu.SemaphoreType.DMA
     return pl.pallas_call(
         functools.partial(ffn_kernel, ctx_size),
         out_shape=(
-            jax.ShapeDtypeStruct((4, 2, rows, model), low),
-            jax.ShapeDtypeStruct((2, 2, 8, shard, 3 * width), low),
+            jax.ShapeDtypeStruct((rows, model), jnp.float32),
+            jax.ShapeDtypeStruct((4, rows, model), low),
+            jax.ShapeDtypeStruct((2, 2, 8, shard, 3 * one), low),
+            jax.ShapeDtypeStruct((2, 2, 8, shard, 3 * two), low),
+            jax.ShapeDtypeStruct((8, shard, 3 * one), low),
+            jax.ShapeDtypeStruct((4, shard, 3 * one), low),
         ),
-        in_specs=[pl.BlockSpec(memory_space=pl.ANY)] * 3,
-        out_specs=[pl.BlockSpec(memory_space=pl.ANY)] * 2,
+        in_specs=[anywhere] * 4,
+        out_specs=[pl.BlockSpec(memory_space=pltpu.VMEM)] + [anywhere] * 5,
         scratch_shapes=[
-            pltpu.VMEM((model, 2 * width), low),
-            pltpu.VMEM((model, width), low),
+            pltpu.VMEM((model, 3 * one), low),
+            pltpu.VMEM((model, 3 * two), low),
             pltpu.VMEM((8, rows, model), low),
             pltpu.VMEM((8, rows, model), low),
-            pltpu.VMEM((8, rows, 2 * width), low),
-            pltpu.VMEM((8, rows, width), low),
-            pltpu.VMEM((2, rows, model), low),
+            pltpu.VMEM((8, rows, 2 * (one + two)), low),
+            pltpu.VMEM((8, rows, one + two), low),
             pltpu.VMEM((2, 2, rows, model), low),
             pltpu.VMEM((4, 2, rows, model), low),
-            pltpu.VMEM((2, 8 * shard, 3 * width), low),
-            pltpu.SemaphoreType.DMA((2,)),
-            pltpu.SemaphoreType.DMA((2,)),
-            pltpu.SemaphoreType.DMA((4,)),
-            pltpu.SemaphoreType.DMA((4,)),
-            pltpu.SemaphoreType.DMA((4,)),
-            pltpu.SemaphoreType.DMA((4,)),
-            pltpu.SemaphoreType.DMA,
-            pltpu.SemaphoreType.DMA((2,)),
-            pltpu.SemaphoreType.DMA((4,)),
-            pltpu.SemaphoreType.DMA((4,)),
-            pltpu.SemaphoreType.DMA((2,)),
+            pltpu.VMEM((2, rows, model), low),
+            pltpu.VMEM((rows, model), low),
+            pltpu.VMEM((2, 8 * shard, 3 * one), low),
+            pltpu.VMEM((4, shard, 3 * one), low),
+            pltpu.VMEM((8, shard, 3 * one), low),
+            sem((4,)), sem((5,)), sem((5,)), sem((4,)), sem((4,)), sem, sem((2,)), sem((4,)), sem((4,)), sem((2,)),
+            sem((1,)), sem((32,)), sem((8,)), sem((8,)), sem((8,)), sem((4,)), sem((4,)), sem((1,)),
         ],
         compiler_params=pltpu.CompilerParams(
-            collective_id=1, has_side_effects=True, vmem_limit_bytes=63 << 20
+            collective_id=1, has_side_effects=True, vmem_limit_bytes=65200 << 10
         ),
         name="ffn",
-    )(n_own, go_all, big)
+    )(n_own, go_all, big, big_two)
 
 
 def turn(values, cosine, sine):
@@ -306,16 +421,16 @@
 
 def front_kernel(
     ctx_size, hidden, cosine, sine, pos_q, pos_k, spread, packed, w_out, w_gate, w_up, w_down, grad_out,
-    normed_o, query_o, kv_o, total_o, mixed_o, resid_o, normed_two_o, small_o, proj_o, out_o, big, go,
-    proj, out_w, source, query, kv, mixed,
-    load_sem, ag_send, ag_recv, core_send, core_recv, big_send, big_recv, go_send, go_recv, kv_send, kv_recv, back_sem,
+    normed_o, query_o, kv_o, total_o, mixed_o, resid_o, normed_two_o, small_o, proj_o, out_o, big, big_two, go, relay,
+    proj, out_w, source, source_two, query, kv, mixed,
+    load_sem, ag_send, ag_recv, core_send, core_recv, big_send, big_recv, two_recv, relay_recv, go_send, go_recv, kv_send, kv_recv, back_sem,
 ):
     dp = lax.axis_index("dp")
     ctx = lax.axis_index("ctx")
     me = dp * ctx_size + ctx
     shard, wide = packed.shape
     rows, model = hidden.shape
-    width = big.shape[1] // 3
+    one, two = big.shape[1] // 3, big_two.shape[1] // 3
     kv_width = KV_HEADS * HD
     q_width = HEADS * HD
     proj_width = q_width + 2 * kv_width
@@ -337,7 +452,7 @@
         pltpu.make_async_copy(ref, ref, sem).wait()
 
     barrier = pltpu.get_barrier_semaphore()
-    partners = (1, 2, 4, 5, 8, 16, 17, 20, 21)
+    partners = (1, 2, 3, 4, 5, 8, 16, 17, 20, 21)
     for mask in partners:
         pl.semaphore_signal(barrier, inc=1, device_id=at(flip(me, mask)), device_id_type=MESH)
 
@@ -350,11 +465,12 @@
     hidden_units = w_gate.shape[1]
     cuts = []
     for k in range(8):
-        size = min(width, hidden_units - k * width)
         for n, ref in enumerate((w_gate, w_up, w_down)):
-            cuts.append((ref.at[:, pl.ds(k * width, size)], source.at[k, :, pl.ds(n * width, size)]))
-            if size < width:
-                source[k, :, pl.ds(n * width + size, width - size)] = jnp.zeros((shard, width - size), source.dtype)
+            for to, start, width in ((source, k * (one + two), one), (source_two, k * (one + two) + one, two)):
+                size = min(width, hidden_units - start)
+                cuts.append((ref.at[:, pl.ds(start, size)], to.at[k, :, pl.ds(n * width, size)]))
+                if size < width:
+                    to[k, :, pl.ds(n * width + size, width - size)] = jnp.zeros((shard, width - size), to.dtype)
     cuts = [pltpu.make_async_copy(a, b, load_sem.at[2 + i]) for i, (a, b) in enumerate(cuts)]
     for copy in cuts:
         copy.start()
@@ -362,31 +478,34 @@
     for copy in own:
         copy.wait()
 
-    pair = ((proj, 0), (out_w, 1))
-
-    def ag(n, mask, over):
-        ref = pair[n][0]
-        remote(ref.at[block(mask)], ref.at[block(mask)], ag_send.at[n], ag_recv.at[n, mask | over], over).start()
+    q_cols, k_cols = pl.ds(0, q_width), pl.ds(q_width, wide - q_width)
+    streams = ((proj, k_cols), (proj, q_cols), (out_w, q_cols))
+
+    def ag(n, mask, *overs):
+        ref, cols = streams[n]
+        part = ref.at[block(mask), cols]
+        for over in overs:
+            remote(part, part, ag_send.at[n], ag_recv.at[n, mask | over], over).start()
 
     def ag_pass(n, mask, *overs):
-        ref = pair[n][0]
-        remote(ref.at[block(mask)], ref.at[block(mask)], ag_send.at[n], ag_recv.at[n, mask], 1).wait_recv()
-        for over in overs:
-            ag(n, mask, over)
+        ref, cols = streams[n]
+        part = ref.at[block(mask), cols]
+        remote(part, part, ag_send.at[n], ag_recv.at[n, mask], 1).wait_recv()
+        ag(n, mask, *overs)
 
     def group(n, mask):
-        ref = pair[n][0]
-        part = ref.at[block(mask, 4)]
+        ref, cols = streams[n]
+        part = ref.at[block(mask, 4), cols]
         return remote(part, part, core_send.at[n, mask // 8], core_recv.at[n, mask // 8], 4)
 
-    def group_wait(mask, n):
-        ref = pair[n][0]
-        remote(ref.at[block(mask | 4, 4)], ref.at[block(mask | 4, 4)], core_send.at[n, mask // 8], core_recv.at[n, mask // 8], 4).wait_recv()
-
-    for over in (2, 1, 8, 16):
-        ag(0, 0, over)
-    for over in (2, 1, 8):
-        ag(1, 0, over)
+    def group_wait(n):
+        ref, cols = streams[n]
+        for mask in (0, 8, 16, 24):
+            part = ref.at[block(mask | 4, 4), cols]
+            remote(part, part, core_send.at[n, mask // 8], core_recv.at[n, mask // 8], 4).wait_recv()
+
+    ag(0, 0, 2, 1, 8, 16)
+    ag(1, 0, 2, 1, 8, 16)
 
     for copy in cuts:
         copy.wait()
@@ -398,47 +517,81 @@
 
     own_big = pltpu.make_async_copy(source.at[column(0)], big.at[block(0)], load_sem.at[0])
     own_big.start()
+    own_two = pltpu.make_async_copy(source_two.at[column(0)], big_two.at[block(0)], load_sem.at[1])
+    own_two.start()
+
     def cut(mask):
         remote(source.at[column(mask)], big.at[block(0)], big_send.at[0], big_recv.at[mask], mask).start()
 
+    def cut_two(mask):
+        return remote(source_two.at[column(mask)], big_two.at[block(0)], big_send.at[1], two_recv.at[mask], mask)
+
+    held = (0, 4, 1, 5, 16, 20, 17, 21)
+    inner = either(h, p) == 1
+
+    def over_z(mask):
+        src = big.at[block(mask)] if mask else source.at[column(0)]
+
+        @pl.when(inner)
+        def _():
+            remote(src, big.at[block(mask)], big_send.at[0], big_recv.at[mask | 2], 2).start()
+
+        @pl.when(jnp.logical_not(inner))
+        def _():
+            i = held.index(mask)
+            remote(src, relay.at[i], big_send.at[0], relay_recv.at[i], 1).start()
+
+    def relay_pass(*masks):
+        @pl.when(inner)
+        def _():
+            for mask in masks:
+                i = held.index(mask)
+                remote(relay.at[i], relay.at[i], big_send.at[0], relay_recv.at[i], 1).wait_recv()
+                remote(relay.at[i], big.at[block(mask ^ 1)], big_send.at[2], big_recv.at[mask | 2], 3).start()
+
     def big_forward(mask, over):
-        remote(big.at[block(mask)], big.at[block(mask)], big_send.at[0], big_recv.at[mask | over], over).start()
+        if over == 2:
+            over_z(mask)
+        else:
+            remote(big.at[block(mask)], big.at[block(mask)], big_send.at[0], big_recv.at[mask | over], over).start()
 
     def big_pass(mask, *overs):
         remote(big.at[block(mask)], big.at[block(mask)], big_send.at[0], big_recv.at[mask], 1).wait_recv()
         for over in overs:
             big_forward(mask, over)
 
-    for mask in (4, 1, 5):
-        cut(mask)
-    remote(source.at[column(0)], big.at[block(0)], big_send.at[0], big_recv.at[2], 2).start()
+    cut(4)
+    over_z(0)
 
     ag_pass(0, 1, 8, 16)
     ag_pass(0, 8, 16)
     ag_pass(0, 2, 1, 8, 16)
     ag_pass(0, 9, 16)
+    ag_pass(1, 1, 8, 16)
+    ag_pass(1, 8, 16)
     ag_pass(0, 3, 8, 16)
+    ag_pass(0, 10, 16)
+    ag_pass(1, 2, 1, 8, 16)
     group(0, 0).start()
-    big_pass(4, 2)
-    ag_pass(0, 10, 16)
+    remote(source.at[column(0)], big.at[block(0)], big_send.at[0], big_recv.at[8], 8).start()
+    cut(1)
+    cut(5)
+    big_pass(4, 2, 8)
     ag_pass(0, 11, 16)
     group(0, 8).start()
-    for mask in (16, 20, 17, 21):
-        cut(mask)
-    ag_pass(1, 1, 8)
-    ag_pass(1, 2, 1, 8)
-    remote(source.at[column(0)], big.at[block(0)], big_send.at[0], big_recv.at[8], 8).start()
-    big_forward(4, 8)
+    relay_pass(0)
+    ag_pass(1, 9, 16)
+    ag(2, 0, 2, 1, 16, 8)
     for mask in (16, 17, 18, 19):
         ag_pass(0, mask)
     group(0, 16).start()
-    ag_pass(1, 3, 8)
-    big_pass(1, 2, 8)
+    ag_pass(1, 3, 8, 16)
+    group(1, 0).start()
     for mask in (24, 25, 26, 27):
         ag_pass(0, mask)
     group(0, 24).start()
-    for mask in (0, 8, 16, 24):
-        group_wait(mask, 0)
+    relay_pass(4)
+    group_wait(0)
 
     small = jnp.transpose(proj[:, proj_width:].astype(jnp.float32))
     small_o[...] = small[:8]
@@ -459,27 +612,55 @@
 
     kv_push(0, 2).start()
     kv_push(0, 1).start()
+    ag_pass(1, 10, 16)
+    ag_pass(1, 11, 16)
+    group(1, 8).start()
+    big_pass(1, 2, 8)
+    ag_pass(2, 1, 16, 8)
+    ag_pass(2, 2, 1, 16, 8)
+    for mask in (16, 20, 17, 21):
+        cut(mask)
+    kv_push(0, 2).wait_recv()
+    kv_push(2, 1).start()
     big_pass(5, 2, 8)
+    relay_pass(1)
+    for mask in (16, 17, 18, 19):
+        ag_pass(1, mask)
+    group(1, 16).start()
+    ag_pass(2, 3, 16, 8)
+    group(2, 0).start()
+    for mask in (24, 25, 26, 27):
+        ag_pass(1, mask)
+    group(1, 24).start()
     big_pass(16, 2, 8)
-    for mask in (0, 1, 2, 3):
-        ag(1, mask, 16)
-    group(1, 0).start()
-    for mask in (8, 9, 10, 11):
-        ag_pass(1, mask, 16)
-    group(1, 8).start()
+    relay_pass(5)
+    group_wait(1)
     for half in range(2):
         part = half * (q_width // 2)
         raw = dot(normed_o[...], proj[:, part : part + q_width // 2], ((1,), (0,)))
         raw = raw + small[1:2, part : part + q_width // 2]
         for i in range(HEADS // 2):
             query[half * (HEADS // 2) + i] = turn(raw[:, i * HD : (i + 1) * HD], cos, sin).astype(jnp.bfloat16)
-    kv_push(0, 2).wait_recv()
-    kv_push(2, 1).start()
-    for mask in (20, 17, 21):
-        big_pass(mask, 2, 8)
-    for o, mask in ((1, 1), (2, 16), (3, 17)):
-        remote(grad_out, go.at[2 * o], go_send.at[o], go_recv.at[2 * o], mask).start()
-    remote(grad_out, go.at[1], go_send.at[0], go_recv.at[1], 4).start()
+    big_pass(20, 2, 8)
+    relay_pass(16)
+    for mask in (16, 17, 18, 19):
+        ag_pass(2, mask, 8)
+    group(2, 16).start()
+    big_pass(17, 2, 8)
+    big_pass(21, 2, 8)
+    relay_pass(20)
+
+    def go_core(o):
+        src = go.at[2 * o] if o else grad_out
+        return remote(src, go.at[2 * o + 1], go_send.at[3 + o], go_recv.at[2 * o + 1], 4)
+
+    def go_push(o):
+        src = go.at[2] if o == 3 else grad_out
+        return remote(src, go.at[2 * o], go_send.at[o - 1], go_recv.at[2 * o], (0, 1, 16, 16)[o])
+
+    go_push(2).start()
+    go_push(1).start()
+    go_core(0).start()
     for mask in (2, 6):
         big_pass(mask, 8)
     kv_push(0, 1).wait_recv()
@@ -506,18 +687,20 @@
 
     total_o[...] = jnp.zeros_like(total_o)
     lax.fori_loop(0, HEADS, head, 0)
-    own_go = pltpu.make_async_copy(grad_out, go.at[0], load_sem.at[1])
+    own_go = pltpu.make_async_copy(grad_out, go.at[0], load_sem.at[2])
     own_go.start()
     mixed_back = pltpu.make_async_copy(mixed, mixed_o, back_sem.at[2])
     mixed_back.start()
+    relay_pass(17, 21)
     for mask in (3, 7):
         big_pass(mask, 8)
-    for n, mask in enumerate((16, 17, 18, 19, 24, 25, 26, 27)):
-        ag_pass(1, mask)
+    for mask in (4, 1, 5, 16, 20, 17, 21):
+        cut_two(mask).start()
+    for n, mask in enumerate((8, 9, 10, 11, 24, 25, 26, 27)):
+        ag_pass(2, mask)
         if n % 4 == 3:
-            group(1, mask & 24).start()
-    for mask in (0, 8, 16, 24):
-        group_wait(mask, 1)
+            group(2, mask & 24).start()
+    group_wait(2)
     proj_back = pltpu.make_async_copy(proj, proj_o, back_sem.at[4])
     proj_back.start()
     out_back = pltpu.make_async_copy(out_w, out_o, back_sem.at[5])
@@ -526,26 +709,39 @@
     resid_o[...] = resid
     factor = lax.rsqrt(jnp.mean(resid * resid, axis=-1, keepdims=True) + norm_eps)
     normed_two_o[...] = (resid * factor * small_o[2:3]).astype(jnp.bfloat16)
-    for o, mask in ((1, 1), (2, 16), (3, 17)):
-        remote(grad_out, go.at[2 * o], go_send.at[o], go_recv.at[2 * o], mask).wait_recv()
-        remote(go.at[2 * o], go.at[2 * o + 1], go_send.at[3 + o], go_recv.at[2 * o + 1], 4).start()
+    go_push(1).wait_recv()
+    go_push(3).start()
+    go_core(1).start()
+    go_push(2).wait_recv()
+    go_core(2).start()
     for mask in (18, 22, 19, 23):
         big_pass(mask, 8)
 
     for mask in (8, 12, 9, 24, 13, 28, 25, 29, 10, 14, 11, 26, 15, 30, 27, 31):
         big_pass(mask)
+    go_push(3).wait_recv()
+    go_core(3).start()
+    for mask in (4, 1, 5, 16, 20, 17, 21):
+        cut_two(mask).wait_recv()
     own_big.wait()
+    own_two.wait()
     own_go.wait()
-    sent = 7 + 8 + 8 + 8
-    drain(big.at[pl.ds(0, sent * shard)], big_send.at[0])
-    for ref, n in pair:
-        drain(ref.at[pl.ds(0, 15 * shard)], ag_send.at[n])
+    drain(big.at[pl.ds(0, 31 * shard)], big_send.at[0])
+    drain(big_two.at[pl.ds(0, 7 * shard)], big_send.at[1])
+
+    @pl.when(inner)
+    def _():
+        drain(relay, big_send.at[2])
+
+    for n in range(3):
+        ref, cols = streams[n]
+        drain(ref.at[pl.ds(0, 15 * shard), cols], ag_send.at[n])
         for mask in (0, 8, 16, 24):
             group(n, mask).wait_send()
-    remote(grad_out, go.at[1], go_send.at[0], go_recv.at[1], 4).wait()
-    for o, mask in ((1, 1), (2, 16), (3, 17)):
-        remote(grad_out, go.at[2 * o], go_send.at[o], go_recv.at[2 * o], mask).wait_send()
-        remote(go.at[2 * o], go.at[2 * o + 1], go_send.at[3 + o], go_recv.at[2 * o + 1], 4).wait()
+    for o in range(4):
+        go_core(o).wait()
+    for o in (1, 2, 3):
+        go_push(o).wait_send()
     kv_push(0, 2).wait_send()
     kv_push(0, 1).wait_send()
     kv_push(2, 1).wait_send()
@@ -558,7 +754,7 @@
     shard, wide = packed.shape
     kv_width = KV_HEADS * HD
     q_width = HEADS * HD
-    width = -(-w_gate.shape[1] // (8 * 128)) * 128
+    one, two = widths(w_gate.shape[1])
     low, full = jnp.bfloat16, jnp.float32
     vmem = pl.BlockSpec(memory_space=pltpu.VMEM)
     anywhere = pl.BlockSpec(memory_space=pl.ANY)
@@ -573,8 +769,10 @@
         ((8, model), full, vmem),
         ((model, wide), low, anywhere),
         ((model, q_width), low, anywhere),
-        ((model, 3 * width), low, anywhere),
+        ((model, 3 * one), low, anywhere),
+        ((model, 3 * two), low, anywhere),
         ((8, rows, model), low, anywhere),
+        ((8, shard, 3 * one), low, anywhere),
     )
     sem = pltpu.SemaphoreType.DMA
     return pl.pallas_call(
@@ -585,11 +783,12 @@
         scratch_shapes=[
             pltpu.VMEM((model, wide), low),
             pltpu.VMEM((model, q_width), low),
-            pltpu.VMEM((8, shard, 3 * width), low),
+            pltpu.VMEM((8, shard, 3 * one), low),
+            pltpu.VMEM((8, shard, 3 * two), low),
             pltpu.VMEM((HEADS, rows, HD), low),
             pltpu.VMEM((ctx_size, rows, 2 * kv_width), low),
             pltpu.VMEM((rows, q_width), low),
-            sem((26,)), sem((2,)), sem((2, 32)), sem((2, 4)), sem((2, 4)), sem((1,)), sem((32,)),
+            sem((50,)), sem((3,)), sem((3, 32)), sem((3, 4)), sem((3, 4)), sem((3,)), sem((32,)), sem((32,)), sem((8,)),
             sem((7,)), sem((8,)), sem((4,)), sem((4,)), sem((6,)),
         ],
         compiler_params=pltpu.CompilerParams(
@@ -601,12 +800,12 @@
 
 def back_kernel(
     ctx_size, grad_two, resid, hidden, grad_out, normed, mixed, query, kv, total, cosine, sine, pos_q, pos_k, small, spread,
-    proj, out_w, grads,
-    hidden_o, query_o, key_o, outw_o, gate_o, up_o, down_o,
+    proj, out_w, grads, grads_two, near, zin_first, r_part,
+    result_o, hidden_o, query_o, key_o, outw_o, gate_o, up_o, down_o, r_in,
     weight, turned, left_n, left_a, right_b, right_p, side, side_in, g_b, g_q, g_k,
     y_b, y_q, y_k, x_b, x_q, x_k, p_b, p_q, p_k, h_b, h_q, h_k,
-    own, far, zin, fin, stage, heads_g, lse, dkv, kv_out, kv_p, kv_h, grad_resid,
-    load_sem, xs, xr, zs, zr, fs, fr, cs, cr, rs, rr, ks, kr, st_sem,
+    own, far, zin, fin, own_two, far_two, zin_two, fin_two, r_mid, r_one, stage, heads_g, lse, dkv, kv_out, kv_p, kv_h, grad_resid,
+    load_sem, xs, xr, zs, zr, fs, fr, xs2, xr2, zs2, zr2, fs2, fr2, cs, cr, rs, rr, ks, kr, st_sem, os, orr,
 ):
     dp = lax.axis_index("dp")
     ctx = lax.axis_index("ctx")
@@ -615,8 +814,8 @@
     h, p = ctx // 2, ctx % 2
     rows, model = resid.shape
     shard = grads.shape[3]
-    width = grads.shape[4] // 3
     hidden_units = gate_o.shape[1]
+    one, two = widths(hidden_units)
     kv_width = KV_HEADS * HD
     q_width = HEADS * HD
     groups = HEADS // KV_HEADS
@@ -643,15 +842,66 @@
         pl.semaphore_signal(barrier, inc=1, device_id=at(flip(me, mask)), device_id_type=MESH)
     load_w = pltpu.make_async_copy(out_w, weight.at[:, pl.ds(0, q_width)], load_sem.at[0])
     load_w.start()
-    load_own = [pltpu.make_async_copy(grads.at[0, 1], own, load_sem.at[1]), pltpu.make_async_copy(grads.at[0, 0], own, load_sem.at[2])]
-    load_own[0].start()
+    load_own = [
+        pltpu.make_async_copy(grads.at[0, 0], own, load_sem.at[1]),
+        pltpu.make_async_copy(grads_two.at[0], own_two, load_sem.at[2]),
+        pltpu.make_async_copy(zin_first, zin.at[pl.ds(0, 4)], load_sem.at[3]),
+        pltpu.make_async_copy(r_part.at[1], r_one, load_sem.at[4]),
+    ]
+    for copy in load_own:
+        copy.start()
     pl.semaphore_wait(barrier, len(partners))
 
-    def far_push(half, j):
-        return remote(grads.at[1, half, j], far.at[half, j], xs.at[half, j], xr.at[half, j], 8)
-
+    def far_push(j):
+        return remote(grads.at[1, 0, j], far.at[j], xs.at[j], xr.at[j], 8)
+
+    def far_two_push(half, j):
+        return remote(grads_two.at[1, half, j], far_two.at[half, j], xs2.at[half, j], xr2.at[half, j], 8)
+
+    def z_push(j):
+        return remote(near.at[j], zin.at[j], zs.at[j], zr.at[j], 2)
+
+    def z_two_push(j):
+        return remote(far_two.at[1, j], zin_two.at[j], zs2.at[j], zr2.at[j], 2)
+
+    def fin_push(j):
+        return remote(own.at[j], fin.at[j], fs.at[j], fr.at[j], mask_of(j))
+
+    def fin_two_push(j):
+        return remote(own_two.at[0, j], fin_two.at[j], fs2.at[j], fr2.at[j], mask_of(j))
+
+    def z_two_step(j):
+        far_two_push(1, j).wait_recv()
+        far_two[1, j] = (far_two[1, j].astype(full) + own_two[1, j].astype(full)).astype(low)
+        z_two_push(j).start()
+
+    def total_step(j):
+        far_push(j).wait_recv()
+        if j > 3:
+            z_push(j).wait_recv()
+        own[j] = (own[j].astype(full) + far[j].astype(full) + zin[j].astype(full)).astype(low)
+        if j:
+            fin_push(j).start()
+
+    def total_two_step(j):
+        far_two_push(0, j).wait_recv()
+        z_two_push(j).wait_recv()
+        own_two[0, j] = (own_two[0, j].astype(full) + far_two[0, j].astype(full) + zin_two[j].astype(full)).astype(low)
+        if j:
+            fin_two_push(j).start()
+
+    def r_push(o):
+        src = r_one if o == 1 else r_part.at[o]
+        dst = r_mid if o == 3 else r_in.at[o - 1]
+        return remote(src, dst, os.at[o], orr.at[o], (0, 1, 16, 16)[o])
+
+    r_push(3).start()
+    for j in range(4, 8):
+        z_push(j).start()
     for j in range(8):
-        far_push(1, j).start()
+        far_two_push(1, j).start()
+    for j in range(8):
+        far_push(j).start()
 
     def transposed(value, left, n):
         turned[n] = jnp.transpose(value)
@@ -746,18 +996,7 @@
     cross_mixed.wait_recv()
     for i in (3, 2, 1, 0):
         g_b[i] = dot(left_a[i], right_b[...], ((1,), (0,))).astype(low)
-        if i > 1:
-            y_push(0, i - 2).start()
-
-    def z_push(j):
-        return remote(far.at[1, j], zin.at[j], zs.at[j], zr.at[j], 2)
-
-    def far_step(j):
-        far_push(1, j).wait_recv()
-        far[1, j] = (far[1, j].astype(full) + own[j].astype(full)).astype(low)
-        z_push(j).start()
-
-    load_own[0].wait()
+    y_push(0, 1).start()
 
     def head(n, carry):
         g = n // groups
@@ -779,10 +1018,7 @@
         return carry
 
     dkv[...] = jnp.zeros_like(dkv)
-    lax.fori_loop(0, HEADS // 2, head, 0)
-    far_step(0)
-    lax.fori_loop(HEADS // 2, HEADS, head, 0)
-    far_step(1)
+    lax.fori_loop(0, HEADS, head, 0)
 
     for z in range(ctx_size):
         part = dkv[pl.ds(z * rows, rows)]
@@ -801,13 +1037,11 @@
         right_p.at[pl.ds(0, rows), pl.ds(0, q_width)], right_p.at[pl.ds(rows, rows), pl.ds(0, q_width)], 2, 1
     )
     cross_q.start()
-    y_pass(0)
-    kv_push(1).wait_recv()
-    add(kv_out.at[2 * (1 - h) + p], kv_p.at[1])
-    kv_cross().start()
-    kv_push(0).wait_recv()
-    add(kv_out.at[2 * h + p], kv_p.at[0])
-    far_step(2)
+    for copy in load_own:
+        copy.wait()
+    r_push(3).wait_recv()
+    add(r_one, r_mid)
+    r_push(1).start()
     for i, mask in enumerate((0, 8, 16, 24)):
         cross_left(left_n, 0, i, mask).wait_recv()
     cross_q.wait_recv()
@@ -815,10 +1049,18 @@
         g_q[i] = dot(left_n[i], right_p[:, pl.ds(0, q_width)], ((1,), (0,))).astype(low)
         if i > 1:
             y_push(1, i - 2).start()
+    y_push(0, 0).start()
     load_p.wait()
     hidden_o[...] = dot(right_p[pl.ds(0, rows), pl.ds(0, q_width)], weight[:, pl.ds(0, q_width)], ((1,), (1,)))
-    far_step(3)
-    far_step(4)
+    kv_push(1).wait_recv()
+    add(kv_out.at[2 * (1 - h) + p], kv_p.at[1])
+    kv_cross().start()
+    kv_push(0).wait_recv()
+    add(kv_out.at[2 * h + p], kv_p.at[0])
+    for j in range(8):
+        z_two_step(j)
+    for j in range(4):
+        total_step(j)
     kv_cross().wait_recv()
     final = kv_out[2 * h + p].astype(full) + kv_h[...].astype(full)
     for g in range(KV_HEADS):
@@ -862,75 +1104,102 @@
         ).astype(low)
         if i > 1:
             y_push(2, i - 2).start()
-    x_pass(0)
-    far_step(5)
+    outs = (gate_o, up_o, down_o)
+    width = one + two
+    last = hidden_units - 7 * width - one
+
+    def piece(j):
+        mask = mask_of(j)
+        return either(y, mask // 16) * 4 + either(p, mask % 2) * 2 + either(c, (mask // 4) % 2)
+
+    def write(j, start, size, count):
+        for n in range(3):
+            pltpu.make_async_copy(
+                stage.at[j % 2, :, pl.ds(n * size, count)],
+                outs[n].at[:, pl.ds(pl.multiple_of(piece(j) * width + start, HD), count)], st_sem.at[j % 2],
+            ).start()
+
+    def settle(slot, count):
+        part = stage.at[slot, :, pl.ds(0, 3 * count)]
+        pltpu.make_async_copy(part, part, st_sem.at[slot]).wait()
+
+    def store(j):
+        if j:
+            fin_push(j).wait_recv()
+        if j > 1:
+            settle(j % 2, one)
+        stage[j % 2] = (fin[j] if j else own[0]).astype(full)
+        write(j, 0, one, one)
+
+    def settle_two(j):
+        pl.when(piece(j) < 7)(lambda: settle(j % 2, two))
+        pl.when(piece(j) == 7)(lambda: settle(j % 2, last))
+
+    def store_two(j):
+        if j:
+            fin_two_push(j).wait_recv()
+        if j > 1:
+            settle_two(j - 2)
+        else:
+            settle(j % 2, one)
+        stage[j % 2, :, pl.ds(0, 3 * two)] = (fin_two[j] if j else own_two[0, 0]).astype(full)
+        pl.when(piece(j) < 7)(lambda: write(j, one, two, two))
+        pl.when(piece(j) == 7)(lambda: write(j, one, two, last))
+
     y_pass(1)
-    far_step(6)
     y_pass(2)
-    far_step(7)
-    p_pass(0)
+    y_pass(0)
     for j in range(8):
-        far_push(0, j).start()
-    load_own[1].start()
+        far_two_push(0, j).start()
+    for j in range(4):
+        store(j)
     x_pass(1)
     x_pass(2)
-    h_pass(0, outw_o)
+    r_push(2).start()
+    for j in range(4, 8):
+        total_step(j)
     p_pass(1)
     p_pass(2)
-    load_own[1].wait()
-
-    def fin_push(j):
-        return remote(own.at[j], fin.at[j], fs.at[j], fr.at[j], mask_of(j))
-
-    def total_step(j):
-        far_push(0, j).wait_recv()
-        z_push(j).wait_recv()
-        own[j] = (own[j].astype(full) + far[0, j].astype(full) + zin[j].astype(full)).astype(low)
-
-    outs = (gate_o, up_o, down_o)
-    last = hidden_units - 7 * width
-
-    def store(j, ref):
-        slot = j % 2
-        stage[slot] = ref[...].astype(full)
-        mask = mask_of(j)
-        k = either(y, mask // 16) * 4 + either(p, mask % 2) * 2 + either(c, (mask // 4) % 2)
-
-        @pl.when(k < 7)
-        def _():
-            for n in range(3):
-                pltpu.make_async_copy(
-                    stage.at[slot, :, pl.ds(n * width, width)],
-                    outs[n].at[:, pl.ds(pl.multiple_of(k * width, HD), width)], st_sem.at[slot],
-                ).start()
-            pltpu.make_async_copy(stage.at[slot], stage.at[slot], st_sem.at[slot]).wait()
-
-        @pl.when(k == 7)
-        def _():
-            for n in range(3):
-                pltpu.make_async_copy(
-                    stage.at[slot, :, pl.ds(n * width, last)], outs[n].at[:, pl.ds(7 * width, last)], st_sem.at[slot]
-                ).start()
-            part = stage.at[slot, :, pl.ds(0, 3 * last)]
-            pltpu.make_async_copy(part, part, st_sem.at[slot]).wait()
-
-    total_step(0)
-    store(0, own.at[0])
-    for j in range(1, 8):
-        total_step(j)
-        fin_push(j).start()
+    x_pass(0)
+    for j in range(4, 8):
+        store(j)
+    for j in range(8):
+        total_two_step(j)
+    p_pass(0)
     h_pass(1, query_o)
     h_pass(2, key_o)
-    for j in range(1, 8):
-        fin_push(j).wait_recv()
-        store(j, fin.at[j])
-
+    h_pass(0, outw_o)
     for j in range(8):
-        far_push(0, j).wait_send()
-        far_push(1, j).wait_send()
-        z_push(j).wait_send()
+        store_two(j)
+    settle_two(6)
+    settle_two(7)
+    for o in (1, 2):
+        r_push(o).wait()
+    r_push(3).wait_send()
+    tiles = (r_part.at[0], r_in.at[0], r_in.at[1])
+    loads = [
+        pltpu.make_async_copy(ref, weight.at[pl.ds(o * rows, rows), pl.ds(0, model)], os.at[o])
+        for o, ref in enumerate(tiles)
+    ]
+    for copy in loads:
+        copy.start()
+    for copy in loads:
+        copy.wait()
+    value = resid[...]
+    for o in range(3):
+        value = value + weight[pl.ds(o * rows, rows), pl.ds(0, model)].astype(full)
+    result_o[...] = value.astype(low)
+
+    for j in range(8):
+        far_push(j).wait_send()
+        far_two_push(0, j).wait_send()
+        far_two_push(1, j).wait_send()
+        if j > 3:
+            z_push(j).wait_send()
+        z_two_push(j).wait_send()
         if j:
             fin_push(j).wait_send()
+            fin_two_push(j).wait_send()
     for i, mask in enumerate((0, 8, 16, 24)):
         cross_left(left_n, 0, i, mask).wait_send()
         cross_left(left_a, 1, i, mask).wait_send()
@@ -950,10 +1219,11 @@
 
 def back_call(
     ctx_size, hidden_units, grad_two, resid, hidden, grad_out, normed, mixed, query, kv, total, cosine, sine, pos_q, pos_k,
-    small, spread, proj, out_w, grads,
+    small, spread, proj, out_w, grads, grads_two, near, zin_first, r_part,
 ):
     rows, model = resid.shape
-    shard, wide = grads.shape[3:]
+    shard = grads.shape[3]
+    one, two = widths(hidden_units)
     kv_width = KV_HEADS * HD
     q_width = HEADS * HD
     k_cols = 2 * kv_width + HD
@@ -962,13 +1232,15 @@
     vmem = pl.BlockSpec(memory_space=pltpu.VMEM)
     anywhere = pl.BlockSpec(memory_space=pl.ANY)
     shapes = (
-        ((rows, model), vmem),
-        ((shard, q_width), vmem),
-        ((shard, k_cols), vmem),
-        ((shard, q_width), vmem),
-        ((shard, hidden_units), anywhere),
-        ((shard, hidden_units), anywhere),
-        ((shard, hidden_units), anywhere),
+        ((rows, model), vmem, low),
+        ((rows, model), vmem, full),
+        ((shard, q_width), vmem, full),
+        ((shard, k_cols), vmem, full),
+        ((shard, q_width), vmem, full),
+        ((shard, hidden_units), anywhere, full),
+        ((shard, hidden_units), anywhere, full),
+        ((shard, hidden_units), anywhere, full),
+        ((2, rows, model), anywhere, low),
     )
     sem = pltpu.SemaphoreType.DMA
     cols = (q_width, q_width, k_cols)
@@ -978,9 +1250,9 @@
 
     return pl.pallas_call(
         functools.partial(back_kernel, ctx_size),
-        out_shape=tuple(jax.ShapeDtypeStruct(shape, full) for shape, _ in shapes),
-        in_specs=[vmem] * 15 + [anywhere] * 3,
-        out_specs=tuple(spec for _, spec in shapes),
+        out_shape=tuple(jax.ShapeDtypeStruct(shape, kind) for shape, _, kind in shapes),
+        in_specs=[vmem] * 15 + [anywhere] * 7,
+        out_specs=tuple(spec for _, spec, _ in shapes),
         scratch_shapes=[
             pltpu.VMEM(proj.shape, low),
             pltpu.VMEM((2, model, rows), low),
@@ -995,11 +1267,11 @@
             *each(span),
             *each(2, shard),
             *each(shard),
-            pltpu.VMEM((8, shard, wide), low),
-            pltpu.VMEM((2, 8, shard, wide), low),
-            pltpu.VMEM((8, shard, wide), low),
-            pltpu.VMEM((8, shard, wide), low),
-            pltpu.VMEM((2, shard, wide), full),
+            *([pltpu.VMEM((8, shard, 3 * one), low)] * 4),
+            *([pltpu.VMEM((2, 8, shard, 3 * two), low)] * 2),
+            *([pltpu.VMEM((8, shard, 3 * two), low)] * 2),
+            *([pltpu.VMEM((rows, model), low)] * 2),
+            pltpu.VMEM((2, shard, 3 * one), full),
             pltpu.VMEM((HEADS, rows, HD), low),
             pltpu.VMEM((HD, rows), full),
             pltpu.VMEM((ctx_size * rows, 2 * kv_width), full),
@@ -1007,8 +1279,8 @@
             pltpu.VMEM((2, rows, 2 * kv_width), low),
             pltpu.VMEM((rows, 2 * kv_width), low),
             pltpu.VMEM((rows, model), full),
-            sem((3,)), sem((2, 8)), sem((2, 8)), sem((8,)), sem((8,)), sem((8,)), sem((8,)),
-            sem((4, 4)), sem((4, 4)), sem((3, 6)), sem((3, 6)), sem((3,)), sem((3,)), sem((2,)),
+            sem((5,)), *([sem((8,))] * 6), *([sem((2, 8))] * 2), *([sem((8,))] * 4),
+            sem((4, 4)), sem((4, 4)), sem((3, 6)), sem((3, 6)), sem((3,)), sem((3,)), sem((2,)), sem((4,)), sem((4,)),
         ],
         compiler_params=pltpu.CompilerParams(
             collective_id=2, has_side_effects=True, vmem_limit_bytes=63 << 20
@@ -1016,7 +1288,7 @@
         name="back",
     )(
         grad_two, resid, hidden, grad_out, normed, mixed, query, kv, total, cosine, sine, pos_q, pos_k, small, spread,
-        proj, out_w, grads,
+        proj, out_w, grads, grads_two, near, zin_first, r_part,
     )
 
 
@@ -1070,21 +1342,19 @@
     unit = unit % kv_width // per * shard_rows + unit // kv_width * per + unit % per
     spread = (jnp.arange(D)[:, None] == unit[None, :]).astype(jnp.bfloat16)
     source = hidden.reshape(row_count, D)
-    normed, query_heads, key_value, log_total, mixed, resid, normed_two, small, proj_full, out_full, big, go_all = front_call(
+    normed, query_heads, key_value, log_total, mixed, resid, normed_two, small, proj_full, out_full, big, big_two, go_all, _ = front_call(
         ctx_size, source, cos_full, sin_full, local_pos.reshape(length, 1), every_pos.reshape(1, seq_len), spread,
         packed, w_out, w_gate, w_up, w_down, grad_out,
     )
-    tiles, grads = ffn_call(ctx_size, shard_rows, normed_two, go_all, big)
-    sums = jnp.sum(tiles.astype(jnp.float32), axis=0)
-    result = (resid + sums[1]).astype(jnp.bfloat16).reshape(batches, length, D)
-    hidden_grad, w_query_grad, kv_sum, w_out_grad, w_gate_grad, w_up_grad, w_down_grad = back_call(
-        ctx_size, w_gate.shape[1], sums[0], resid, source, grad_out, normed, mixed, query_heads, key_value, log_total,
+    grad_two, r_part, grads, grads_two, near, zin = ffn_call(ctx_size, shard_rows, normed_two, go_all, big, big_two)
+    result, hidden_grad, w_query_grad, kv_sum, w_out_grad, w_gate_grad, w_up_grad, w_down_grad, _ = back_call(
+        ctx_size, w_gate.shape[1], grad_two, resid, source, grad_out, normed, mixed, query_heads, key_value, log_total,
         cos_full, sin_full, local_pos.reshape(1, length), every_pos.reshape(seq_len, 1), small, spread,
-        proj_full, out_full, grads,
+        proj_full, out_full, grads, grads_two, near, zin, r_part,
     )
     sides = kv_sum[:, 2 * kv_width : 2 * kv_width + 4]
     return (
-        result,
+        result.reshape(batches, length, D),
         hidden_grad.reshape(batches, length, D),
         sides[:, 0],
         w_query_grad,

time: 585 us -> 493 us (0.84)
  Pallas kernels: 547 us -> 465 us
  other arithmetic: 12.1 us -> 4.94 us
    pallas_call x1, Pallas kernels: 214 us -> 153 us  [front_call(): pl.pallas_call(functools.partial(front_kernel, ctx_size), out_shape=tuple...]
    pallas_call x1, Pallas kernels: 193 us -> 173 us  [back_call(): pl.pallas_call(functools.partial(back_kernel, ctx_size), out_shape=tuple(...]
where the time goes in v4:
time: 493 us; the launch traced here: 488 us
  Pallas kernels  465 us (94%)
  local copies, waits for them, and re-layouts  16.9 us (3%)
  other arithmetic  4.94 us (1%)
    pallas_call x1, Pallas kernels, back_call(): pl.pallas_call(functools.partial(back_kernel, ctx_size), out_shape=tuple(...  173 us
    pallas_call x1, Pallas kernels, front_call(): pl.pallas_call(functools.partial(front_kernel, ctx_size), out_shape=tuple...  153 us
    pallas_call x1, Pallas kernels, ffn_call(): pl.pallas_call(functools.partial(ffn_kernel, ctx_size), out_shape=(jax.Sh...  139 us
    unnamed x39, local copies, waits for them, and re-layouts  10 us

profile of v4, /device:TPU:0, one launch (start us, length us, event | category | flops | bytes accessed | tf_op | source)
XLA Modules:
  0.0 488.1 jit_solution(423621519531970624)
XLA Ops:
  0.6 0.0 copy-start.15
  0.7 0.0 copy-start.14
  0.7 0.0 copy-start.11
  0.7 0.0 copy-start.12
  0.7 0.0 copy-start.13
  0.7 0.0 copy-start.6
  0.7 0.0 copy-start.7
  0.7 0.0 copy-start.8
  0.7 0.7 multiply_bitcast_fusion
  1.5 0.1 broadcast_in_dim.6
  1.6 0.0 copy-start.10
  1.6 0.5 fusion.5
  2.2 0.8 pad_maximum_fusion
  3.0 0.8 copy.37.pos_q
  3.8 1.9 fusion.spread
  5.7 0.0 copy-done.15
  5.7 0.0 copy-done.14
  5.7 0.1 fusion.26
  5.7 0.1 copy.36
  5.8 0.0 copy-done.11
  5.8 0.1 copy.33
  6.0 0.0 copy-done.12
  6.0 0.1 copy.34
  6.1 0.0 copy-done.13
  6.1 0.1 copy.35
  6.2 0.0 copy-done.6
  6.2 0.0 copy-done.7
  6.2 0.0 copy-done.8
  6.2 0.8 concatenate.15.packed
  7.0 0.0 copy-done.9
  7.0 153.0 %front.1 = (bf16[256,1536]{1,0:T(8,128)(2,1)}, bf16[12,256,128]{2,1,0:T(8,128)(2,1)}, bf16[4,256,512]{2,1,0:T(8,128)(2,1)}, f32[256,128]{1,0:T(8,128)}, bf16[256...) custom-call(bf16[256,1536]{1,0:T(8,128)(2,1)} %bitcast.15, ...), custom_call_target="tpu_custom_call" | custom-call | tf_op jit(solution)/shard_map/front/pallas_call | solution.py:778
  160.0 0.0 copy-done.10
  160.0 138.6 %ffn.1 = (f32[256,1536]{1,0:T(8,128)}, bf16[4,256,1536]{2,1,0:T(8,128)(2,1)}, bf16[2,2,8,48,2304]{4,3,2,1,0:T(8,128)(2,1)}, bf16[2,2,8,48,1152]{4,3,2,1,0:T(8,12...) custom-call(bf16[256,1536]{1,0:T(8,128)(2,1)} %get-tuple-element.41.n_own, ...), custom_call_target="tpu_custom_call" | custom-call | tf_op jit(solution)/shard_map/ffn/pallas_call | solution.py:382
  298.7 0.2 copy.38
  298.9 0.9 fusion.1.pos_k
  299.7 173.5 %back.1 = (bf16[256,1536]{1,0:T(8,128)(2,1)}, f32[256,1536]{1,0:T(8,128)}, f32[48,1536]{1,0:T(8,128)}, f32[48,640]{1,0:T(8,128)}, f32[48,1536]{1,0:T(8,128)}, /*...) custom-call(f32[256,1536]{1,0:T(8,128)} %get-tuple-element.45.grad_two, ...), custom_call_target="tpu_custom_call" | custom-call | tf_op jit(solution)/shard_map/back/pallas_call | solution.py:1251
  473.2 1.6 fusion.28
  474.8 1.6 slice_reduce_fusion
  476.4 1.4 slice_reduce_fusion.3
  477.8 2.1 copy.46
  479.9 1.1 copy.47
  481.1 0.7 copy.48
  481.8 0.7 copy.49
  482.5 1.2 copy.50
  483.7 0.9 copy-done.1
  484.6 1.2 copy.51
  485.8 0.9 copy-done
  486.7 1.2 copy.52
  (16 shorter events, 0.1 us)
Async XLA Ops:
  0.6 5.0 %copy-start.15 = (bf16[8]{0:T(256)(128)(2,1)S(1)}, bf16[8]{0:T(256)(128)(2,1)}, u32[]{:S(2)}) copy-start(bf16[8]{0:T(256)(128)(2,1)} %param.22) | copy-start | bytes 52
  0.7 5.0 %copy-start.14 = (bf16[8]{0:T(256)(128)(2,1)S(1)}, bf16[8]{0:T(256)(128)(2,1)}, u32[]{:S(2)}) copy-start(bf16[8]{0:T(256)(128)(2,1)} %param.24) | copy-start | bytes 52
  0.7 5.2 %copy-start.11 = (bf16[48]{0:T(256)(128)(2,1)S(1)}, bf16[48]{0:T(256)(128)(2,1)}, u32[]{:S(2)}) copy-start(bf16[48]{0:T(256)(128)(2,1)} %param.18) | copy-start | bytes 292
  0.7 5.3 %copy-start.12 = (bf16[48]{0:T(256)(128)(2,1)S(1)}, bf16[48]{0:T(256)(128)(2,1)}, u32[]{:S(2)}) copy-start(bf16[48]{0:T(256)(128)(2,1)} %param.20) | copy-start | bytes 292
  0.7 5.4 %copy-start.13 = (bf16[48]{0:T(256)(128)(2,1)S(1)}, bf16[48]{0:T(256)(128)(2,1)}, u32[]{:S(2)}) copy-start(bf16[48]{0:T(256)(128)(2,1)} %param.26) | copy-start | bytes 292
  0.7 5.5 %copy-start.6 = (bf16[48,1536]{1,0:T(8,128)(2,1)S(1)}, bf16[48,1536]{1,0:T(8,128)(2,1)}, u32[]{:S(2)}) copy-start(bf16[48,1536]{1,0:T(8,128)(2,1)} %param.19) | copy-start | bytes 442372
  0.7 5.5 %copy-start.7 = (bf16[48,256]{1,0:T(8,128)(2,1)S(1)}, bf16[48,256]{1,0:T(8,128)(2,1)}, u32[]{:S(2)}) copy-start(bf16[48,256]{1,0:T(8,128)(2,1)} %param.21) | copy-start | bytes 73732
  0.7 5.5 %copy-start.8 = (bf16[48,256]{1,0:T(8,128)(2,1)S(1)}, bf16[48,256]{1,0:T(8,128)(2,1)}, u32[]{:S(2)}) copy-start(bf16[48,256]{1,0:T(8,128)(2,1)} %param.23) | copy-start | bytes 73732
  1.6 5.4 %copy-start.9 = (s32[1,1024]{1,0:T(1,128)}, s32[1,1024]{1,0:T(1,128)S(1)}, u32[]{:S(2)}) copy-start(s32[1,1024]{1,0:T(1,128)S(1)} %fusion.14.pos_k) | copy-start | bytes 12292
  1.6 158.4 %copy-start.10 = (s32[1,256]{1,0:T(1,128)}, s32[1,256]{1,0:T(1,128)S(1)}, u32[]{:S(2)}) copy-start(s32[1,256]{1,0:T(1,128)S(1)} %get-tuple-element.74.pos_q) | copy-start | bytes 3076
  473.2 6.7 %copy-start.3 = (f32[256,1536]{1,0:T(8,128)S(1)}, f32[256,1536]{1,0:T(8,128)}, u32[]{:S(2)}) copy-start(f32[256,1536]{1,0:T(8,128)} %get-tuple-element.61) | copy-start | bytes 4718596
  479.9 1.2 copy-start.5
  479.9 1.9 copy-start.4
  479.9 2.6 copy-start.2
  482.5 2.1 copy-start.1
  484.6 2.1 copy-start

commit v5 on v4

--- a/solution.py
+++ b/solution.py
@@ -134,7 +134,7 @@
     load_n = pltpu.make_async_copy(n_own, nt.at[0], io_sem.at[0])
     load_w = pltpu.make_async_copy(big, w_one, io_sem.at[1])
     load_go = pltpu.make_async_copy(go_all, go, io_sem.at[2])
-    held = (0, 4, 1, 5, 16, 20, 17, 21)
+    held = (0, 4, 1, 5, 16, 20, 17, 21, 2, 6, 3, 7)
     load_l = [
         pltpu.make_async_copy(big_two.at[block(mask)], w_two.at[block(mask)], l_sem.at[i]) for i, mask in enumerate(held)
     ]
@@ -163,7 +163,7 @@
     n_push(1).start()
     n_push(2).start()
     n_core(0).start()
-    for mask in held:
+    for mask in (16, 20, 17, 21):
         spread_two(mask, 2)
     for mask in held:
         spread_two(mask, 8)
@@ -209,28 +209,17 @@
 
         first(2 * o)
 
-        @pl.when(o == 1)
-        def _():
-            for mask in (2, 6, 3):
-                w_pass(mask)
-
-        @pl.when(o == 2)
-        def _():
-            for mask in (7, 18, 22):
-                w_pass(mask)
 
         n_core(2 * o).wait_recv()
         first(2 * o + 1)
         return carry
 
     lax.fori_loop(0, 4, early, 0)
-    for mask in (19, 23):
-        w_pass(mask)
     def stage_wait(slot, size):
         part_of = stage.at[slot, :, pl.ds(0, size)]
         pltpu.make_async_copy(part_of, part_of, st_sem.at[slot]).wait()
 
-    def weights(size, start_gu, start_act, to, q, carry):
+    def weights(size, start_gu, start_act, to, passes, q, carry):
         slot = q % 2
 
         @pl.when(q > 1)
@@ -249,6 +238,12 @@
             count = min(one, 2 * size - start)
             product(nt, ggu, start_gu + start, count, start)
         product(go, act, start_act, size, 2 * size)
+        for n, masks in enumerate(passes):
+            @pl.when(q == n)
+            def _():
+                for mask in masks:
+                    w_pass(mask)
+
         yr, xr = either(q // 2, y), either(q % 2, x)
         for j in range(8):
             cr, hrel, pr = either(j // 4, c), either((j // 2) % 2, h), either(j % 2, p)
@@ -258,8 +253,8 @@
             ).start()
         return carry
 
-    def all_weights(size, start_gu, start_act, to):
-        lax.fori_loop(0, 4, functools.partial(weights, size, start_gu, start_act, to), 0)
+    def all_weights(size, start_gu, start_act, to, passes=()):
+        lax.fori_loop(0, 4, functools.partial(weights, size, start_gu, start_act, to, passes), 0)
         stage_wait(0, 3 * size)
         stage_wait(1, 3 * size)
 
@@ -281,7 +276,7 @@
             if j < 4:
                 z_push(j).start()
 
-    all_weights(one, 0, 0, grads)
+    all_weights(one, 0, 0, grads, ((18, 22, 19, 23),))
     for j in range(8):
         far_push(j).start()
     load_own(0).start()
@@ -369,7 +364,7 @@
     for o in (1, 2, 3):
         n_push(o).wait_send()
         final(o).wait_send()
-    sent = w_two.at[pl.ds(0, 24 * shard)]
+    sent = w_two.at[pl.ds(0, 20 * shard)]
     pltpu.make_async_copy(sent, sent, w_send.at[0]).wait()
 
 
@@ -406,7 +401,7 @@
             pltpu.VMEM((4, shard, 3 * one), low),
             pltpu.VMEM((8, shard, 3 * one), low),
             sem((4,)), sem((5,)), sem((5,)), sem((4,)), sem((4,)), sem, sem((2,)), sem((4,)), sem((4,)), sem((2,)),
-            sem((1,)), sem((32,)), sem((8,)), sem((8,)), sem((8,)), sem((4,)), sem((4,)), sem((1,)),
+            sem((1,)), sem((32,)), sem((12,)), sem((8,)), sem((8,)), sem((4,)), sem((4,)), sem((1,)),
         ],
         compiler_params=pltpu.CompilerParams(
             collective_id=1, has_side_effects=True, vmem_limit_bytes=65200 << 10
@@ -692,6 +687,11 @@
     mixed_back = pltpu.make_async_copy(mixed, mixed_o, back_sem.at[2])
     mixed_back.start()
     relay_pass(17, 21)
+
+    def two_over_z(mask):
+        src = big_two.at[block(mask)] if mask else source_two.at[column(0)]
+        return remote(src, big_two.at[block(mask)], big_send.at[1], two_recv.at[mask | 2], 2)
+
     for mask in (3, 7):
         big_pass(mask, 8)
     for mask in (4, 1, 5, 16, 20, 17, 21):
@@ -714,20 +714,26 @@
     go_core(1).start()
     go_push(2).wait_recv()
     go_core(2).start()
-    for mask in (18, 22, 19, 23):
-        big_pass(mask, 8)
+    two_over_z(0).start()
+    for mask, passed in ((4, 18), (1, 22), (5, 19), (0, 23)):
+        big_pass(passed, 8)
+        if mask:
+            cut_two(mask).wait_recv()
+            two_over_z(mask).start()
 
     for mask in (8, 12, 9, 24, 13, 28, 25, 29, 10, 14, 11, 26, 15, 30, 27, 31):
         big_pass(mask)
     go_push(3).wait_recv()
     go_core(3).start()
-    for mask in (4, 1, 5, 16, 20, 17, 21):
+    for mask in (16, 20, 17, 21):
         cut_two(mask).wait_recv()
+    for mask in (0, 4, 1, 5):
+        two_over_z(mask).wait_recv()
     own_big.wait()
     own_two.wait()
     own_go.wait()
     drain(big.at[pl.ds(0, 31 * shard)], big_send.at[0])
-    drain(big_two.at[pl.ds(0, 7 * shard)], big_send.at[1])
+    drain(big_two.at[pl.ds(0, 11 * shard)], big_send.at[1])
 
     @pl.when(inner)
     def _():
@@ -801,11 +807,11 @@
 def back_kernel(
     ctx_size, grad_two, resid, hidden, grad_out, normed, mixed, query, kv, total, cosine, sine, pos_q, pos_k, small, spread,
     proj, out_w, grads, grads_two, near, zin_first, r_part,
-    result_o, hidden_o, query_o, key_o, outw_o, gate_o, up_o, down_o, r_in,
+    result_o, hidden_o, query_o, key_o, outw_o, gate_o, up_o, down_o, r_in, relay, relay_two,
     weight, turned, left_n, left_a, right_b, right_p, side, side_in, g_b, g_q, g_k,
     y_b, y_q, y_k, x_b, x_q, x_k, p_b, p_q, p_k, h_b, h_q, h_k,
     own, far, zin, fin, own_two, far_two, zin_two, fin_two, r_mid, r_one, stage, heads_g, lse, dkv, kv_out, kv_p, kv_h, grad_resid,
-    load_sem, xs, xr, zs, zr, fs, fr, xs2, xr2, zs2, zr2, fs2, fr2, cs, cr, rs, rr, ks, kr, st_sem, os, orr,
+    load_sem, xs, xr, zs, zr, fs, fr, xs2, xr2, zs2, zr2, fs2, fr2, relay_recv, relay_send, cs, cr, rs, rr, ks, kr, st_sem, os, orr,
 ):
     dp = lax.axis_index("dp")
     ctx = lax.axis_index("ctx")
@@ -837,7 +843,7 @@
         return (j // 4) * 16 + ((j // 2) % 2) * 4 + j % 2
 
     barrier = pltpu.get_barrier_semaphore()
-    partners = (1, 2, 4, 5, 8, 16, 17, 20, 21)
+    partners = (1, 2, 3, 4, 5, 8, 16, 17, 20, 21)
     for mask in partners:
         pl.semaphore_signal(barrier, inc=1, device_id=at(flip(me, mask)), device_id_type=MESH)
     load_w = pltpu.make_async_copy(out_w, weight.at[:, pl.ds(0, q_width)], load_sem.at[0])
@@ -864,6 +870,39 @@
     def z_two_push(j):
         return remote(far_two.at[1, j], zin_two.at[j], zs2.at[j], zr2.at[j], 2)
 
+    inner = either(h, p) == 1
+
+    def over_z(push, src, to, send, n):
+        @pl.when(inner)
+        def _():
+            push.start()
+
+        @pl.when(jnp.logical_not(inner))
+        def _():
+            remote(src, to, send, relay_recv.at[n], 1).start()
+
+    def over_z_one(j):
+        over_z(z_push(j), near.at[j], relay.at[j - 4], zs.at[j], j)
+
+    def over_z_two(j):
+        over_z(z_two_push(j), far_two.at[1, j], relay_two.at[j], zs2.at[j], 8 + j)
+
+    def relay_one(*blocks):
+        @pl.when(inner)
+        def _():
+            for j in blocks:
+                part = relay.at[j - 4]
+                remote(part, part, relay_send.at[j], relay_recv.at[j], 1).wait_recv()
+                remote(part, zin.at[j], relay_send.at[j], zr.at[j], 3).start()
+
+    def relay_two_pass(*blocks):
+        @pl.when(inner)
+        def _():
+            for j in blocks:
+                part = relay_two.at[j]
+                remote(part, part, relay_send.at[8 + j], relay_recv.at[8 + j], 1).wait_recv()
+                remote(part, zin_two.at[j], relay_send.at[8 + j], zr2.at[j], 3).start()
+
     def fin_push(j):
         return remote(own.at[j], fin.at[j], fs.at[j], fr.at[j], mask_of(j))
 
@@ -873,7 +912,7 @@
     def z_two_step(j):
         far_two_push(1, j).wait_recv()
         far_two[1, j] = (far_two[1, j].astype(full) + own_two[1, j].astype(full)).astype(low)
-        z_two_push(j).start()
+        over_z_two(j)
 
     def total_step(j):
         far_push(j).wait_recv()
@@ -897,7 +936,7 @@
 
     r_push(3).start()
     for j in range(4, 8):
-        z_push(j).start()
+        over_z_one(j)
     for j in range(8):
         far_two_push(1, j).start()
     for j in range(8):
@@ -1018,7 +1057,9 @@
         return carry
 
     dkv[...] = jnp.zeros_like(dkv)
-    lax.fori_loop(0, HEADS, head, 0)
+    lax.fori_loop(0, HEADS // 2, head, 0)
+    relay_one(4, 5)
+    lax.fori_loop(HEADS // 2, HEADS, head, 0)
 
     for z in range(ctx_size):
         part = dkv[pl.ds(z * rows, rows)]
@@ -1039,9 +1080,6 @@
     cross_q.start()
     for copy in load_own:
         copy.wait()
-    r_push(3).wait_recv()
-    add(r_one, r_mid)
-    r_push(1).start()
     for i, mask in enumerate((0, 8, 16, 24)):
         cross_left(left_n, 0, i, mask).wait_recv()
     cross_q.wait_recv()
@@ -1049,7 +1087,6 @@
         g_q[i] = dot(left_n[i], right_p[:, pl.ds(0, q_width)], ((1,), (0,))).astype(low)
         if i > 1:
             y_push(1, i - 2).start()
-    y_push(0, 0).start()
     load_p.wait()
     hidden_o[...] = dot(right_p[pl.ds(0, rows), pl.ds(0, q_width)], weight[:, pl.ds(0, q_width)], ((1,), (1,)))
     kv_push(1).wait_recv()
@@ -1057,10 +1094,12 @@
     kv_cross().start()
     kv_push(0).wait_recv()
     add(kv_out.at[2 * h + p], kv_p.at[0])
+    relay_one(6, 7)
     for j in range(8):
         z_two_step(j)
     for j in range(4):
         total_step(j)
+    relay_two_pass(0, 1, 2)
     kv_cross().wait_recv()
     final = kv_out[2 * h + p].astype(full) + kv_h[...].astype(full)
     for g in range(KV_HEADS):
@@ -1146,25 +1185,30 @@
         pl.when(piece(j) < 7)(lambda: write(j, one, two, two))
         pl.when(piece(j) == 7)(lambda: write(j, one, two, last))
 
+    y_push(0, 0).start()
+    r_push(3).wait_recv()
+    add(r_one, r_mid)
+    r_push(1).start()
+    relay_two_pass(3, 4, 5, 6, 7)
+    for j in range(4, 8):
+        total_step(j)
     y_pass(1)
     y_pass(2)
-    y_pass(0)
     for j in range(8):
         far_two_push(0, j).start()
-    for j in range(4):
-        store(j)
+    y_pass(0)
     x_pass(1)
     x_pass(2)
     r_push(2).start()
-    for j in range(4, 8):
-        total_step(j)
+    for j in range(4):
+        store(j)
     p_pass(1)
     p_pass(2)
-    x_pass(0)
+    for j in range(8):
+        total_two_step(j)
     for j in range(4, 8):
         store(j)
-    for j in range(8):
-        total_two_step(j)
+    x_pass(0)
     p_pass(0)
     h_pass(1, query_o)
     h_pass(2, key_o)
@@ -1200,6 +1244,13 @@
         if j:
             fin_push(j).wait_send()
             fin_two_push(j).wait_send()
+    @pl.when(inner)
+    def _():
+        for j in range(4, 8):
+            remote(relay.at[j - 4], relay.at[j - 4], relay_send.at[j], relay_recv.at[j], 1).wait_send()
+        for j in range(8):
+            remote(relay_two.at[j], relay_two.at[j], relay_send.at[8 + j], relay_recv.at[8 + j], 1).wait_send()
+
     for i, mask in enumerate((0, 8, 16, 24)):
         cross_left(left_n, 0, i, mask).wait_send()
         cross_left(left_a, 1, i, mask).wait_send()
@@ -1241,6 +1292,8 @@
         ((shard, hidden_units), anywhere, full),
         ((shard, hidden_units), anywhere, full),
         ((2, rows, model), anywhere, low),
+        ((4, shard, 3 * one), anywhere, low),
+        ((8, shard, 3 * two), anywhere, low),
     )
     sem = pltpu.SemaphoreType.DMA
     cols = (q_width, q_width, k_cols)
@@ -1279,7 +1332,7 @@
             pltpu.VMEM((2, rows, 2 * kv_width), low),
             pltpu.VMEM((rows, 2 * kv_width), low),
             pltpu.VMEM((rows, model), full),
-            sem((5,)), *([sem((8,))] * 6), *([sem((2, 8))] * 2), *([sem((8,))] * 4),
+            sem((5,)), *([sem((8,))] * 6), *([sem((2, 8))] * 2), *([sem((8,))] * 4), sem((16,)), sem((16,)),
             sem((4, 4)), sem((4, 4)), sem((3, 6)), sem((3, 6)), sem((3,)), sem((3,)), sem((2,)), sem((4,)), sem((4,)),
         ],
         compiler_params=pltpu.CompilerParams(
@@ -1346,8 +1399,8 @@
         ctx_size, source, cos_full, sin_full, local_pos.reshape(length, 1), every_pos.reshape(1, seq_len), spread,
         packed, w_out, w_gate, w_up, w_down, grad_out,
     )
-    grad_two, r_part, grads, grads_two, near, zin = ffn_call(ctx_size, shard_rows, normed_two, go_all, big, big_two)
-    result, hidden_grad, w_query_grad, kv_sum, w_out_grad, w_gate_grad, w_up_grad, w_down_grad, _ = back_call(
+    grad_two, r_part, grads, grads_two, near, zin, *_ = ffn_call(ctx_size, shard_rows, normed_two, go_all, big, big_two)
+    result, hidden_grad, w_query_grad, kv_sum, w_out_grad, w_gate_grad, w_up_grad, w_down_grad, *_ = back_call(
         ctx_size, w_gate.shape[1], grad_two, resid, source, grad_out, normed, mixed, query_heads, key_value, log_total,
         cos_full, sin_full, local_pos.reshape(1, length), every_pos.reshape(seq_len, 1), small, spread,
         proj_full, out_full, grads, grads_two, near, zin, r_part,

time: 493 us -> 462 us (0.937)
  Pallas kernels: 465 us -> 435 us
    pallas_call x1, Pallas kernels: 173 us -> 150 us  [back_call(): pl.pallas_call(functools.partial(back_kernel, ctx_size), out_shape=tuple(...]
    pallas_call x1, Pallas kernels: 139 us -> 130 us  [ffn_call(): pl.pallas_call(functools.partial(ffn_kernel, ctx_size), out_shape=(jax.Sh...]
where the time goes in v5:
time: 462 us; the launch traced here: 458 us
  Pallas kernels  435 us (94%)
  local copies, waits for them, and re-layouts  17 us (4%)
  other arithmetic  4.94 us (1%)
    pallas_call x1, Pallas kernels, front_call(): pl.pallas_call(functools.partial(front_kernel, ctx_size), out_shape=tuple...  155 us
    pallas_call x1, Pallas kernels, back_call(): pl.pallas_call(functools.partial(back_kernel, ctx_size), out_shape=tuple(...  150 us
    pallas_call x1, Pallas kernels, ffn_call(): pl.pallas_call(functools.partial(ffn_kernel, ctx_size), out_shape=(jax.Sh...  130 us
    unnamed x39, local copies, waits for them, and re-layouts  10 us

profile of v5, /device:TPU:0, one launch (start us, length us, event | category | flops | bytes accessed | tf_op | source)
XLA Modules:
  0.0 457.7 jit_solution(9989843869261536444)
XLA Ops:
  0.6 0.0 copy-start.15
  0.7 0.0 copy-start.14
  0.7 0.0 copy-start.11
  0.7 0.0 copy-start.12
  0.7 0.0 copy-start.13
  0.7 0.0 copy-start.6
  0.7 0.0 copy-start.7
  0.7 0.0 copy-start.8
  0.7 0.7 multiply_bitcast_fusion
  1.5 0.1 broadcast_in_dim.6
  1.6 0.0 copy-start.10
  1.6 0.5 fusion.5
  2.2 0.8 pad_maximum_fusion
  3.0 0.8 copy.37.pos_q
  3.8 1.9 fusion.spread
  5.7 0.0 copy-done.15
  5.7 0.0 copy-done.14
  5.7 0.1 fusion.26
  5.7 0.1 copy.36
  5.8 0.0 copy-done.11
  5.8 0.1 copy.33
  6.0 0.0 copy-done.12
  6.0 0.1 copy.34
  6.1 0.0 copy-done.13
  6.1 0.1 copy.35
  6.2 0.0 copy-done.6
  6.2 0.0 copy-done.7
  6.2 0.0 copy-done.8
  6.2 0.8 concatenate.15.packed
  7.0 0.0 copy-done.9
  7.0 155.3 %front.1 = (bf16[256,1536]{1,0:T(8,128)(2,1)}, bf16[12,256,128]{2,1,0:T(8,128)(2,1)}, bf16[4,256,512]{2,1,0:T(8,128)(2,1)}, f32[256,128]{1,0:T(8,128)}, bf16[256...) custom-call(bf16[256,1536]{1,0:T(8,128)(2,1)} %bitcast.15, ...), custom_call_target="tpu_custom_call" | custom-call | tf_op jit(solution)/shard_map/front/pallas_call | solution.py:784
  162.3 129.6 %ffn.1 = (f32[256,1536]{1,0:T(8,128)}, bf16[4,256,1536]{2,1,0:T(8,128)(2,1)}, bf16[2,2,8,48,2304]{4,3,2,1,0:T(8,128)(2,1)}, bf16[2,2,8,48,1152]{4,3,2,1,0:T(8,12...) custom-call(bf16[256,1536]{1,0:T(8,128)(2,1)} %get-tuple-element.41.n_own, ...), custom_call_target="tpu_custom_call" | custom-call | tf_op jit(solution)/shard_map/ffn/pallas_call | solution.py:377
  291.9 0.2 copy.38
  292.2 0.9 fusion.1.pos_k
  293.0 149.8 %back.1 = (bf16[256,1536]{1,0:T(8,128)(2,1)}, f32[256,1536]{1,0:T(8,128)}, f32[48,1536]{1,0:T(8,128)}, f32[48,640]{1,0:T(8,128)}, f32[48,1536]{1,0:T(8,128)}, /*...) custom-call(f32[256,1536]{1,0:T(8,128)} %get-tuple-element.45.grad_t, ...), custom_call_target="tpu_custom_call" | custom-call | tf_op jit(solution)/shard_map/back/pallas_call | solution.py:1304
  442.8 0.0 copy-start.3
  442.8 1.6 fusion.28
  444.4 1.6 slice_reduce_fusion
  446.0 1.4 slice_reduce_fusion.3
  447.4 2.1 copy.46
  449.5 1.1 copy.47
  450.6 0.7 copy.48
  451.3 0.7 copy.49
  452.1 1.2 copy.50
  453.2 0.9 copy-done.1
  454.1 1.2 copy.51
  455.3 0.9 copy-done
  456.2 1.2 copy.52
  (16 shorter events, 0.1 us)
Async XLA Ops:
  0.6 5.0 %copy-start.15 = (bf16[8]{0:T(256)(128)(2,1)S(1)}, bf16[8]{0:T(256)(128)(2,1)}, u32[]{:S(2)}) copy-start(bf16[8]{0:T(256)(128)(2,1)} %param.22) | copy-start | bytes 52
  0.7 5.0 %copy-start.14 = (bf16[8]{0:T(256)(128)(2,1)S(1)}, bf16[8]{0:T(256)(128)(2,1)}, u32[]{:S(2)}) copy-start(bf16[8]{0:T(256)(128)(2,1)} %param.24) | copy-start | bytes 52
  0.7 5.2 %copy-start.11 = (bf16[48]{0:T(256)(128)(2,1)S(1)}, bf16[48]{0:T(256)(128)(2,1)}, u32[]{:S(2)}) copy-start(bf16[48]{0:T(256)(128)(2,1)} %param.18) | copy-start | bytes 292
  0.7 5.3 %copy-start.12 = (bf16[48]{0:T(256)(128)(2,1)S(1)}, bf16[48]{0:T(256)(128)(2,1)}, u32[]{:S(2)}) copy-start(bf16[48]{0:T(256)(128)(2,1)} %param.20) | copy-start | bytes 292
  0.7 5.4 %copy-start.13 = (bf16[48]{0:T(256)(128)(2,1)S(1)}, bf16[48]{0:T(256)(128)(2,1)}, u32[]{:S(2)}) copy-start(bf16[48]{0:T(256)(128)(2,1)} %param.26) | copy-start | bytes 292
  0.7 5.5 %copy-start.6 = (bf16[48,1536]{1,0:T(8,128)(2,1)S(1)}, bf16[48,1536]{1,0:T(8,128)(2,1)}, u32[]{:S(2)}) copy-start(bf16[48,1536]{1,0:T(8,128)(2,1)} %param.19) | copy-start | bytes 442372
  0.7 5.5 %copy-start.7 = (bf16[48,256]{1,0:T(8,128)(2,1)S(1)}, bf16[48,256]{1,0:T(8,128)(2,1)}, u32[]{:S(2)}) copy-start(bf16[48,256]{1,0:T(8,128)(2,1)} %param.21) | copy-start | bytes 73732
  0.7 5.5 %copy-start.8 = (bf16[48,256]{1,0:T(8,128)(2,1)S(1)}, bf16[48,256]{1,0:T(8,128)(2,1)}, u32[]{:S(2)}) copy-start(bf16[48,256]{1,0:T(8,128)(2,1)} %param.23) | copy-start | bytes 73732
  1.6 5.4 %copy-start.9 = (s32[1,1024]{1,0:T(1,128)}, s32[1,1024]{1,0:T(1,128)S(1)}, u32[]{:S(2)}) copy-start(s32[1,1024]{1,0:T(1,128)S(1)} %fusion.14.pos_k) | copy-start | bytes 12292
  1.6 160.7 %copy-start.10 = (s32[1,256]{1,0:T(1,128)}, s32[1,256]{1,0:T(1,128)S(1)}, u32[]{:S(2)}) copy-start(s32[1,256]{1,0:T(1,128)S(1)} %get-tuple-element.74.pos_q) | copy-start | bytes 3076
  442.8 6.7 %copy-start.3 = (f32[256,1536]{1,0:T(8,128)S(1)}, f32[256,1536]{1,0:T(8,128)}, u32[]{:S(2)}) copy-start(f32[256,1536]{1,0:T(8,128)} %get-tuple-element.61) | copy-start | bytes 4718596
  449.5 1.2 copy-start.5
  449.5 1.9 copy-start.4
  449.5 2.6 copy-start.2
  452.1 2.1 copy-start.1
  454.1 2.1 copy-start

commit v6 on v5

--- a/solution.py
+++ b/solution.py
@@ -101,7 +101,7 @@
 
 
 def ffn_kernel(
-    ctx_size, n_own, go_all, big, big_two,
+    ctx_size, n_own, norm_y, go_all, big, big_two,
     grad_two, r_part, grads, grads_two, near, zin,
     w_one, w_two, nt, go, ggu, act, crecv, part, h_in, h_mid, stage, own, far,
     io_sem, n_send, n_recv, f_send, f_recv, c_send, c_recv, o_send, o_recv, st_sem, w_send, w_recv, l_sem, x_send, x_recv, z_send, z_recv, d_sem,
@@ -132,13 +132,14 @@
     for mask in partners:
         pl.semaphore_signal(barrier, inc=1, device_id=at(flip(me, mask)), device_id_type=MESH)
     load_n = pltpu.make_async_copy(n_own, nt.at[0], io_sem.at[0])
+    load_y = pltpu.make_async_copy(norm_y, nt.at[4], io_sem.at[3])
     load_w = pltpu.make_async_copy(big, w_one, io_sem.at[1])
     load_go = pltpu.make_async_copy(go_all, go, io_sem.at[2])
     held = (0, 4, 1, 5, 16, 20, 17, 21, 2, 6, 3, 7)
     load_l = [
         pltpu.make_async_copy(big_two.at[block(mask)], w_two.at[block(mask)], l_sem.at[i]) for i, mask in enumerate(held)
     ]
-    for copy in (load_n, load_w, load_go, *load_l):
+    for copy in (load_n, load_y, load_w, load_go, *load_l):
         copy.start()
     pl.semaphore_wait(barrier, len(partners))
 
@@ -156,13 +157,17 @@
         return remote(nt.at[slot], nt.at[slot + 1], f_send.at[slot // 2], f_recv.at[slot // 2], 4)
 
     def n_push(o):
-        src = nt.at[2] if o == 3 else nt.at[0]
-        return remote(src, nt.at[2 * o], n_send.at[o], n_recv.at[o], (0, 1, 16, 16)[o])
+        half = pl.ds((o - 1) % 2 * (rows // 2), rows // 2)
+        if o == 1:
+            return remote(nt.at[0], nt.at[2], n_send.at[1], n_recv.at[1], 1)
+        return remote(nt.at[(0, 0, 4, 2)[o], half], nt.at[6, half], n_send.at[o], n_recv.at[o], (0, 0, 1, 16)[o])
 
     load_n.wait()
     n_push(1).start()
+    n_core(0).start()
+    load_y.wait()
     n_push(2).start()
-    n_core(0).start()
+    n_core(4).start()
     for mask in (16, 20, 17, 21):
         spread_two(mask, 2)
     for mask in held:
@@ -193,17 +198,18 @@
         out = out + dot(act[slot, :, one:], w_two[:, 2 * two :], ((1,), (1,)))
         return (grad.astype(low), out.astype(low))
 
-    def early(o, carry):
+    def early(n, carry):
+        o = n % 2 * 2 + n // 2
+
         @pl.when(o == 1)
         def _():
             n_push(1).wait_recv()
             n_push(3).start()
             n_core(2).start()
-            n_push(2).wait_recv()
-            n_core(4).start()
 
         @pl.when(o == 3)
         def _():
+            n_push(2).wait_recv()
             n_push(3).wait_recv()
             n_core(6).start()
 
@@ -368,7 +374,7 @@
     pltpu.make_async_copy(sent, sent, w_send.at[0]).wait()
 
 
-def ffn_call(ctx_size, shard, n_own, go_all, big, big_two):
+def ffn_call(ctx_size, shard, n_own, norm_y, go_all, big, big_two):
     rows, model = n_own.shape
     one, two = big.shape[1] // 3, big_two.shape[1] // 3
     low = jnp.bfloat16
@@ -384,7 +390,7 @@
             jax.ShapeDtypeStruct((8, shard, 3 * one), low),
             jax.ShapeDtypeStruct((4, shard, 3 * one), low),
         ),
-        in_specs=[anywhere] * 4,
+        in_specs=[anywhere] * 5,
         out_specs=[pl.BlockSpec(memory_space=pltpu.VMEM)] + [anywhere] * 5,
         scratch_shapes=[
             pltpu.VMEM((model, 3 * one), low),
@@ -407,7 +413,7 @@
             collective_id=1, has_side_effects=True, vmem_limit_bytes=65200 << 10
         ),
         name="ffn",
-    )(n_own, go_all, big, big_two)
+    )(n_own, norm_y, go_all, big, big_two)
 
 
 def turn(values, cosine, sine):
@@ -415,15 +421,15 @@
 
 
 def front_kernel(
-    ctx_size, hidden, cosine, sine, pos_q, pos_k, spread, packed, w_out, w_gate, w_up, w_down, grad_out,
-    normed_o, query_o, kv_o, total_o, mixed_o, resid_o, normed_two_o, small_o, proj_o, out_o, big, big_two, go, relay,
+    ctx_size, hidden, cosine, sine, pos_q, pos_k, w_query, w_key, w_value, sides, w_out, w_gate, w_up, w_down, grad_out,
+    normed_o, query_o, kv_o, total_o, mixed_o, resid_o, normed_two_o, small_o, proj_o, out_o, big, big_two, go, relay, spread, norm_y,
     proj, out_w, source, source_two, query, kv, mixed,
-    load_sem, ag_send, ag_recv, core_send, core_recv, big_send, big_recv, two_recv, relay_recv, go_send, go_recv, kv_send, kv_recv, back_sem,
+    load_sem, ag_send, ag_recv, core_send, core_recv, big_send, big_recv, two_recv, relay_recv, go_send, go_recv, kv_send, kv_recv, back_sem, norm_sem,
 ):
     dp = lax.axis_index("dp")
     ctx = lax.axis_index("ctx")
     me = dp * ctx_size + ctx
-    shard, wide = packed.shape
+    shard, wide = w_out.shape[0], proj.shape[1]
     rows, model = hidden.shape
     one, two = big.shape[1] // 3, big_two.shape[1] // 3
     kv_width = KV_HEADS * HD
@@ -452,8 +458,11 @@
         pl.semaphore_signal(barrier, inc=1, device_id=at(flip(me, mask)), device_id_type=MESH)
 
     own = (
-        pltpu.make_async_copy(packed, proj.at[block(0)], load_sem.at[0]),
+        pltpu.make_async_copy(w_query, proj.at[block(0), pl.ds(0, q_width)], load_sem.at[0]),
         pltpu.make_async_copy(w_out, out_w.at[block(0)], load_sem.at[1]),
+        pltpu.make_async_copy(w_key, proj.at[block(0), pl.ds(q_width, kv_width)], load_sem.at[50]),
+        pltpu.make_async_copy(w_value, proj.at[block(0), pl.ds(q_width + kv_width, kv_width)], load_sem.at[51]),
+        pltpu.make_async_copy(sides, proj.at[block(0), pl.ds(proj_width, HD)], load_sem.at[52]),
     )
     for copy in own:
         copy.start()
@@ -557,6 +566,14 @@
 
     cut(4)
     over_z(0)
+
+    row = lax.broadcasted_iota(jnp.int32, (model, 2 * kv_width), 0)
+    col = lax.broadcasted_iota(jnp.int32, (model, 2 * kv_width), 1)
+    per = kv_width * shard // model
+    unit = (col % kv_width) // per * shard + col // kv_width * per + col % per
+    spread[...] = jnp.where(row == unit, 1.0, 0.0).astype(jnp.bfloat16)
+    own_pos = jnp.transpose(jnp.broadcast_to(pos_q[...].astype(jnp.float32), (HD, rows)))[:, :1]
+    signs = jnp.where(lax.broadcasted_iota(jnp.int32, (rows, HD), 1) < HD // 2, -1.0, 1.0)
 
     ag_pass(0, 1, 8, 16)
     ag_pass(0, 8, 16)
@@ -594,7 +611,7 @@
     values = hidden[...].astype(jnp.float32)
     factor = lax.rsqrt(jnp.mean(values * values, axis=-1, keepdims=True) + norm_eps)
     normed_o[...] = (values * factor * small[0:1]).astype(jnp.bfloat16)
-    cos, sin = cosine[...], sine[...]
+    cos, sin = cosine[...], sine[...] * signs
     raw = dot(normed_o[...], proj[:, q_width:proj_width], ((1,), (0,))) + kv_bias
     mine = block(0)
     for g in range(KV_HEADS):
@@ -670,7 +687,7 @@
         keys = kv[:, :, pl.ds(pl.multiple_of(g * HD, HD), HD)].reshape(ctx_size * rows, HD)
         vals = kv[:, :, pl.ds(pl.multiple_of(kv_width + g * HD, HD), HD)].reshape(ctx_size * rows, HD)
         scores = dot(query[n], keys, ((1,), (1,))) * HD ** (-0.5)
-        scores = jnp.where(pos_k[...] <= pos_q[...], scores, masked_fill)
+        scores = jnp.where(pos_k[...] <= own_pos, scores, masked_fill)
         top = jnp.max(scores, axis=-1, keepdims=True)
         expo = jnp.exp(scores - top)
         expo_sum = jnp.sum(expo, axis=-1, keepdims=True)
@@ -709,6 +726,8 @@
     resid_o[...] = resid
     factor = lax.rsqrt(jnp.mean(resid * resid, axis=-1, keepdims=True) + norm_eps)
     normed_two_o[...] = (resid * factor * small_o[2:3]).astype(jnp.bfloat16)
+    norm_push = remote(normed_two_o, norm_y, norm_sem.at[0], norm_sem.at[1], 16)
+    norm_push.start()
     go_push(1).wait_recv()
     go_push(3).start()
     go_core(1).start()
@@ -721,6 +740,7 @@
             cut_two(mask).wait_recv()
             two_over_z(mask).start()
 
+    norm_push.wait()
     for mask in (8, 12, 9, 24, 13, 28, 25, 29, 10, 14, 11, 26, 15, 30, 27, 31):
         big_pass(mask)
     go_push(3).wait_recv()
@@ -755,11 +775,14 @@
         copy.wait()
 
 
-def front_call(ctx_size, hidden, cosine, sine, pos_q, pos_k, spread, packed, w_out, w_gate, w_up, w_down, grad_out):
+def front_call(
+    ctx_size, hidden, cosine, sine, pos_q, pos_k, w_query, w_key, w_value, sides, w_out, w_gate, w_up, w_down, grad_out
+):
     rows, model = hidden.shape
-    shard, wide = packed.shape
+    shard = w_out.shape[0]
     kv_width = KV_HEADS * HD
     q_width = HEADS * HD
+    wide = q_width + 2 * kv_width + HD
     one, two = widths(w_gate.shape[1])
     low, full = jnp.bfloat16, jnp.float32
     vmem = pl.BlockSpec(memory_space=pltpu.VMEM)
@@ -779,12 +802,14 @@
         ((model, 3 * two), low, anywhere),
         ((8, rows, model), low, anywhere),
         ((8, shard, 3 * one), low, anywhere),
+        ((model, 2 * kv_width), low, vmem),
+        ((rows, model), low, anywhere),
     )
     sem = pltpu.SemaphoreType.DMA
     return pl.pallas_call(
         functools.partial(front_kernel, ctx_size),
         out_shape=tuple(jax.ShapeDtypeStruct(shape, kind) for shape, kind, _ in shapes),
-        in_specs=[vmem] * 6 + [anywhere] * 6,
+        in_specs=[vmem] * 5 + [anywhere] * 9,
         out_specs=tuple(spec for _, _, spec in shapes),
         scratch_shapes=[
             pltpu.VMEM((model, wide), low),
@@ -794,24 +819,24 @@
             pltpu.VMEM((HEADS, rows, HD), low),
             pltpu.VMEM((ctx_size, rows, 2 * kv_width), low),
             pltpu.VMEM((rows, q_width), low),
-            sem((50,)), sem((3,)), sem((3, 32)), sem((3, 4)), sem((3, 4)), sem((3,)), sem((32,)), sem((32,)), sem((8,)),
-            sem((7,)), sem((8,)), sem((4,)), sem((4,)), sem((6,)),
+            sem((53,)), sem((3,)), sem((3, 32)), sem((3, 4)), sem((3, 4)), sem((3,)), sem((32,)), sem((32,)), sem((8,)),
+            sem((7,)), sem((8,)), sem((4,)), sem((4,)), sem((6,)), sem((2,)),
         ],
         compiler_params=pltpu.CompilerParams(
             collective_id=0, has_side_effects=True, vmem_limit_bytes=56 << 20
         ),
         name="front",
-    )(hidden, cosine, sine, pos_q, pos_k, spread, packed, w_out, w_gate, w_up, w_down, grad_out)
+    )(hidden, cosine, sine, pos_q, pos_k, w_query, w_key, w_value, sides, w_out, w_gate, w_up, w_down, grad_out)
 
 
 def back_kernel(
     ctx_size, grad_two, resid, hidden, grad_out, normed, mixed, query, kv, total, cosine, sine, pos_q, pos_k, small, spread,
     proj, out_w, grads, grads_two, near, zin_first, r_part,
-    result_o, hidden_o, query_o, key_o, outw_o, gate_o, up_o, down_o, r_in, relay, relay_two,
+    hidden_o, query_o, key_o, outw_o, fin, fin_two, r_in, relay, relay_two,
     weight, turned, left_n, left_a, right_b, right_p, side, side_in, g_b, g_q, g_k,
     y_b, y_q, y_k, x_b, x_q, x_k, p_b, p_q, p_k, h_b, h_q, h_k,
-    own, far, zin, fin, own_two, far_two, zin_two, fin_two, r_mid, r_one, stage, heads_g, lse, dkv, kv_out, kv_p, kv_h, grad_resid,
-    load_sem, xs, xr, zs, zr, fs, fr, xs2, xr2, zs2, zr2, fs2, fr2, relay_recv, relay_send, cs, cr, rs, rr, ks, kr, st_sem, os, orr,
+    own, far, zin, own_two, far_two, zin_two, r_mid, r_one, heads_g, lse, dkv, kv_out, kv_p, kv_h, grad_resid,
+    load_sem, xs, xr, zs, zr, fs, fr, xs2, xr2, zs2, zr2, fs2, fr2, relay_recv, relay_send, cs, cr, rs, rr, ks, kr, os, orr, keep_sem,
 ):
     dp = lax.axis_index("dp")
     ctx = lax.axis_index("ctx")
@@ -820,8 +845,6 @@
     h, p = ctx // 2, ctx % 2
     rows, model = resid.shape
     shard = grads.shape[3]
-    hidden_units = gate_o.shape[1]
-    one, two = widths(hidden_units)
     kv_width = KV_HEADS * HD
     q_width = HEADS * HD
     groups = HEADS // KV_HEADS
@@ -909,6 +932,9 @@
     def fin_two_push(j):
         return remote(own_two.at[0, j], fin_two.at[j], fs2.at[j], fr2.at[j], mask_of(j))
 
+    keep_one = pltpu.make_async_copy(own.at[0], fin.at[0], keep_sem.at[0])
+    keep_two = pltpu.make_async_copy(own_two.at[0, 0], fin_two.at[0], keep_sem.at[1])
+
     def z_two_step(j):
         far_two_push(1, j).wait_recv()
         far_two[1, j] = (far_two[1, j].astype(full) + own_two[1, j].astype(full)).astype(low)
@@ -921,6 +947,8 @@
         own[j] = (own[j].astype(full) + far[j].astype(full) + zin[j].astype(full)).astype(low)
         if j:
             fin_push(j).start()
+        else:
+            keep_one.start()
 
     def total_two_step(j):
         far_two_push(0, j).wait_recv()
@@ -928,6 +956,8 @@
         own_two[0, j] = (own_two[0, j].astype(full) + far_two[0, j].astype(full) + zin_two[j].astype(full)).astype(low)
         if j:
             fin_two_push(j).start()
+        else:
+            keep_two.start()
 
     def r_push(o):
         src = r_one if o == 1 else r_part.at[o]
@@ -970,6 +1000,9 @@
     grad_attn = grad_resid[...].astype(low)
     transposed(grad_attn, left_a, 1)
     lse[...] = jnp.transpose(total[...])
+    signs = jnp.where(lax.broadcasted_iota(jnp.int32, (rows, HD), 1) < HD // 2, 1.0, -1.0)
+    sin_back = sine[...] * signs
+    key_pos = jnp.transpose(jnp.broadcast_to(pos_k[...], (HD, pos_k.shape[1])).astype(full))[:, :1]
     load_w.wait()
     for half in range(2):
         part = half * (q_width // 2)
@@ -1044,7 +1077,7 @@
         keys = kv[:, :, k_cols].reshape(ctx_size * rows, HD)
         vals = kv[:, :, v_cols].reshape(ctx_size * rows, HD)
         scores = dot(keys, query[n], ((1,), (1,))) * HD ** (-0.5)
-        scores = jnp.where(pos_k[...] <= pos_q[...], scores, masked_fill)
+        scores = jnp.where(key_pos <= pos_q[...].astype(full), scores, masked_fill)
         attend = jnp.exp(scores - lse[pl.ds(n, 1), :])
         grad_attend = dot(vals, heads_g[n], ((1,), (1,)))
         delta = jnp.sum(grad_attend * attend, axis=0, keepdims=True)
@@ -1052,7 +1085,7 @@
         dkv[:, k_cols] += dot(grad_scores, query[n], ((1,), (0,)))
         dkv[:, v_cols] += dot(attend.astype(low), heads_g[n], ((1,), (0,)))
         back = dot(grad_scores, keys, ((0,), (0,))) * HD ** (-0.5)
-        back = turn(back, cosine[...], -sine[...]).astype(low)
+        back = turn(back, cosine[...], sin_back).astype(low)
         right_p[pl.ds(0, rows), pl.ds(pl.multiple_of(n * HD, HD), HD)] = back
         return carry
 
@@ -1104,7 +1137,7 @@
     final = kv_out[2 * h + p].astype(full) + kv_h[...].astype(full)
     for g in range(KV_HEADS):
         right_p[pl.ds(0, rows), pl.ds(q_width + g * HD, HD)] = turn(
-            final[:, g * HD : (g + 1) * HD], cosine[...], -sine[...]
+            final[:, g * HD : (g + 1) * HD], cosine[...], sin_back
         ).astype(low)
     right_p[pl.ds(0, rows), pl.ds(q_width + kv_width, kv_width)] = final[:, kv_width:].astype(low)
     cross_kv = cross(
@@ -1143,48 +1176,6 @@
         ).astype(low)
         if i > 1:
             y_push(2, i - 2).start()
-    outs = (gate_o, up_o, down_o)
-    width = one + two
-    last = hidden_units - 7 * width - one
-
-    def piece(j):
-        mask = mask_of(j)
-        return either(y, mask // 16) * 4 + either(p, mask % 2) * 2 + either(c, (mask // 4) % 2)
-
-    def write(j, start, size, count):
-        for n in range(3):
-            pltpu.make_async_copy(
-                stage.at[j % 2, :, pl.ds(n * size, count)],
-                outs[n].at[:, pl.ds(pl.multiple_of(piece(j) * width + start, HD), count)], st_sem.at[j % 2],
-            ).start()
-
-    def settle(slot, count):
-        part = stage.at[slot, :, pl.ds(0, 3 * count)]
-        pltpu.make_async_copy(part, part, st_sem.at[slot]).wait()
-
-    def store(j):
-        if j:
-            fin_push(j).wait_recv()
-        if j > 1:
-            settle(j % 2, one)
-        stage[j % 2] = (fin[j] if j else own[0]).astype(full)
-        write(j, 0, one, one)
-
-    def settle_two(j):
-        pl.when(piece(j) < 7)(lambda: settle(j % 2, two))
-        pl.when(piece(j) == 7)(lambda: settle(j % 2, last))
-
-    def store_two(j):
-        if j:
-            fin_two_push(j).wait_recv()
-        if j > 1:
-            settle_two(j - 2)
-        else:
-            settle(j % 2, one)
-        stage[j % 2, :, pl.ds(0, 3 * two)] = (fin_two[j] if j else own_two[0, 0]).astype(full)
-        pl.when(piece(j) < 7)(lambda: write(j, one, two, two))
-        pl.when(piece(j) == 7)(lambda: write(j, one, two, last))
-
     y_push(0, 0).start()
     r_push(3).wait_recv()
     add(r_one, r_mid)
@@ -1200,39 +1191,23 @@
     x_pass(1)
     x_pass(2)
     r_push(2).start()
-    for j in range(4):
-        store(j)
     p_pass(1)
     p_pass(2)
     for j in range(8):
         total_two_step(j)
-    for j in range(4, 8):
-        store(j)
     x_pass(0)
     p_pass(0)
     h_pass(1, query_o)
     h_pass(2, key_o)
     h_pass(0, outw_o)
-    for j in range(8):
-        store_two(j)
-    settle_two(6)
-    settle_two(7)
+    for j in range(1, 8):
+        fin_push(j).wait_recv()
+        fin_two_push(j).wait_recv()
     for o in (1, 2):
         r_push(o).wait()
     r_push(3).wait_send()
-    tiles = (r_part.at[0], r_in.at[0], r_in.at[1])
-    loads = [
-        pltpu.make_async_copy(ref, weight.at[pl.ds(o * rows, rows), pl.ds(0, model)], os.at[o])
-        for o, ref in enumerate(tiles)
-    ]
-    for copy in loads:
-        copy.start()
-    for copy in loads:
-        copy.wait()
-    value = resid[...]
-    for o in range(3):
-        value = value + weight[pl.ds(o * rows, rows), pl.ds(0, model)].astype(full)
-    result_o[...] = value.astype(low)
+    keep_one.wait()
+    keep_two.wait()
 
     for j in range(8):
         far_push(j).wait_send()
@@ -1269,12 +1244,12 @@
 
 
 def back_call(
-    ctx_size, hidden_units, grad_two, resid, hidden, grad_out, normed, mixed, query, kv, total, cosine, sine, pos_q, pos_k,
+    ctx_size, grad_two, resid, hidden, grad_out, normed, mixed, query, kv, total, cosine, sine, pos_q, pos_k,
     small, spread, proj, out_w, grads, grads_two, near, zin_first, r_part,
 ):
     rows, model = resid.shape
     shard = grads.shape[3]
-    one, two = widths(hidden_units)
+    one, two = grads.shape[4] // 3, grads_two.shape[4] // 3
     kv_width = KV_HEADS * HD
     q_width = HEADS * HD
     k_cols = 2 * kv_width + HD
@@ -1283,14 +1258,12 @@
     vmem = pl.BlockSpec(memory_space=pltpu.VMEM)
     anywhere = pl.BlockSpec(memory_space=pl.ANY)
     shapes = (
-        ((rows, model), vmem, low),
         ((rows, model), vmem, full),
         ((shard, q_width), vmem, full),
         ((shard, k_cols), vmem, full),
         ((shard, q_width), vmem, full),
-        ((shard, hidden_units), anywhere, full),
-        ((shard, hidden_units), anywhere, full),
-        ((shard, hidden_units), anywhere, full),
+        ((8, shard, 3 * one), anywhere, low),
+        ((8, shard, 3 * two), anywhere, low),
         ((2, rows, model), anywhere, low),
         ((4, shard, 3 * one), anywhere, low),
         ((8, shard, 3 * two), anywhere, low),
@@ -1320,11 +1293,10 @@
             *each(span),
             *each(2, shard),
             *each(shard),
-            *([pltpu.VMEM((8, shard, 3 * one), low)] * 4),
+            *([pltpu.VMEM((8, shard, 3 * one), low)] * 3),
             *([pltpu.VMEM((2, 8, shard, 3 * two), low)] * 2),
-            *([pltpu.VMEM((8, shard, 3 * two), low)] * 2),
+            pltpu.VMEM((8, shard, 3 * two), low),
             *([pltpu.VMEM((rows, model), low)] * 2),
-            pltpu.VMEM((2, shard, 3 * one), full),
             pltpu.VMEM((HEADS, rows, HD), low),
             pltpu.VMEM((HD, rows), full),
             pltpu.VMEM((ctx_size * rows, 2 * kv_width), full),
@@ -1333,7 +1305,7 @@
             pltpu.VMEM((rows, 2 * kv_width), low),
             pltpu.VMEM((rows, model), full),
             sem((5,)), *([sem((8,))] * 6), *([sem((2, 8))] * 2), *([sem((8,))] * 4), sem((16,)), sem((16,)),
-            sem((4, 4)), sem((4, 4)), sem((3, 6)), sem((3, 6)), sem((3,)), sem((3,)), sem((2,)), sem((4,)), sem((4,)),
+            sem((4, 4)), sem((4, 4)), sem((3, 6)), sem((3, 6)), sem((3,)), sem((3,)), sem((4,)), sem((4,)), sem((2,)),
         ],
         compiler_params=pltpu.CompilerParams(
             collective_id=2, has_side_effects=True, vmem_limit_bytes=63 << 20
@@ -1343,6 +1315,104 @@
         grad_two, resid, hidden, grad_out, normed, mixed, query, kv, total, cosine, sine, pos_q, pos_k, small, spread,
         proj, out_w, grads, grads_two, near, zin_first, r_part,
     )
+
+
+def finish_kernel(
+    ctx_size, fin, fin_two, key, resid, r_part, r_in, hidden, query, outw,
+    result_o, hidden_o, attn_o, query_o, bias_q, key_o, bias_k, value_o, bias_v, outw_o, ffn_o, gate_o, up_o, down_o,
+    one_v, two_v, tiles, sems,
+):
+    dp = lax.axis_index("dp")
+    ctx = lax.axis_index("ctx")
+    y, c, p = dp // 4, dp % 2, ctx % 2
+    full = jnp.float32
+    rows, model = resid.shape
+    shard = key.shape[0]
+    one, two = fin.shape[2] // 3, fin_two.shape[2] // 3
+    width = one + two
+    kv_width = key_o.shape[1]
+    per = bias_k.shape[1]
+    moves = [
+        pltpu.make_async_copy(fin, one_v, sems.at[0]),
+        pltpu.make_async_copy(fin_two, two_v, sems.at[1]),
+        pltpu.make_async_copy(r_part.at[0], tiles.at[0], sems.at[2]),
+        pltpu.make_async_copy(r_in, tiles.at[pl.ds(1, 2)], sems.at[3]),
+    ]
+    for copy in moves:
+        copy.start()
+    hidden_o[...] = hidden[...]
+    query_o[...] = query[...]
+    outw_o[...] = outw[...]
+    key_o[...] = key[:, :kv_width]
+    value_o[...] = key[:, kv_width : 2 * kv_width]
+    side = jnp.transpose(key[:, 2 * kv_width :])
+    attn_o[...] = side[0:1]
+    bias_q[...] = side[1:2]
+    ffn_o[...] = side[2:3]
+    bias_k[...] = side[3:4, :per]
+    bias_v[...] = side[3:4, per : 2 * per]
+    moves[0].wait()
+    moves[1].wait()
+    last = gate_o.shape[1] - 7 * width - one
+    for j in range(8):
+        k = either(y, j // 4) * 4 + either(p, j % 2) * 2 + either(c, (j // 2) % 2)
+        for n, out in enumerate((gate_o, up_o, down_o)):
+            at = pl.multiple_of(k * width, HD)
+            out[:, pl.ds(at, one)] = one_v[j, :, n * one : (n + 1) * one].astype(full)
+
+            @pl.when(k < 7)
+            def _():
+                out[:, pl.ds(at + one, two)] = two_v[j, :, n * two : (n + 1) * two].astype(full)
+
+            @pl.when(k == 7)
+            def _():
+                out[:, pl.ds(7 * width + one, last)] = two_v[j, :, n * two : n * two + last].astype(full)
+
+    moves[2].wait()
+    moves[3].wait()
+    value = resid[...]
+    for o in range(3):
+        value = value + tiles[o].astype(full)
+    result_o[...] = value.astype(result_o.dtype)
+
+
+def finish_call(ctx_size, hidden_units, per, fin, fin_two, key, resid, r_part, r_in, hidden, query, outw):
+    rows, model = resid.shape
+    shard = key.shape[0]
+    kv_width = KV_HEADS * HD
+    low, full = jnp.bfloat16, jnp.float32
+    vmem = pl.BlockSpec(memory_space=pltpu.VMEM)
+    anywhere = pl.BlockSpec(memory_space=pl.ANY)
+    shapes = (
+        ((rows, model), low, vmem),
+        ((rows, model), full, vmem),
+        ((1, shard), full, vmem),
+        (query.shape, full, vmem),
+        ((1, shard), full, vmem),
+        ((shard, kv_width), full, vmem),
+        ((1, per), full, vmem),
+        ((shard, kv_width), full, vmem),
+        ((1, per), full, vmem),
+        (outw.shape, full, vmem),
+        ((1, shard), full, vmem),
+        ((shard, hidden_units), full, vmem),
+        ((shard, hidden_units), full, vmem),
+        ((shard, hidden_units), full, vmem),
+    )
+    return pl.pallas_call(
+        functools.partial(finish_kernel, ctx_size),
+        out_shape=tuple(jax.ShapeDtypeStruct(shape, kind) for shape, kind, _ in shapes),
+        in_specs=[anywhere, anywhere, vmem, vmem, anywhere, anywhere] + [vmem] * 3,
+        out_specs=tuple(spec for _, _, spec in shapes),
+        scratch_shapes=[
+            pltpu.VMEM(fin.shape, low),
+            pltpu.VMEM(fin_two.shape, low),
+            pltpu.VMEM((3, rows, model), low),
+            pltpu.SemaphoreType.DMA((4,)),
+        ],
+        compiler_params=pltpu.CompilerParams(vmem_limit_bytes=63 << 20),
+        name="finish",
+    )(fin, fin_two, key, resid, r_part, r_in, hidden, query, outw)
 
 
 def fits(mesh):
@@ -1381,43 +1451,42 @@
     places = jnp.arange(seq_len, dtype=jnp.int32)
     every_pos = jnp.repeat(span_order, span_len, axis=1) * span_len + places[None, :] % span_len
     local_pos = lax.dynamic_slice_in_dim(every_pos, ctx_rank * length, length, 1)
-    cosine, sine = angles_for(local_pos.reshape(row_count), HD)
-    cos_full = jnp.concatenate([cosine[:, 0], cosine[:, 0]], axis=1)
-    sin_full = jnp.concatenate([-sine[:, 0], sine[:, 0]], axis=1)
-
-    gains = jnp.stack([attn_gain, b_query, ffn_gain], axis=1)
+    freqs = rope_base ** (-((jnp.arange(HD) % (HD // 2)).astype(jnp.float32) * 2.0 / HD))
+    angles = local_pos.reshape(row_count, 1).astype(jnp.float32) * freqs[None, :]
+    cosine, sine = jnp.cos(angles), jnp.sin(angles)
+
     per = b_key.shape[0]
     pair = jnp.pad(jnp.concatenate([b_key, b_value]), (0, shard_rows - 2 * per))
-    packed = jnp.concatenate(
-        [w_query, w_key, w_value, gains, pair[:, None], jnp.zeros((shard_rows, 124), jnp.bfloat16)], axis=1
-    )
-    unit = jnp.arange(2 * kv_width)
-    unit = unit % kv_width // per * shard_rows + unit // kv_width * per + unit % per
-    spread = (jnp.arange(D)[:, None] == unit[None, :]).astype(jnp.bfloat16)
+    sides = jnp.pad(jnp.stack([attn_gain, b_query, ffn_gain, pair]), ((0, HD - 4), (0, 0))).T
     source = hidden.reshape(row_count, D)
-    normed, query_heads, key_value, log_total, mixed, resid, normed_two, small, proj_full, out_full, big, big_two, go_all, _ = front_call(
-        ctx_size, source, cos_full, sin_full, local_pos.reshape(length, 1), every_pos.reshape(1, seq_len), spread,
-        packed, w_out, w_gate, w_up, w_down, grad_out,
-    )
-    grad_two, r_part, grads, grads_two, near, zin, *_ = ffn_call(ctx_size, shard_rows, normed_two, go_all, big, big_two)
-    result, hidden_grad, w_query_grad, kv_sum, w_out_grad, w_gate_grad, w_up_grad, w_down_grad, *_ = back_call(
-        ctx_size, w_gate.shape[1], grad_two, resid, source, grad_out, normed, mixed, query_heads, key_value, log_total,
-        cos_full, sin_full, local_pos.reshape(1, length), every_pos.reshape(seq_len, 1), small, spread,
+    normed, query_heads, key_value, log_total, mixed, resid, normed_two, small, proj_full, out_full, big, big_two, go_all, _, spread, norm_y = front_call(
+        ctx_size, source, cosine, sine, local_pos, every_pos, w_query, w_key, w_value, sides, w_out, w_gate, w_up,
+        w_down, grad_out,
+    )
+    grad_two, r_part, grads, grads_two, near, zin, *_ = ffn_call(ctx_size, shard_rows, normed_two, norm_y, go_all, big, big_two)
+    hidden_back, query_sum, kv_sum, out_sum, fin, fin_two, r_in, *_ = back_call(
+        ctx_size, grad_two, resid, source, grad_out, normed, mixed, query_heads, key_value, log_total,
+        cosine, sine, local_pos, every_pos, small, spread,
         proj_full, out_full, grads, grads_two, near, zin, r_part,
     )
-    sides = kv_sum[:, 2 * kv_width : 2 * kv_width + 4]
+    (
+        result, hidden_grad, attn_gain_grad, w_query_grad, b_query_grad, w_key_grad, b_key_grad, w_value_grad,
+        b_value_grad, w_out_grad, ffn_gain_grad, w_gate_grad, w_up_grad, w_down_grad,
+    ) = finish_call(
+        ctx_size, w_gate.shape[1], per, fin, fin_two, kv_sum, resid, r_part, r_in, hidden_back, query_sum, out_sum
+    )
     return (
         result.reshape(batches, length, D),
         hidden_grad.reshape(batches, length, D),
-        sides[:, 0],
+        attn_gain_grad.reshape(shard_rows),
         w_query_grad,
-        sides[:, 1],
-        kv_sum[:, :kv_width],
-        sides[:per, 3],
-        kv_sum[:, kv_width : 2 * kv_width],
-        sides[per : 2 * per, 3],
+        b_query_grad.reshape(shard_rows),
+        w_key_grad,
+        b_key_grad.reshape(per),
+        w_value_grad,
+        b_value_grad.reshape(per),
         w_out_grad,
-        sides[:, 2],
+        ffn_gain_grad.reshape(shard_rows),
         w_gate_grad,
         w_up_grad,
         w_down_grad,

time: 462 us -> 442 us (0.957)
  local copies, waits for them, and re-layouts: 17 us -> 0.79 us
    unnamed x39 -> x2, local copies, waits for them, and re-layouts: 10 us -> 0.01 us
    pallas_call x0 -> x1, Pallas kernels: none -> 7.92 us  [finish_call(): pl.pallas_call(functools.partial(finish_kernel, ctx_size), out_shape=tupl...]
    pallas_call x1, Pallas kernels: 130 us -> 124 us  [ffn_call(): pl.pallas_call(functools.partial(ffn_kernel, ctx_size), out_shape=(jax.Sh...]
    pallas_call x1, Pallas kernels: 150 us -> 145 us  [back_call(): pl.pallas_call(functools.partial(back_kernel, ctx_size), out_shape=tuple(...]
where the time goes in v6:
time: 442 us; the launch traced here: 438 us
  Pallas kernels  432 us (98%)
    pallas_call x1, Pallas kernels, front_call(): pl.pallas_call(functools.partial(front_kernel, ctx_size), out_shape=tuple...  155 us
    pallas_call x1, Pallas kernels, back_call(): pl.pallas_call(functools.partial(back_kernel, ctx_size), out_shape=tuple(...  145 us
    pallas_call x1, Pallas kernels, ffn_call(): pl.pallas_call(functools.partial(ffn_kernel, ctx_size), out_shape=(jax.Sh...  124 us

profile of v6, /device:TPU:0, one launch (start us, length us, event | category | flops | bytes accessed | tf_op | source)
XLA Modules:
  0.0 437.7 jit_solution(1006520720436943210)
XLA Ops:
  0.6 0.7 multiply_bitcast_fusion
  1.3 0.7 fusion.6
  2.1 0.7 pad_maximum_fusion
  2.8 0.1 broadcast_in_dim.2
  2.8 0.0 copy-start
  2.9 0.6 fusion.7
  3.4 0.1 copy.33
  3.5 0.6 pad_bitcast_fusion.sides
  4.1 1.2 multiply_sine_fusion
  5.4 0.0 copy-done
  5.4 155.3 %front.1 = (bf16[256,1536]{1,0:T(8,128)(2,1)}, bf16[12,256,128]{2,1,0:T(8,128)(2,1)}, bf16[4,256,512]{2,1,0:T(8,128)(2,1)}, f32[256,128]{1,0:T(8,128)}, bf16[256...) custom-call(bf16[256,1536]{1,0:T(8,128)(2,1)} %bitcast.20, ...), custom_call_target="tpu_custom_call" | custom-call | tf_op jit(solution)/shard_map/front/pallas_call | solution.py:809
  160.7 124.2 %ffn.1 = (f32[256,1536]{1,0:T(8,128)}, bf16[4,256,1536]{2,1,0:T(8,128)(2,1)}, bf16[2,2,8,48,2304]{4,3,2,1,0:T(8,128)(2,1)}, bf16[2,2,8,48,1152]{4,3,2,1,0:T(8,12...) custom-call(bf16[256,1536]{1,0:T(8,128)(2,1)} %get-tuple-element.56.n_own, ...), custom_call_target="tpu_custom_call" | custom-call | tf_op jit(solution)/shard_map/ffn/pallas_call | solution.py:383
  284.9 144.6 %back.1 = (f32[256,1536]{1,0:T(8,128)}, f32[48,1536]{1,0:T(8,128)}, f32[48,640]{1,0:T(8,128)}, f32[48,1536]{1,0:T(8,128)}, bf16[8,48,2304]{2,1,0:T(8,128)(2,1)},...) custom-call(f32[256,1536]{1,0:T(8,128)} %get-tuple-element.61.grad_t, ...), custom_call_target="tpu_custom_call" | custom-call | tf_op jit(solution)/shard_map/back/pallas_call | solution.py:1277
  429.5 7.9 %finish.1 = (bf16[256,1536]{1,0:T(8,128)(2,1)}, f32[256,1536]{1,0:T(8,128)}, f32[1,48]{1,0:T(1,128)}, f32[48,1536]{1,0:T(8,128)}, f32[1,48]{1,0:T(1,128)}, /*ind...) custom-call(bf16[8,48,2304]{2,1,0:T(8,128)(2,1)} %get-tuple-element., ...), custom_call_target="tpu_custom_call" | custom-call | tf_op jit(solution)/shard_map/finish/pallas_call | solution.py:1402
  (2 shorter events, 0.0 us)
Async XLA Ops:
  2.8 2.5 copy-start

commit v7 on v6

--- a/solution.py
+++ b/solution.py
@@ -1,4 +1,5 @@
 import functools
+import math
 
 import jax
 import jax.numpy as jnp
@@ -421,8 +422,8 @@
 
 
 def front_kernel(
-    ctx_size, hidden, cosine, sine, pos_q, pos_k, w_query, w_key, w_value, sides, w_out, w_gate, w_up, w_down, grad_out,
-    normed_o, query_o, kv_o, total_o, mixed_o, resid_o, normed_two_o, small_o, proj_o, out_o, big, big_two, go, relay, spread, norm_y,
+    ctx_size, span, hidden, sides, w_query, w_key, w_value, w_out, w_gate, w_up, w_down, grad_out,
+    normed_o, query_o, kv_o, total_o, mixed_o, resid_o, normed_two_o, small_o, proj_o, out_o, big, big_two, go, relay, spread, norm_y, cosine, sine, pos_k, pos_q,
     proj, out_w, source, source_two, query, kv, mixed,
     load_sem, ag_send, ag_recv, core_send, core_recv, big_send, big_recv, two_recv, relay_recv, go_send, go_recv, kv_send, kv_recv, back_sem, norm_sem,
 ):
@@ -572,8 +573,18 @@
     per = kv_width * shard // model
     unit = (col % kv_width) // per * shard + col // kv_width * per + col % per
     spread[...] = jnp.where(row == unit, 1.0, 0.0).astype(jnp.bfloat16)
-    own_pos = jnp.transpose(jnp.broadcast_to(pos_q[...].astype(jnp.float32), (HD, rows)))[:, :1]
-    signs = jnp.where(lax.broadcasted_iota(jnp.int32, (rows, HD), 1) < HD // 2, -1.0, 1.0)
+    length = rows // 2
+    for j in range(2 * ctx_size):
+        lane = lax.broadcasted_iota(jnp.int32, (1, length), 1)
+        pos_k[:, pl.ds(j * length, length)] = (span[0, j] * length + lane).astype(jnp.float32)
+    pos_q[...] = pos_k[:, pl.ds(pl.multiple_of(ctx * rows, rows), rows)]
+    own_pos = jnp.transpose(jnp.broadcast_to(pos_q[...], (HD, rows)))
+    lane = lax.broadcasted_iota(jnp.int32, (rows, HD), 1)
+    turns = (lane % (HD // 2)).astype(jnp.float32) * (2.0 / HD)
+    angles = own_pos * jnp.exp(turns * -math.log(rope_base))
+    cosine[...] = jnp.cos(angles)
+    sine[...] = jnp.sin(angles) * jnp.where(lane < HD // 2, -1.0, 1.0)
+    own_pos = own_pos[:, :1]
 
     ag_pass(0, 1, 8, 16)
     ag_pass(0, 8, 16)
@@ -611,7 +622,7 @@
     values = hidden[...].astype(jnp.float32)
     factor = lax.rsqrt(jnp.mean(values * values, axis=-1, keepdims=True) + norm_eps)
     normed_o[...] = (values * factor * small[0:1]).astype(jnp.bfloat16)
-    cos, sin = cosine[...], sine[...] * signs
+    cos, sin = cosine[...], sine[...]
     raw = dot(normed_o[...], proj[:, q_width:proj_width], ((1,), (0,))) + kv_bias
     mine = block(0)
     for g in range(KV_HEADS):
@@ -776,7 +787,7 @@
 
 
 def front_call(
-    ctx_size, hidden, cosine, sine, pos_q, pos_k, w_query, w_key, w_value, sides, w_out, w_gate, w_up, w_down, grad_out
+    ctx_size, span, hidden, sides, w_query, w_key, w_value, w_out, w_gate, w_up, w_down, grad_out
 ):
     rows, model = hidden.shape
     shard = w_out.shape[0]
@@ -804,12 +815,16 @@
         ((8, shard, 3 * one), low, anywhere),
         ((model, 2 * kv_width), low, vmem),
         ((rows, model), low, anywhere),
+        ((rows, HD), full, vmem),
+        ((rows, HD), full, vmem),
+        ((1, ctx_size * rows), full, vmem),
+        ((1, rows), full, vmem),
     )
     sem = pltpu.SemaphoreType.DMA
     return pl.pallas_call(
         functools.partial(front_kernel, ctx_size),
         out_shape=tuple(jax.ShapeDtypeStruct(shape, kind) for shape, kind, _ in shapes),
-        in_specs=[vmem] * 5 + [anywhere] * 9,
+        in_specs=[pl.BlockSpec(memory_space=pltpu.SMEM), vmem] + [anywhere] * 9,
         out_specs=tuple(spec for _, _, spec in shapes),
         scratch_shapes=[
             pltpu.VMEM((model, wide), low),
@@ -826,7 +841,7 @@
             collective_id=0, has_side_effects=True, vmem_limit_bytes=56 << 20
         ),
         name="front",
-    )(hidden, cosine, sine, pos_q, pos_k, w_query, w_key, w_value, sides, w_out, w_gate, w_up, w_down, grad_out)
+    )(span, hidden, sides, w_query, w_key, w_value, w_out, w_gate, w_up, w_down, grad_out)
 
 
 def back_kernel(
@@ -1000,9 +1015,8 @@
     grad_attn = grad_resid[...].astype(low)
     transposed(grad_attn, left_a, 1)
     lse[...] = jnp.transpose(total[...])
-    signs = jnp.where(lax.broadcasted_iota(jnp.int32, (rows, HD), 1) < HD // 2, 1.0, -1.0)
-    sin_back = sine[...] * signs
-    key_pos = jnp.transpose(jnp.broadcast_to(pos_k[...], (HD, pos_k.shape[1])).astype(full))[:, :1]
+    sin_back = -sine[...]
+    key_pos = jnp.transpose(jnp.broadcast_to(pos_k[...], (HD, pos_k.shape[1])))[:, :1]
     load_w.wait()
     for half in range(2):
         part = half * (q_width // 2)
@@ -1077,7 +1091,7 @@
         keys = kv[:, :, k_cols].reshape(ctx_size * rows, HD)
         vals = kv[:, :, v_cols].reshape(ctx_size * rows, HD)
         scores = dot(keys, query[n], ((1,), (1,))) * HD ** (-0.5)
-        scores = jnp.where(key_pos <= pos_q[...].astype(full), scores, masked_fill)
+        scores = jnp.where(key_pos <= pos_q[...], scores, masked_fill)
         attend = jnp.exp(scores - lse[pl.ds(n, 1), :])
         grad_attend = dot(vals, heads_g[n], ((1,), (1,)))
         delta = jnp.sum(grad_attend * attend, axis=0, keepdims=True)
@@ -1320,7 +1334,7 @@
 def finish_kernel(
     ctx_size, fin, fin_two, key, resid, r_part, r_in, hidden, query, outw,
     result_o, hidden_o, attn_o, query_o, bias_q, key_o, bias_k, value_o, bias_v, outw_o, ffn_o, gate_o, up_o, down_o,
-    one_v, two_v, tiles, sems,
+    one_v, two_v, tiles, full_v, sems,
 ):
     dp = lax.axis_index("dp")
     ctx = lax.axis_index("ctx")
@@ -1358,15 +1372,19 @@
         k = either(y, j // 4) * 4 + either(p, j % 2) * 2 + either(c, (j // 2) % 2)
         for n, out in enumerate((gate_o, up_o, down_o)):
             at = pl.multiple_of(k * width, HD)
-            out[:, pl.ds(at, one)] = one_v[j, :, n * one : (n + 1) * one].astype(full)
+            full_v[n, :, pl.ds(at, one)] = one_v[j, :, n * one : (n + 1) * one].astype(full)
 
             @pl.when(k < 7)
             def _():
-                out[:, pl.ds(at + one, two)] = two_v[j, :, n * two : (n + 1) * two].astype(full)
+                whole = pl.ds(at, width)
+                full_v[n, :, pl.ds(at + one, two)] = two_v[j, :, n * two : (n + 1) * two].astype(full)
+                pltpu.make_async_copy(full_v.at[n, :, whole], out.at[:, whole], sems.at[4]).start()
 
             @pl.when(k == 7)
             def _():
-                out[:, pl.ds(7 * width + one, last)] = two_v[j, :, n * two : n * two + last].astype(full)
+                whole = pl.ds(7 * width, one + last)
+                full_v[n, :, pl.ds(7 * width + one, last)] = two_v[j, :, n * two : n * two + last].astype(full)
+                pltpu.make_async_copy(full_v.at[n, :, whole], out.at[:, whole], sems.at[4]).start()
 
     moves[2].wait()
     moves[3].wait()
@@ -1374,6 +1392,7 @@
     for o in range(3):
         value = value + tiles[o].astype(full)
     result_o[...] = value.astype(result_o.dtype)
+    pltpu.make_async_copy(full_v, full_v, sems.at[4]).wait()
 
 
 def finish_call(ctx_size, hidden_units, per, fin, fin_two, key, resid, r_part, r_in, hidden, query, outw):
@@ -1395,9 +1414,9 @@
         ((1, per), full, vmem),
         (outw.shape, full, vmem),
         ((1, shard), full, vmem),
-        ((shard, hidden_units), full, vmem),
-        ((shard, hidden_units), full, vmem),
-        ((shard, hidden_units), full, vmem),
+        ((shard, hidden_units), full, anywhere),
+        ((shard, hidden_units), full, anywhere),
+        ((shard, hidden_units), full, anywhere),
     )
     return pl.pallas_call(
         functools.partial(finish_kernel, ctx_size),
@@ -1408,7 +1427,8 @@
             pltpu.VMEM(fin.shape, low),
             pltpu.VMEM(fin_two.shape, low),
             pltpu.VMEM((3, rows, model), low),
-            pltpu.SemaphoreType.DMA((4,)),
+            pltpu.VMEM((3, shard, hidden_units), full),
+            pltpu.SemaphoreType.DMA((5,)),
         ],
         compiler_params=pltpu.CompilerParams(vmem_limit_bytes=63 << 20),
         name="finish",
@@ -1437,36 +1457,25 @@
     w_down,
 ):
     ctx_size = lax.axis_size("ctx")
-    ctx_rank = lax.axis_index("ctx")
     batches = hidden.shape[0]
     length = hidden.shape[1]
-    span_len = length // 2
-    seq_len = length * ctx_size
     row_count = batches * length
     shard_rows = w_query.shape[0]
     kv_width = KV_HEADS * HD
     q_width = HEADS * HD
 
     grad_out = cotangent.reshape(row_count, D)
-    places = jnp.arange(seq_len, dtype=jnp.int32)
-    every_pos = jnp.repeat(span_order, span_len, axis=1) * span_len + places[None, :] % span_len
-    local_pos = lax.dynamic_slice_in_dim(every_pos, ctx_rank * length, length, 1)
-    freqs = rope_base ** (-((jnp.arange(HD) % (HD // 2)).astype(jnp.float32) * 2.0 / HD))
-    angles = local_pos.reshape(row_count, 1).astype(jnp.float32) * freqs[None, :]
-    cosine, sine = jnp.cos(angles), jnp.sin(angles)
-
     per = b_key.shape[0]
     pair = jnp.pad(jnp.concatenate([b_key, b_value]), (0, shard_rows - 2 * per))
     sides = jnp.pad(jnp.stack([attn_gain, b_query, ffn_gain, pair]), ((0, HD - 4), (0, 0))).T
     source = hidden.reshape(row_count, D)
-    normed, query_heads, key_value, log_total, mixed, resid, normed_two, small, proj_full, out_full, big, big_two, go_all, _, spread, norm_y = front_call(
-        ctx_size, source, cosine, sine, local_pos, every_pos, w_query, w_key, w_value, sides, w_out, w_gate, w_up,
-        w_down, grad_out,
+    normed, query_heads, key_value, log_total, mixed, resid, normed_two, small, proj_full, out_full, big, big_two, go_all, _, spread, norm_y, *turns = front_call(
+        ctx_size, span_order, source, sides, w_query, w_key, w_value, w_out, w_gate, w_up, w_down, grad_out
     )
     grad_two, r_part, grads, grads_two, near, zin, *_ = ffn_call(ctx_size, shard_rows, normed_two, norm_y, go_all, big, big_two)
     hidden_back, query_sum, kv_sum, out_sum, fin, fin_two, r_in, *_ = back_call(
         ctx_size, grad_two, resid, source, grad_out, normed, mixed, query_heads, key_value, log_total,
-        cosine, sine, local_pos, every_pos, small, spread,
+        turns[0], turns[1], turns[3], turns[2], small, spread,
         proj_full, out_full, grads, grads_two, near, zin, r_part,
     )
     (

time: 442 us -> 439 us (level)
  no operation moved by 1% of the time
where the time goes in v7:
time: 439 us; the launch traced here: 435 us
  Pallas kernels  432 us (98%)
    pallas_call x1, Pallas kernels, front_call(): pl.pallas_call(functools.partial(front_kernel, ctx_size), out_shape=tuple...  154 us
    pallas_call x1, Pallas kernels, back_call(): pl.pallas_call(functools.partial(back_kernel, ctx_size), out_shape=tuple(...  145 us
    pallas_call x1, Pallas kernels, ffn_call(): pl.pallas_call(functools.partial(ffn_kernel, ctx_size), out_shape=(jax.Sh...  125 us

profile of v7, /device:TPU:0, one launch (start us, length us, event | category | flops | bytes accessed | tf_op | source)
XLA Modules:
  0.0 435.0 jit_solution(982205286776188765)
XLA Ops:
  0.6 0.7 fusion.1
  1.4 0.7 pad_maximum_fusion
  2.1 0.1 copy.33
  2.2 0.6 pad_bitcast_fusion.sides
  2.8 154.3 %front.1 = (bf16[256,1536]{1,0:T(8,128)(2,1)}, bf16[12,256,128]{2,1,0:T(8,128)(2,1)}, bf16[4,256,512]{2,1,0:T(8,128)(2,1)}, f32[256,128]{1,0:T(8,128)}, bf16[256...) custom-call(s32[1,8]{1,0:T(1,128)} %span.1, ...), custom_call_target="tpu_custom_call" | custom-call | tf_op jit(solution)/shard_map/front/pallas_call | solution.py:824
  157.1 125.2 %ffn.1 = (f32[256,1536]{1,0:T(8,128)}, bf16[4,256,1536]{2,1,0:T(8,128)(2,1)}, bf16[2,2,8,48,2304]{4,3,2,1,0:T(8,128)(2,1)}, bf16[2,2,8,48,1152]{4,3,2,1,0:T(8,12...) custom-call(bf16[256,1536]{1,0:T(8,128)(2,1)} %get-tuple-element.60.n_own, ...), custom_call_target="tpu_custom_call" | custom-call | tf_op jit(solution)/shard_map/ffn/pallas_call | solution.py:384
  282.4 144.6 %back.1 = (f32[256,1536]{1,0:T(8,128)}, f32[48,1536]{1,0:T(8,128)}, f32[48,640]{1,0:T(8,128)}, f32[48,1536]{1,0:T(8,128)}, bf16[8,48,2304]{2,1,0:T(8,128)(2,1)},...) custom-call(f32[256,1536]{1,0:T(8,128)} %get-tuple-element.65.grad_t, ...), custom_call_target="tpu_custom_call" | custom-call | tf_op jit(solution)/shard_map/back/pallas_call | solution.py:1291
  426.9 7.8 %finish.1 = (bf16[256,1536]{1,0:T(8,128)(2,1)}, f32[256,1536]{1,0:T(8,128)}, f32[1,48]{1,0:T(1,128)}, f32[48,1536]{1,0:T(8,128)}, f32[1,48]{1,0:T(1,128)}, /*ind...) custom-call(bf16[8,48,2304]{2,1,0:T(8,128)(2,1)} %get-tuple-element., ...), custom_call_target="tpu_custom_call" | custom-call | tf_op jit(solution)/shard_map/finish/pallas_call | solution.py:1421

commit v8 on v7

--- a/solution.py
+++ b/solution.py
@@ -463,10 +463,11 @@
         pltpu.make_async_copy(w_out, out_w.at[block(0)], load_sem.at[1]),
         pltpu.make_async_copy(w_key, proj.at[block(0), pl.ds(q_width, kv_width)], load_sem.at[50]),
         pltpu.make_async_copy(w_value, proj.at[block(0), pl.ds(q_width + kv_width, kv_width)], load_sem.at[51]),
-        pltpu.make_async_copy(sides, proj.at[block(0), pl.ds(proj_width, HD)], load_sem.at[52]),
     )
     for copy in own:
         copy.start()
+    table = jnp.concatenate([sides[...].astype(jnp.float32), jnp.zeros((HD - 8, shard), jnp.float32)], axis=0)
+    proj[block(0), pl.ds(proj_width, HD)] = jnp.transpose(table).astype(jnp.bfloat16)
     hidden_units = w_gate.shape[1]
     cuts = []
     for k in range(8):
@@ -628,11 +629,9 @@
     for g in range(KV_HEADS):
         kv[ctx, :, pl.ds(g * HD, HD)] = turn(raw[:, g * HD : (g + 1) * HD], cos, sin).astype(jnp.bfloat16)
     kv[ctx, :, pl.ds(kv_width, kv_width)] = raw[:, kv_width:].astype(jnp.bfloat16)
-
     def kv_push(mask, over):
         slot = flip(ctx, mask)
         return remote(kv.at[slot], kv.at[slot], kv_send.at[mask | over], kv_recv.at[mask | over], over)
-
     kv_push(0, 2).start()
     kv_push(0, 1).start()
     ag_pass(1, 10, 16)
@@ -640,13 +639,15 @@
     group(1, 8).start()
     big_pass(1, 2, 8)
     ag_pass(2, 1, 16, 8)
+    relay_pass(1)
     ag_pass(2, 2, 1, 16, 8)
-    for mask in (16, 20, 17, 21):
-        cut(mask)
+    cut(16)
+    cut(20)
+    cut(17)
+    cut(21)
     kv_push(0, 2).wait_recv()
     kv_push(2, 1).start()
     big_pass(5, 2, 8)
-    relay_pass(1)
     for mask in (16, 17, 18, 19):
         ag_pass(1, mask)
     group(1, 16).start()
@@ -672,27 +673,23 @@
     big_pass(17, 2, 8)
     big_pass(21, 2, 8)
     relay_pass(20)
-
     def go_core(o):
         src = go.at[2 * o] if o else grad_out
         return remote(src, go.at[2 * o + 1], go_send.at[3 + o], go_recv.at[2 * o + 1], 4)
-
     def go_push(o):
         src = go.at[2] if o == 3 else grad_out
         return remote(src, go.at[2 * o], go_send.at[o - 1], go_recv.at[2 * o], (0, 1, 16, 16)[o])
-
     go_push(2).start()
     go_push(1).start()
     go_core(0).start()
-    for mask in (2, 6):
-        big_pass(mask, 8)
+    big_pass(2, 8)
+    big_pass(6, 8)
     kv_push(0, 1).wait_recv()
     kv_push(2, 1).wait_recv()
     query_back = pltpu.make_async_copy(query, query_o, back_sem.at[0])
     query_back.start()
     kv_back = pltpu.make_async_copy(kv, kv_o, back_sem.at[1])
     kv_back.start()
-
     def head(n, carry):
         g = n // groups
         keys = kv[:, :, pl.ds(pl.multiple_of(g * HD, HD), HD)].reshape(ctx_size * rows, HD)
@@ -707,28 +704,31 @@
         lane = lax.broadcasted_iota(jnp.int32, (rows, HD), 1)
         total_o[...] = jnp.where(lane == n, top + jnp.log(expo_sum), total_o[...])
         return carry
-
     total_o[...] = jnp.zeros_like(total_o)
     lax.fori_loop(0, HEADS, head, 0)
     own_go = pltpu.make_async_copy(grad_out, go.at[0], load_sem.at[2])
     own_go.start()
+    big_pass(3, 8)
     mixed_back = pltpu.make_async_copy(mixed, mixed_o, back_sem.at[2])
     mixed_back.start()
-    relay_pass(17, 21)
-
+    relay_pass(17)
+    relay_pass(21)
     def two_over_z(mask):
         src = big_two.at[block(mask)] if mask else source_two.at[column(0)]
         return remote(src, big_two.at[block(mask)], big_send.at[1], two_recv.at[mask | 2], 2)
-
-    for mask in (3, 7):
-        big_pass(mask, 8)
-    for mask in (4, 1, 5, 16, 20, 17, 21):
-        cut_two(mask).start()
+    big_pass(7, 8)
+    cut_two(1).start()
+    cut_two(5).start()
+    cut_two(16).start()
+    cut_two(20).start()
+    cut_two(17).start()
+    cut_two(21).start()
     for n, mask in enumerate((8, 9, 10, 11, 24, 25, 26, 27)):
         ag_pass(2, mask)
         if n % 4 == 3:
             group(2, mask & 24).start()
     group_wait(2)
+    cut_two(4).start()
     proj_back = pltpu.make_async_copy(proj, proj_o, back_sem.at[4])
     proj_back.start()
     out_back = pltpu.make_async_copy(out_w, out_o, back_sem.at[5])
@@ -824,7 +824,7 @@
     return pl.pallas_call(
         functools.partial(front_kernel, ctx_size),
         out_shape=tuple(jax.ShapeDtypeStruct(shape, kind) for shape, kind, _ in shapes),
-        in_specs=[pl.BlockSpec(memory_space=pltpu.SMEM), vmem] + [anywhere] * 9,
+        in_specs=[pl.BlockSpec(memory_space=pltpu.SMEM), vmem, vmem] + [anywhere] * 8,
         out_specs=tuple(spec for _, _, spec in shapes),
         scratch_shapes=[
             pltpu.VMEM((model, wide), low),
@@ -834,7 +834,7 @@
             pltpu.VMEM((HEADS, rows, HD), low),
             pltpu.VMEM((ctx_size, rows, 2 * kv_width), low),
             pltpu.VMEM((rows, q_width), low),
-            sem((53,)), sem((3,)), sem((3, 32)), sem((3, 4)), sem((3, 4)), sem((3,)), sem((32,)), sem((32,)), sem((8,)),
+            sem((52,)), sem((3,)), sem((3, 32)), sem((3, 4)), sem((3, 4)), sem((3,)), sem((32,)), sem((32,)), sem((8,)),
             sem((7,)), sem((8,)), sem((4,)), sem((4,)), sem((6,)), sem((2,)),
         ],
         compiler_params=pltpu.CompilerParams(
@@ -1194,26 +1194,45 @@
     r_push(3).wait_recv()
     add(r_one, r_mid)
     r_push(1).start()
-    relay_two_pass(3, 4, 5, 6, 7)
-    for j in range(4, 8):
-        total_step(j)
+    relay_two_pass(3)
+    relay_two_pass(4)
+    relay_two_pass(5)
+    relay_two_pass(6)
+    relay_two_pass(7)
+    total_step(4)
+    total_step(5)
+    total_step(6)
+    total_step(7)
     y_pass(1)
     y_pass(2)
-    for j in range(8):
-        far_two_push(0, j).start()
+    far_two_push(0, 2).start()
+    far_two_push(0, 0).start()
+    far_two_push(0, 3).start()
+    far_two_push(0, 1).start()
+    far_two_push(0, 4).start()
+    far_two_push(0, 5).start()
+    far_two_push(0, 6).start()
+    total_two_step(1)
+    far_two_push(0, 7).start()
     y_pass(0)
     x_pass(1)
     x_pass(2)
     r_push(2).start()
     p_pass(1)
     p_pass(2)
-    for j in range(8):
-        total_two_step(j)
+    total_two_step(0)
+    total_two_step(2)
+    total_two_step(4)
+    total_two_step(5)
+    total_two_step(6)
+    total_two_step(7)
     x_pass(0)
     p_pass(0)
     h_pass(1, query_o)
     h_pass(2, key_o)
+    total_two_step(3)
     h_pass(0, outw_o)
+
     for j in range(1, 8):
         fin_push(j).wait_recv()
         fin_two_push(j).wait_recv()
@@ -1466,8 +1485,8 @@
 
     grad_out = cotangent.reshape(row_count, D)
     per = b_key.shape[0]
-    pair = jnp.pad(jnp.concatenate([b_key, b_value]), (0, shard_rows - 2 * per))
-    sides = jnp.pad(jnp.stack([attn_gain, b_query, ffn_gain, pair]), ((0, HD - 4), (0, 0))).T
+    flat = jnp.concatenate([attn_gain, b_query, ffn_gain, b_key, b_value])
+    sides = jnp.pad(flat, (0, 8 * shard_rows - flat.shape[0])).reshape(8, shard_rows)
     source = hidden.reshape(row_count, D)
     normed, query_heads, key_value, log_total, mixed, resid, normed_two, small, proj_full, out_full, big, big_two, go_all, _, spread, norm_y, *turns = front_call(
         ctx_size, span_order, source, sides, w_query, w_key, w_value, w_out, w_gate, w_up, w_down, grad_out

time: 439 us -> 439 us (level)
  no operation moved by 1% of the time
where the time goes in v8:
time: 439 us; the launch traced here: 435 us
  Pallas kernels  430 us (98%)
    pallas_call x1, Pallas kernels, front_call(): pl.pallas_call(functools.partial(front_kernel, ctx_size), out_shape=tuple...  157 us
    pallas_call x1, Pallas kernels, back_call(): pl.pallas_call(functools.partial(back_kernel, ctx_size), out_shape=tuple(...  142 us
    pallas_call x1, Pallas kernels, ffn_call(): pl.pallas_call(functools.partial(ffn_kernel, ctx_size), out_shape=(jax.Sh...  123 us

profile of v8, /device:TPU:0, one launch (start us, length us, event | category | flops | bytes accessed | tf_op | source)
XLA Modules:
  0.0 434.8 jit_solution(11440598417604318768)
XLA Ops:
  0.6 3.4 concatenate.3
  4.1 0.7 reshape.59.sides
  4.8 156.8 %front.1 = (bf16[256,1536]{1,0:T(8,128)(2,1)}, bf16[12,256,128]{2,1,0:T(8,128)(2,1)}, bf16[4,256,512]{2,1,0:T(8,128)(2,1)}, f32[256,128]{1,0:T(8,128)}, bf16[256...) custom-call(s32[1,8]{1,0:T(1,128)} %span.1, ...), custom_call_target="tpu_custom_call" | custom-call | tf_op jit(solution)/shard_map/front/pallas_call | solution.py:824
  161.6 122.7 %ffn.1 = (f32[256,1536]{1,0:T(8,128)}, bf16[4,256,1536]{2,1,0:T(8,128)(2,1)}, bf16[2,2,8,48,2304]{4,3,2,1,0:T(8,128)(2,1)}, bf16[2,2,8,48,1152]{4,3,2,1,0:T(8,12...) custom-call(bf16[256,1536]{1,0:T(8,128)(2,1)} %get-tuple-element.60.n_own, ...), custom_call_target="tpu_custom_call" | custom-call | tf_op jit(solution)/shard_map/ffn/pallas_call | solution.py:384
  284.3 142.4 %back.1 = (f32[256,1536]{1,0:T(8,128)}, f32[48,1536]{1,0:T(8,128)}, f32[48,640]{1,0:T(8,128)}, f32[48,1536]{1,0:T(8,128)}, bf16[8,48,2304]{2,1,0:T(8,128)(2,1)},...) custom-call(f32[256,1536]{1,0:T(8,128)} %get-tuple-element.65.grad_t, ...), custom_call_target="tpu_custom_call" | custom-call | tf_op jit(solution)/shard_map/back/pallas_call | solution.py:1310
  426.7 7.8 %finish.1 = (bf16[256,1536]{1,0:T(8,128)(2,1)}, f32[256,1536]{1,0:T(8,128)}, f32[1,48]{1,0:T(1,128)}, f32[48,1536]{1,0:T(8,128)}, f32[1,48]{1,0:T(1,128)}, /*ind...) custom-call(bf16[8,48,2304]{2,1,0:T(8,128)(2,1)} %get-tuple-element., ...), custom_call_target="tpu_custom_call" | custom-call | tf_op jit(solution)/shard_map/finish/pallas_call | solution.py:1440
  (1 shorter events, 0.0 us)

commit v9 on v8

--- a/solution.py
+++ b/solution.py
@@ -463,11 +463,10 @@
         pltpu.make_async_copy(w_out, out_w.at[block(0)], load_sem.at[1]),
         pltpu.make_async_copy(w_key, proj.at[block(0), pl.ds(q_width, kv_width)], load_sem.at[50]),
         pltpu.make_async_copy(w_value, proj.at[block(0), pl.ds(q_width + kv_width, kv_width)], load_sem.at[51]),
+        pltpu.make_async_copy(sides, proj.at[block(0), pl.ds(proj_width, HD)], load_sem.at[52]),
     )
     for copy in own:
         copy.start()
-    table = jnp.concatenate([sides[...].astype(jnp.float32), jnp.zeros((HD - 8, shard), jnp.float32)], axis=0)
-    proj[block(0), pl.ds(proj_width, HD)] = jnp.transpose(table).astype(jnp.bfloat16)
     hidden_units = w_gate.shape[1]
     cuts = []
     for k in range(8):
@@ -824,7 +823,7 @@
     return pl.pallas_call(
         functools.partial(front_kernel, ctx_size),
         out_shape=tuple(jax.ShapeDtypeStruct(shape, kind) for shape, kind, _ in shapes),
-        in_specs=[pl.BlockSpec(memory_space=pltpu.SMEM), vmem, vmem] + [anywhere] * 8,
+        in_specs=[pl.BlockSpec(memory_space=pltpu.SMEM), vmem] + [anywhere] * 9,
         out_specs=tuple(spec for _, _, spec in shapes),
         scratch_shapes=[
             pltpu.VMEM((model, wide), low),
@@ -834,7 +833,7 @@
             pltpu.VMEM((HEADS, rows, HD), low),
             pltpu.VMEM((ctx_size, rows, 2 * kv_width), low),
             pltpu.VMEM((rows, q_width), low),
-            sem((52,)), sem((3,)), sem((3, 32)), sem((3, 4)), sem((3, 4)), sem((3,)), sem((32,)), sem((32,)), sem((8,)),
+            sem((53,)), sem((3,)), sem((3, 32)), sem((3, 4)), sem((3, 4)), sem((3,)), sem((32,)), sem((32,)), sem((8,)),
             sem((7,)), sem((8,)), sem((4,)), sem((4,)), sem((6,)), sem((2,)),
         ],
         compiler_params=pltpu.CompilerParams(
@@ -1485,8 +1484,8 @@
 
     grad_out = cotangent.reshape(row_count, D)
     per = b_key.shape[0]
-    flat = jnp.concatenate([attn_gain, b_query, ffn_gain, b_key, b_value])
-    sides = jnp.pad(flat, (0, 8 * shard_rows - flat.shape[0])).reshape(8, shard_rows)
+    pair = jnp.pad(jnp.concatenate([b_key, b_value]), (0, shard_rows - 2 * per))
+    sides = jnp.pad(jnp.stack([attn_gain, b_query, ffn_gain, pair]), ((0, HD - 4), (0, 0))).T
     source = hidden.reshape(row_count, D)
     normed, query_heads, key_value, log_total, mixed, resid, normed_two, small, proj_full, out_full, big, big_two, go_all, _, spread, norm_y, *turns = front_call(
         ctx_size, span_order, source, sides, w_query, w_key, w_value, w_out, w_gate, w_up, w_down, grad_out

time: 439 us -> 437 us (level)
  no operation moved by 1% of the time
where the time goes in v9:
time: 437 us; the launch traced here: 433 us
  Pallas kernels  430 us (98%)
    pallas_call x1, Pallas kernels, front_call(): pl.pallas_call(functools.partial(front_kernel, ctx_size), out_shape=tuple...  157 us
    pallas_call x1, Pallas kernels, back_call(): pl.pallas_call(functools.partial(back_kernel, ctx_size), out_shape=tuple(...  142 us
    pallas_call x1, Pallas kernels, ffn_call(): pl.pallas_call(functools.partial(ffn_kernel, ctx_size), out_shape=(jax.Sh...  123 us

profile of v9, /device:TPU:0, one launch (start us, length us, event | category | flops | bytes accessed | tf_op | source)
XLA Modules:
  0.0 432.9 jit_solution(12406847181786264277)
XLA Ops:
  0.6 0.7 fusion.1
  1.4 0.7 pad_maximum_fusion
  2.1 0.1 copy.33
  2.2 0.6 pad_bitcast_fusion.sides
  2.8 156.8 %front.1 = (bf16[256,1536]{1,0:T(8,128)(2,1)}, bf16[12,256,128]{2,1,0:T(8,128)(2,1)}, bf16[4,256,512]{2,1,0:T(8,128)(2,1)}, f32[256,128]{1,0:T(8,128)}, bf16[256...) custom-call(s32[1,8]{1,0:T(1,128)} %span.1, ...), custom_call_target="tpu_custom_call" | custom-call | tf_op jit(solution)/shard_map/front/pallas_call | solution.py:823
  159.6 122.8 %ffn.1 = (f32[256,1536]{1,0:T(8,128)}, bf16[4,256,1536]{2,1,0:T(8,128)(2,1)}, bf16[2,2,8,48,2304]{4,3,2,1,0:T(8,128)(2,1)}, bf16[2,2,8,48,1152]{4,3,2,1,0:T(8,12...) custom-call(bf16[256,1536]{1,0:T(8,128)(2,1)} %get-tuple-element.60.n_own, ...), custom_call_target="tpu_custom_call" | custom-call | tf_op jit(solution)/shard_map/ffn/pallas_call | solution.py:384
  282.4 142.4 %back.1 = (f32[256,1536]{1,0:T(8,128)}, f32[48,1536]{1,0:T(8,128)}, f32[48,640]{1,0:T(8,128)}, f32[48,1536]{1,0:T(8,128)}, bf16[8,48,2304]{2,1,0:T(8,128)(2,1)},...) custom-call(f32[256,1536]{1,0:T(8,128)} %get-tuple-element.65.grad_t, ...), custom_call_target="tpu_custom_call" | custom-call | tf_op jit(solution)/shard_map/back/pallas_call | solution.py:1309
  424.8 7.8 %finish.1 = (bf16[256,1536]{1,0:T(8,128)(2,1)}, f32[256,1536]{1,0:T(8,128)}, f32[1,48]{1,0:T(1,128)}, f32[48,1536]{1,0:T(8,128)}, f32[1,48]{1,0:T(1,128)}, /*ind...) custom-call(bf16[8,48,2304]{2,1,0:T(8,128)(2,1)} %get-tuple-element., ...), custom_call_target="tpu_custom_call" | custom-call | tf_op jit(solution)/shard_map/finish/pallas_call | solution.py:1439
